TPU v7x, 1024 devices: a whole 4x4x32 slice. The times are simulated.
1024 devices in a mesh: dp: 4 (over x), expert: 32 (over z), seq: 8 (over y, core).
Axes of the slice: x: 4, y: 4, z: 32, core: 2. Of those that a mesh axis runs over, the one named last changes fastest.
Arguments:
- tokens: bfloat16 [131072, 1024], P(('dp', 'expert', 'seq')), parts along dimension 0, may hold values from -6 to 6
- picks: int32 [1024, 32, 16], P(('dp', 'expert', 'seq')), parts along dimension 0, may hold values from 0 to 127, as said below
- gates: float32 [1024, 32, 16], P(('dp', 'expert', 'seq')), parts along dimension 0, may hold values from 0.1 to 2
- counts: int32 [1024, 32], P(('dp', 'expert', 'seq')), parts along dimension 0, may hold values from 1 to 16, as said below
- norm_in: float32 [1024], replicated, may hold values from 0.1 to 1.9
- norm_out: float32 [1024], replicated, may hold values from 0.1 to 1.9
- w_in: bfloat16 [32, 1024, 1408], P('expert'), may hold values from -0.1875 to 0.1875
- w_out: bfloat16 [32, 1408, 1024], P('expert'), may hold values from -0.15625 to 0.15625
- w_key: bfloat16 [1024, 512], replicated, may hold values from -0.1875 to 0.1875
- w_value: bfloat16 [1024, 512], replicated, may hold values from -0.1875 to 0.1875
- queries: bfloat16 [32768, 512], P(('dp', 'expert', 'seq')), parts along dimension 0, may hold values from -300 to 300
- w_proj: bfloat16 [512, 1024], replicated, may hold values from -0.25 to 0.25
Outputs:
- encoded: bfloat16 [131072, 1024], P(('dp', 'expert', 'seq')), parts along dimension 0
- dec_out: bfloat16 [32768, 1024], P(('dp', 'expert', 'seq')), parts along dimension 0
There are 4 independent parts, one for each index of `dp`. A program takes and returns all parts, laid end to end along the dimension named above; an argument that names none is the same for every part. Nothing has to cross between parts.
Inputs may be any that keep to these rules, and one draw needn't show every extreme that they name: `picks`: for each source device and expert, 16 different row numbers of that device's 128 tokens. Slots c < counts are live, the rest are padding; some source device and expert has all 16 slots live.
All inputs are finite; a program needn't handle non-finite values.
Results may differ from a plain program's by a relative error of at most 0.015.
The roundings to bfloat16 on the way count: a program that leaves them out, or rounds other values in their place, can miss the bound.
Values may be sent and summed in bfloat16 or wider, within the bound.
No kernel may reach another device: no remote copies, remote signals or barrier semaphores. Data moves between devices by JAX's collectives and lax.ppermute only.
A program may use at most 32 MiB of HBM per device.

v0:
```python
import math

import jax
import jax.numpy as jnp
from jax import lax
from jax.sharding import Mesh
from jax.sharding import PartitionSpec as P

HEADS = 8
SEQ = ("seq_0", "seq_1")
DP_EXPERT_SEQ = ("dp", "expert", "seq_0", "seq_1")


EPSILON = 1e-06


def in_order(parts, dim):
    parts = jnp.moveaxis(parts, 0, dim)
    shape = parts.shape
    return parts.reshape(*shape[:dim], shape[dim] * shape[dim + 1], *shape[dim + 2 :])


def stacked_from(x, axes, turns):
    parts = x
    for k in turns:
        parts = lax.all_gather(parts, axes[k])
    done = turns[::-1]
    back = [done.index(k) for k in range(len(axes))]
    parts = parts.transpose(*back, *range(len(axes), parts.ndim))
    return parts.reshape(-1, *x.shape)


def whole_of(x, axes, turns, dim):
    return in_order(stacked_from(x, axes, turns), dim)


def sent_together(arrays, axis, split_dim, concat_dim, along):
    widths = [math.prod(a.shape[along:]) for a in arrays]
    both = jnp.concatenate(
        [a.reshape(*a.shape[:along], w) for a, w in zip(arrays, widths)], axis=along
    )
    filled = lax.all_to_all(both, axis, split_axis=split_dim, concat_axis=concat_dim, tiled=True)
    parts = jnp.split(filled, [sum(widths[:k]) for k in range(1, len(widths))], axis=along)
    return tuple(
        (b.reshape(*filled.shape[:along], *a.shape[along:]) for a, b in zip(arrays, parts))
    )


def rms_norm(values, gain):
    mean_square = jnp.mean(values * values, axis=-1, keepdims=True)
    return values * lax.rsqrt(mean_square + EPSILON) * gain


def absorb(running, pieces, query_heads, score_scale):
    row_max, row_total, weighted = running
    key_piece, value_piece = pieces
    head_size = query_heads.shape[2]
    key_heads = key_piece.reshape(key_piece.shape[0], HEADS, head_size)
    value_heads = value_piece.reshape(value_piece.shape[0], HEADS, head_size)
    scores = (
        jnp.einsum("qhd,khd->qhk", query_heads, key_heads, preferred_element_type=jnp.float32)
        * score_scale
    )
    new_max = jnp.maximum(row_max, jnp.max(scores, axis=-1))
    weights = jnp.exp(scores - new_max[..., None])
    row_total = jnp.sum(weights, axis=-1)
    weighted = jnp.einsum(
        "qhk,khd->qhd",
        weights.astype(jnp.bfloat16),
        value_heads,
        preferred_element_type=jnp.float32,
    )
    return (new_max, row_total, weighted)


def starting(rows_count, head_size):
    return (
        jnp.full((rows_count, HEADS), -1e30, jnp.float32),
        jnp.zeros((rows_count, HEADS), jnp.float32),
        jnp.zeros((rows_count, HEADS, head_size), jnp.float32),
    )


def local(
    tokens, picks, gates, counts, norm_in, norm_out, w_in, w_out, w_key, w_value, queries, w_proj
):
    tok_rows, model_width = tokens.shape
    expert_total, slot_total = (picks.shape[1], picks.shape[2])
    plain = tokens.astype(jnp.float32)
    normed = rms_norm(plain, norm_in).astype(jnp.bfloat16)
    slot_index = picks[0].reshape(-1)
    outgoing = jnp.take(normed, slot_index, axis=0).reshape(expert_total, slot_total, model_width)
    slot_rows = lax.all_to_all(outgoing, "expert", split_axis=0, concat_axis=0, tiled=True)
    sources = slot_rows.shape[0]
    items = slot_rows.shape[1]
    flat = slot_rows.reshape(sources * items, model_width)
    hidden = jax.nn.gelu(
        jnp.dot(flat, w_in[0], preferred_element_type=jnp.float32), approximate=True
    ).astype(jnp.bfloat16)
    result = jnp.dot(hidden, w_out[0], preferred_element_type=jnp.float32).astype(jnp.bfloat16)
    returned = lax.all_to_all(
        result.reshape(sources, items, model_width),
        "expert",
        split_axis=0,
        concat_axis=0,
        tiled=True,
    )
    live_slots = lax.broadcasted_iota(jnp.int32, (expert_total, slot_total), 1) < counts[0][:, None]
    slot_weight = (gates[0] * live_slots.astype(jnp.float32)).reshape(-1)
    positions = lax.broadcasted_iota(jnp.int32, (tok_rows, expert_total * slot_total), 0)
    onehot = jnp.where(positions == slot_index[None, :], slot_weight[None, :], 0.0)
    expert_sum = jnp.dot(
        onehot,
        returned.reshape(-1, model_width).astype(jnp.float32),
        precision=lax.Precision.HIGHEST,
    )
    mixed = plain + expert_sum
    encoded = rms_norm(mixed, norm_out).astype(jnp.bfloat16)
    key_proj = jnp.dot(encoded, w_key, preferred_element_type=jnp.float32).astype(jnp.bfloat16)
    value_proj = jnp.dot(encoded, w_value, preferred_element_type=jnp.float32).astype(jnp.bfloat16)
    dec_rows = queries.shape[0]
    head_size = queries.shape[1] // HEADS
    score_scale = head_size ** (-0.5)
    group = lax.axis_size(SEQ)
    all_queries = whole_of(queries, ("seq_0", "seq_1"), (0, 1), 0)
    query_heads = all_queries.reshape(group * dec_rows, HEADS, head_size)
    part_max, part_total, part_weighted = absorb(
        starting(group * dec_rows, head_size), (key_proj, value_proj), query_heads, score_scale
    )
    got_max, got_total, got_weighted = sent_together(
        (
            part_max.reshape(group, dec_rows, HEADS),
            part_total.reshape(group, dec_rows, HEADS),
            part_weighted.reshape(group, dec_rows, HEADS, head_size),
        ),
        SEQ,
        0,
        0,
        3,
    )
    row_max = jnp.max(got_max, axis=0)
    rescale = jnp.exp(got_max - row_max[None])
    row_total = jnp.sum(got_total * rescale, axis=0)
    weighted = jnp.sum(got_weighted * rescale[..., None], axis=0)
    context = (
        (weighted / row_total[..., None]).reshape(dec_rows, HEADS * head_size).astype(jnp.bfloat16)
    )
    dec_out = jnp.dot(context, w_proj, preferred_element_type=jnp.float32).astype(jnp.bfloat16)
    return (encoded, dec_out)


def solution(mesh):
    split = Mesh(
        mesh.devices.reshape(mesh.shape["dp"], mesh.shape["expert"], 4, 2),
        ("dp", "expert", "seq_0", "seq_1"),
    )
    in_specs = (
        P(DP_EXPERT_SEQ, None),
        P(DP_EXPERT_SEQ, None, None),
        P(DP_EXPERT_SEQ, None, None),
        P(DP_EXPERT_SEQ, None),
        P(),
        P(),
        P("expert", None, None),
        P("expert", None, None),
        P(),
        P(),
        P(DP_EXPERT_SEQ, None),
        P(),
    )
    out_specs = (P(DP_EXPERT_SEQ, None), P(DP_EXPERT_SEQ, None))
    return jax.shard_map(local, mesh=split, in_specs=in_specs, out_specs=out_specs, check_vma=False)
```

profile of v0, /device:TPU:1, one launch (start us, length us, event | category | flops | bytes accessed | tf_op | source)
XLA Modules:
  0.0 312.6 jit_solution(13259815738018194860)
XLA Ops:
  0.6 0.0 copy-start
  0.6 0.9 compare_and_fusion
  1.5 0.8 copy.111
  2.3 1.1 fusion.23
  3.4 0.1 copy.113
  3.5 0.1 reshape_squeeze.3
  3.6 1.1 fusion.25
  4.7 2.8 gather_fusion
  7.5 1.4 broadcast_select_fusion
  8.9 134.2 %all_to_all.15 = bf16[32,16,1024]{2,1,0:T(8,128)(2,1)} all-to-all(bf16[32,16,1024]{2,1,0:T(8,128)(2,1)S(1)} %broadcast_select_fusion), channel_id=1, replica_groups=mesh['dp'=4,'expert'=32,'seq_0'=4,'seq_1'=2] {'expert'}, dimensions={0} | all-to-all | bytes 2097152 | tf_op jit(solution)/shard_map/all_to_all | solution.py:93
  143.1 6.6 %fusion.14 = bf16[512,1024]{1,0:T(8,128)(2,1)} fusion(bf16[1,1408,1024]{2,1,0:T(8,128)(2,1)S(1)} %copy-done, bf16[512,1024]{1,0:T(8,128)(2,1)} %bitcast.64, bf16[1,1024,1408]{2,1,0:T(8,128)(2,1)} %param.18), kind=kOutput, calls=%fused_computation.14 | convolution fusion | flops 2959802368 | bytes 7864320 | tf_op jit(solution)/shard_map/dot_general | solution.py:100
  149.7 7.8 %all-to-all-start.1 = ((bf16[32,16,1024]{2,1,0:T(8,128)(2,1)}), bf16[32,16,1024]{2,1,0:T(8,128)(2,1)}, u32[]{:S(2)}, u32[]{:S(2)}) async-start(bf16[32,16,1024]{2,1,0:T(8,128)(2,1)} %bitcast.63), calls=%async_computation.1 | async-start | bytes 2097152 | tf_op jit(solution)/shard_map/all_to_all | solution.py:101
  157.6 0.1 eq.12
  157.7 0.1 iota_compare_fusion.2
  157.7 0.1 lt.42
  157.8 0.1 copy.112
  157.9 0.1 squeeze.9
  158.0 10.0 %all-gather = bf16[128,512]{1,0:T(8,128)(2,1)S(1)} all-gather(bf16[32,512]{1,0:T(8,128)(2,1)S(1)} %copy-done.4), channel_id=2, replica_groups=mesh['dp'=4,'expert'=32,'seq_0'=4,'seq_1'=2] {'seq_0'}, dimensions={0}, use_global_device_ids=true | all-gather | bytes 163840 | tf_op jit(solution)/shard_map/all_gather | solution.py:26
  168.0 4.9 %all-gather.1 = bf16[8,32,512]{2,1,0:T(8,128)(2,1)S(1)} all-gather(bf16[4,32,512]{2,1,0:T(8,128)(2,1)S(1)} %bitcast.66), channel_id=3, replica_groups=mesh['dp'=4,'expert'=32,'seq_0'=4,'seq_1'=2] {'seq_1'}, dimensions={0}, use_global_device_ids=true | all-gather | bytes 393216 | tf_op jit(solution)/shard_map/all_gather | solution.py:26
  172.9 1.1 reshape_reshape_reshape.3
  174.0 88.5 %all-to-all-done.1 = bf16[32,16,1024]{2,1,0:T(8,128)(2,1)} async-done(((bf16[32,16,1024]{2,1,0:T(8,128)(2,1)}), bf16[32,16,1024]{2,1,0:T(8,128)(2,1)}, u32[]{:S(2)}, u32[]{:S(2)}) %all-to-all-start.1) | async-done | bytes 1048608 | tf_op jit(solution)/shard_map/all_to_all | solution.py:101
  262.5 1.9 multiply_reduce_fusion
  264.5 0.1 multiply_convert_fusion
  264.6 1.6 convolution_convert_fusion
  266.2 0.1 copy.118
  266.4 1.5 convolution_convert_fusion.1
  267.9 0.1 copy.115
  268.0 2.4 fusion.42
  270.4 0.7 max_broadcast_in_dim.18
  271.1 1.4 fusion.20
  272.5 1.5 convolution_bitcast_fusion
  274.0 0.1 reshape_reshape.4
  274.1 1.3 copy.120
  275.5 1.5 copy.122
  276.9 2.2 copy.121
  279.1 2.5 pad_maximum_fusion
  281.6 20.3 %all_to_all.16 = f32[8,32,8,66]{3,2,1,0:T(8,128)S(1)} all-to-all(f32[8,32,8,66]{3,2,1,0:T(8,128)S(1)} %pad_maximum_fusion), channel_id=1, replica_groups=mesh['dp'=4,'expert'=32,'seq_0'=4,'seq_1'=2] {'seq_0','seq_1'}, dimensions={0} | all-to-all | bytes 1081344 | tf_op jit(solution)/shard_map/all_to_all | solution.py:42
  301.9 1.0 copy-done.1
  302.9 1.7 fusion.41
  304.6 1.7 copy.131
  306.3 0.1 copy.132
  306.4 1.7 copy.130
  308.1 0.1 copy.124
  308.2 1.8 fusion.18
  310.0 0.2 copy.129
  310.2 0.1 copy.127
  310.4 0.1 convert_element_type.44
  310.5 2.1 convolution_convert_fusion.2
  (24 shorter events, 0.1 us)
Async XLA Ops:
  0.6 142.5 %copy-start = (bf16[1,1408,1024]{2,1,0:T(8,128)(2,1)S(1)}, bf16[1,1408,1024]{2,1,0:T(8,128)(2,1)}, u32[]{:S(2)}) copy-start(bf16[1,1408,1024]{2,1,0:T(8,128)(2,1)} %param.19) | copy-start | bytes 8650756
  143.1 14.6 %copy-start.7 = (s32[1,32]{1,0:T(1,128)S(1)}, s32[1,32]{1,0:T(1,128)}, u32[]{:S(2)}) copy-start(s32[1,32]{1,0:T(1,128)} %param.15) | copy-start | bytes 388
  143.1 14.7 %copy-start.5 = (f32[1,32,16]{1,2,0:T(8,128)S(1)}, f32[1,32,16]{1,2,0:T(8,128)}, u32[]{:S(2)}) copy-start(f32[1,32,16]{1,2,0:T(8,128)} %param.14) | copy-start | bytes 6148
  143.1 14.9 %copy-start.4 = (bf16[32,512]{1,0:T(8,128)(2,1)S(1)}, bf16[32,512]{1,0:T(8,128)(2,1)}, u32[]{:S(2)}) copy-start(bf16[32,512]{1,0:T(8,128)(2,1)} %param.22) | copy-start | bytes 98308
  149.7 112.8 %copy-start.2 = (bf16[128,1024]{1,0:T(8,128)(2,1)S(1)}, bf16[128,1024]{1,0:T(8,128)(2,1)}, u32[]{:S(2)}) copy-start(bf16[128,1024]{1,0:T(8,128)(2,1)} %param.12) | copy-start | bytes 786436
  149.7 114.7 %copy-start.6 = (f32[1024]{0:T(1024)S(1)}, f32[1024]{0:T(1024)}, u32[]{:S(2)}) copy-start(f32[1024]{0:T(1024)} %param.17) | copy-start | bytes 12292
  149.7 112.8 %all-to-all-start.1 = ((bf16[32,16,1024]{2,1,0:T(8,128)(2,1)}), bf16[32,16,1024]{2,1,0:T(8,128)(2,1)}, u32[]{:S(2)}, u32[]{:S(2)}) async-start(bf16[32,16,1024]{2,1,0:T(8,128)(2,1)} %bitcast.63), calls=%async_computation.1 | async-start | bytes 2097152 | tf_op jit(solution)/shard_map/all_to_all | solution.py:101
  264.6 7.9 %copy-start.3 = (bf16[128,1024]{1,0:T(8,128)(2,1)}, bf16[128,1024]{1,0:T(8,128)(2,1)S(1)}, u32[]{:S(2)}) copy-start(bf16[128,1024]{1,0:T(8,128)(2,1)S(1)} %multiply_convert_fusion) | copy-start | bytes 786436
  301.9 1.0 copy-start.1
where the time goes:
time: 314 us; the launch traced here: 313 us
  blocking collectives  169 us (54%)
  waiting for transfers between devices  88.5 us (28%)
  matrix products  17.8 us (6%)
  local copies, waits for them, and re-layouts  16.1 us (5%)
  other arithmetic  12.1 us (4%)
  starting transfers between devices  7.85 us (2%)
    all_to_all x1, blocking collectives, local(): lax.all_to_all(outgoing, 'expert', split_axis=0, concat_axis=0, tiled=True)  134 us
    all_to_all x1, waiting for transfers between devices, local(): lax.all_to_all(result.reshape(sources, items, model_width), 'expert', spl...  88.5 us
    all_to_all x1, blocking collectives, sent_together(): lax.all_to_all(both, axis, split_axis=split_dim, concat_axis=concat_dim,...  20.3 us
    all_gather x2, blocking collectives, stacked_from(): parts = lax.all_gather(parts, axes[k])  14.9 us
    all_to_all x1, starting transfers between devices, local(): lax.all_to_all(result.reshape(sources, items, model_width), 'expert', spl...  7.85 us
    dot_general x1, matrix products, local(): jnp.dot(hidden, w_out[0], preferred_element_type=jnp.float32)  6.61 us
  transfers between devices with their start and end apart: 1, of which 1 were waited for; matrix products, arithmetic and copies ran while one was open for 0% of the time, Pallas kernels for 0%

commit v1 on v0

v1 whole, which is shorter than its diff:
```python
import functools

import jax
import jax.numpy as jnp
from jax import lax
from jax.experimental import pallas as pl
from jax.experimental.pallas import tpu as pltpu
from jax.sharding import Mesh
from jax.sharding import PartitionSpec as P

HEADS = 8
EPSILON = 1e-06
BLOCK = 2
ALL = ("dp", "block", "parity", "row", "core")
NEAR = ("dp", "parity", "row", "core")
SEQ = ("row", "core")
STEP_J, STEP_E, INV_J = 9, 30, 25
STATS = 5
VMEM = 60 * 1024 * 1024
F32 = jnp.float32
BF16 = jnp.bfloat16

_VM = functools.partial(pl.BlockSpec, memory_space=pltpu.VMEM)


def rms_norm(values, gain):
    mean_square = jnp.mean(values * values, axis=-1, keepdims=True)
    return values * lax.rsqrt(mean_square + EPSILON) * gain


def shard_kernel(which, w_in_ref, w_out_ref, out_ref):
    rows = out_ref.shape[0]
    block, kind = which[0], which[1]

    @pl.when(kind == 0)
    def _():
        out_ref[...] = w_in_ref[0]

    @pl.when(kind == 1)
    def _():
        turned = w_out_ref[0].astype(F32).T
        upper = jnp.where(block % 2 == 1, turned[rows:], turned[:rows])
        out_ref[...] = upper.astype(BF16)


def take_shard(which, w_in, w_out, blocks):
    width, hidden = w_in.shape[1], w_in.shape[2]
    rows = width // blocks
    return pl.pallas_call(
        shard_kernel,
        grid_spec=pltpu.PrefetchScalarGridSpec(
            num_scalar_prefetch=1,
            grid=(1,),
            in_specs=[
                pl.BlockSpec((1, rows, hidden), lambda i, s: (0, s[0], 0)),
                pl.BlockSpec((1, hidden, 2 * rows), lambda i, s: (0, 0, s[0] // 2)),
            ],
            out_specs=pl.BlockSpec((rows, hidden), lambda i, s: (0, 0)),
        ),
        out_shape=jax.ShapeDtypeStruct((rows, hidden), BF16),
        compiler_params=pltpu.CompilerParams(vmem_limit_bytes=VMEM // 4),
    )(which, w_in, w_out)


def pick_kernel(tokens_ref, gain_ref, picks_ref, out_ref):
    rows = tokens_ref.shape[0]
    normed = rms_norm(tokens_ref[...].astype(F32), gain_ref[...]).astype(BF16)
    slots = picks_ref.shape[1]
    here = lax.broadcasted_iota(jnp.int32, (rows, slots), 0) == picks_ref[...]
    onehot = jnp.where(here, 1.0, 0.0).astype(BF16)
    out_ref[...] = lax.dot_general(
        onehot, normed, (((0,), (0,)), ((), ())), preferred_element_type=F32
    ).astype(BF16)


def pick_rows(tokens, gain, picks):
    slots, width = picks.shape[1], tokens.shape[1]
    return pl.pallas_call(
        pick_kernel,
        in_specs=[_VM()] * 3,
        out_specs=_VM(),
        out_shape=jax.ShapeDtypeStruct((slots, width), BF16),
        compiler_params=pltpu.CompilerParams(vmem_limit_bytes=VMEM // 4),
    )(tokens, gain, picks)


def gelu(v):
    return 0.5 * v * (1.0 + jnp.tanh(0.7978845608028654 * (v + 0.044715 * (v * v * v))))


def expert_kernel(rows_ref, weights_ref, out_ref, w_in, w_out, sems):
    first = pltpu.make_async_copy(weights_ref.at[:, 0], w_in, sems.at[0])
    second = pltpu.make_async_copy(weights_ref.at[:, 1], w_out, sems.at[1])
    first.start()
    second.start()
    first.wait()
    width, hidden = rows_ref.shape[1], w_in.shape[2]
    tile = 256
    second.wait()

    @pl.loop(0, rows_ref.shape[0] // tile)
    def _(i):
        here = pl.ds(pl.multiple_of(i * tile, tile), tile)
        mid = gelu(
            jnp.dot(
                rows_ref[here, :], w_in[...].reshape(width, hidden), preferred_element_type=F32
            )
        ).astype(BF16)
        out_ref[here, :] = lax.dot_general(
            mid,
            w_out[...].reshape(width, hidden),
            (((1,), (1,)), ((), ())),
            preferred_element_type=F32,
        ).astype(BF16)


def expert(rows, weights):
    total, width = rows.shape
    blocks, _, part, hidden = weights.shape
    return pl.pallas_call(
        expert_kernel,
        in_specs=[_VM(), pl.BlockSpec(memory_space=pl.ANY)],
        out_specs=_VM(),
        out_shape=jax.ShapeDtypeStruct((total, width), BF16),
        scratch_shapes=[
            pltpu.VMEM((blocks, part, hidden), BF16),
            pltpu.VMEM((blocks, part, hidden), BF16),
            pltpu.SemaphoreType.DMA((2,)),
        ],
        compiler_params=pltpu.CompilerParams(vmem_limit_bytes=VMEM // 2),
        cost_estimate=pl.CostEstimate(
            flops=4 * total * width * hidden,
            bytes_accessed=4 * width * hidden + 4 * total * width,
            transcendentals=total * hidden,
        ),
    )(rows, weights)


def pieces(v, count):
    out = []
    for _ in range(count):
        part = v.astype(BF16)
        out.append(part)
        v = v - part.astype(F32)
    return out


def tail_kernel(
    back_ref, picks_ref, weight_ref, tokens_ref, gain_ref, key_ref, value_ref, query_ref,
    encoded_ref, packet_ref,
):
    rows = tokens_ref.shape[0]
    slots = picks_ref.shape[1]
    here = lax.broadcasted_iota(jnp.int32, (rows, slots), 0) == picks_ref[...]
    spread = jnp.where(here, weight_ref[...], 0.0)
    back = back_ref[...]
    expert_sum = sum(
        jnp.dot(part, back, preferred_element_type=F32) for part in pieces(spread, 3)
    )
    mixed = tokens_ref[...].astype(F32) + expert_sum
    encoded = rms_norm(mixed, gain_ref[...]).astype(BF16)
    encoded_ref[...] = encoded
    keys = jnp.dot(encoded, key_ref[...], preferred_element_type=F32).astype(BF16)
    values = jnp.dot(encoded, value_ref[...], preferred_element_type=F32).astype(BF16)
    query = query_ref[...]
    count, features = query.shape
    size = features // HEADS
    lane = lax.broadcasted_iota(jnp.int32, (rows, 2 * size), 1)
    low = lane < size
    zero = jnp.zeros((), BF16)
    stat_lane = lax.broadcasted_iota(jnp.int32, (count, 128), 1)
    stats = jnp.zeros((count, 128), F32)
    for pair in range(HEADS // 2):
        span = slice(pair * 2 * size, (pair + 1) * 2 * size)
        q, k, v = query[:, span], keys[:, span], values[:, span]
        total = None
        for odd in range(2):
            mask = low if odd == 0 else ~low
            scores = lax.dot_general(
                q,
                jnp.where(mask, k, zero),
                (((1,), (1,)), ((), ())),
                preferred_element_type=F32,
            ) * (size**-0.5)
            top = jnp.max(scores, axis=1, keepdims=True)
            weights = jnp.exp(scores - top)
            amount = jnp.sum(weights, axis=1, keepdims=True)
            term = jnp.dot(
                weights.astype(BF16), jnp.where(mask, v, zero), preferred_element_type=F32
            )
            total = term if total is None else total + term
            entries = pieces(top, 3) + pieces(amount, 2)
            for i, entry in enumerate(entries):
                at = (2 * pair + odd) * STATS + i
                stats = jnp.where(stat_lane == at, entry.astype(F32), stats)
        packet_ref[:, span] = total.astype(BF16)
    packet_ref[:, features:] = stats.astype(BF16)


def tail(back, picks, weight, tokens, gain, w_key, w_value, query):
    rows, width = tokens.shape
    count, features = query.shape
    return pl.pallas_call(
        tail_kernel,
        in_specs=[_VM()] * 8,
        out_specs=(_VM(), _VM()),
        out_shape=(
            jax.ShapeDtypeStruct((rows, width), BF16),
            jax.ShapeDtypeStruct((count, features + 128), BF16),
        ),
        compiler_params=pltpu.CompilerParams(vmem_limit_bytes=VMEM // 2),
    )(back, picks, weight, tokens, gain, w_key, w_value, query)


def merge_kernel(got_ref, proj_ref, out_ref):
    group, count, wide = got_ref.shape
    features = wide - 128
    size = features // HEADS
    lane = lax.broadcasted_iota(jnp.int32, (count, 2 * size), 1)
    low = lane < size
    stats = [got_ref[g, :, features:].astype(F32) for g in range(group)]
    parts = []
    for pair in range(HEADS // 2):
        span = slice(pair * 2 * size, (pair + 1) * 2 * size)
        scales, totals = [], []
        for odd in range(2):
            at = (2 * pair + odd) * STATS
            tops = [s[:, at : at + 1] + s[:, at + 1 : at + 2] + s[:, at + 2 : at + 3] for s in stats]
            amounts = [s[:, at + 3 : at + 4] + s[:, at + 4 : at + 5] for s in stats]
            top = functools.reduce(jnp.maximum, tops)
            scale = [jnp.exp(t - top) for t in tops]
            scales.append(scale)
            totals.append(sum(a * s for a, s in zip(amounts, scale)))
        weighted = sum(
            got_ref[g, :, span].astype(F32) * jnp.where(low, scales[0][g], scales[1][g])
            for g in range(group)
        )
        parts.append((weighted / jnp.where(low, totals[0], totals[1])).astype(BF16))
    context = jnp.concatenate(parts, axis=1)
    out_ref[...] = jnp.dot(context, proj_ref[...], preferred_element_type=F32).astype(BF16)


def merge(got, w_proj):
    return pl.pallas_call(
        merge_kernel,
        in_specs=[_VM()] * 2,
        out_specs=_VM(),
        out_shape=jax.ShapeDtypeStruct((got.shape[1], w_proj.shape[1]), BF16),
        compiler_params=pltpu.CompilerParams(vmem_limit_bytes=VMEM // 4),
    )(got, w_proj)


def scatter_pairs(sizes):
    dps, blocks, parities, rows, cores = sizes
    plane = dps * rows * cores

    def place(dp, z, row, core):
        return ((dp * blocks * parities + z) * rows + row) * cores + core

    pairs = []
    for dp in range(dps):
        for parity in range(parities):
            for row in range(rows):
                e = (dp * parities + parity) * rows + row
                for block in range(blocks):
                    for core in range(cores):
                        j = block * cores + core
                        column = (STEP_J * j + STEP_E * e) % plane
                        source = place(
                            column // (rows * cores), e, column // cores % rows, column % cores
                        )
                        pairs.append((source, place(dp, block * parities + parity, row, core)))
    return pairs


def local(
    sizes, tokens, picks, gates, counts, norm_in, norm_out, w_in, w_out, w_key, w_value, queries, w_proj
):
    dps, blocks, parities, row_count, cores = sizes
    plane = dps * row_count * cores
    experts, cap = picks.shape[1], picks.shape[2]
    width = tokens.shape[1]
    own = lax.axis_index("block") * parities + lax.axis_index("parity")
    column = (lax.axis_index("dp") * row_count + lax.axis_index("row")) * cores + lax.axis_index(
        "core"
    )
    j = (INV_J * (column + (plane - STEP_E) * own)) % plane
    shard = take_shard(jnp.stack([j // cores, j % cores]).astype(jnp.int32), w_in, w_out, blocks)
    shard = lax.ppermute(shard, ALL, scatter_pairs(sizes))
    weights = lax.all_gather(shard, ("block", "core"))
    weights = weights.reshape(blocks, cores, *shard.shape)

    pick_row = picks.reshape(1, experts * cap)
    live = lax.broadcasted_iota(jnp.int32, (experts, cap), 1) < counts[0][:, None]
    slot_weight = jnp.where(live, gates[0], 0.0).reshape(1, experts * cap)
    chosen = pick_rows(tokens, norm_in[None, :], pick_row)
    near = experts * cores
    there = lax.all_to_all(
        chosen.reshape(near, -1, width), NEAR, split_axis=0, concat_axis=0, tiled=True
    )
    query = lax.all_gather(queries, SEQ, tiled=True)

    result = expert(there.reshape(-1, width), weights)
    back = lax.all_to_all(
        result.reshape(near, -1, width), NEAR, split_axis=0, concat_axis=0, tiled=True
    ).reshape(-1, width)
    encoded, packet = tail(
        back, pick_row, slot_weight, tokens, norm_out[None, :], w_key, w_value, query
    )
    group = row_count * cores
    got = lax.all_to_all(
        packet.reshape(group, -1, packet.shape[1]), SEQ, split_axis=0, concat_axis=0, tiled=True
    )
    return encoded, merge(got, w_proj)


def solution(mesh):
    dps, planes, seq = mesh.shape["dp"], mesh.shape["expert"], mesh.shape["seq"]
    sizes = (dps, planes // BLOCK, BLOCK, seq // 2, 2)
    split = Mesh(mesh.devices.reshape(sizes), ALL)
    in_specs = (
        P(ALL, None),
        P(ALL, None, None),
        P(ALL, None, None),
        P(ALL, None),
        P(),
        P(),
        P(("block", "parity"), None, None),
        P(("block", "parity"), None, None),
        P(),
        P(),
        P(ALL, None),
        P(),
    )
    out_specs = (P(ALL, None), P(ALL, None))
    return jax.shard_map(
        functools.partial(local, sizes),
        mesh=split,
        in_specs=in_specs,
        out_specs=out_specs,
        check_vma=False,
    )
```

time: 314 us -> 235 us (0.75)
  blocking collectives: 169 us -> 68.4 us
  starting transfers between devices: 7.85 us -> 32.6 us
  matrix products: 17.8 us -> 0 us
  between operations: 0.82 us -> 14.2 us
  other arithmetic: 12.1 us -> 0.15 us
  waiting for transfers between devices: 88.5 us -> 99 us
  Pallas kernels: 0 us -> 9.89 us
  local copies, waits for them, and re-layouts: 16.1 us -> 8.59 us
    all_to_all x2, blocking collectives: 155 us -> 49.1 us  [the longest x1 38.9 us: local(): lax.all_to_all(chosen.reshape(near, -1, width), NEAR, split_axis=0, conca...]
    all_gather x0 -> x1, waiting for transfers between devices: none -> 94.6 us  [local(): weights = lax.all_gather(shard, ('block', 'core'))]
    all_to_all x1, waiting for transfers between devices: 88.5 us -> 0.01 us  [local(): lax.all_to_all(result.reshape(near, -1, width), NEAR, split_axis=0, conca...]
    ppermute x0 -> x1, starting transfers between devices: none -> 23.5 us  [local(): shard = lax.ppermute(shard, ALL, scatter_pairs(sizes))]
    dot_general x7 -> x0, matrix products: 17.8 us -> none  [the longest x1 6.61 us: local(): jnp.dot(hidden, w_out[0], preferred_element_type=jnp.float32)]
    pallas_call x0 -> x5, Pallas kernels: none -> 9.89 us  [the longest x1 5.04 us: expert(): pl.pallas_call(expert_kernel, in_specs=[_VM(), pl.BlockSpec(memory_space=...]
    another operation x6 -> x0, local copies, waits for them, and re-layouts: 5.59 us -> none  [the longest x2 2.88 us: absorb(): new_max = jnp.maximum(row_max, jnp.max(scores, axis=-1))]
    all_gather x2 -> x1, blocking collectives: 14.9 us -> 19.3 us  [local(): query = lax.all_gather(queries, SEQ, tiled=True)]
  transfers between devices with their start and end apart: 1 -> 3, of which waited for: 1 -> 2; matrix products, arithmetic and copies ran while one was open for 0% -> 0% of each run, Pallas kernels for 0% -> 0%
where the time goes in v1:
time: 235 us; the launch traced here: 233 us
  waiting for transfers between devices  99 us (42%)
  blocking collectives  68.4 us (29%)
  starting transfers between devices  32.6 us (14%)
  between operations  14.2 us (6%)
  Pallas kernels  9.89 us (4%)
  local copies, waits for them, and re-layouts  8.59 us (4%)
    all_gather x1, waiting for transfers between devices, local(): weights = lax.all_gather(shard, ('block', 'core'))  94.6 us
    all_to_all x1, blocking collectives, local(): lax.all_to_all(chosen.reshape(near, -1, width), NEAR, split_axis=0, conca...  38.9 us
    ppermute x1, starting transfers between devices, local(): shard = lax.ppermute(shard, ALL, scatter_pairs(sizes))  23.5 us
    all_gather x1, blocking collectives, local(): query = lax.all_gather(queries, SEQ, tiled=True)  19.3 us
    all_to_all x1, blocking collectives, local(): lax.all_to_all(packet.reshape(group, -1, packet.shape[1]), SEQ, split_axi...  10.2 us
    all_to_all x1, starting transfers between devices, local(): lax.all_to_all(result.reshape(near, -1, width), NEAR, split_axis=0, conca...  9.05 us
    unnamed x30, local copies, waits for them, and re-layouts  8.34 us
    pallas_call x1, Pallas kernels, expert(): pl.pallas_call(expert_kernel, in_specs=[_VM(), pl.BlockSpec(memory_space=...  5.04 us
  transfers between devices with their start and end apart: 3, of which 2 were waited for; matrix products, arithmetic and copies ran while one was open for 0% of the time, Pallas kernels for 0%

profile of v1, /device:TPU:1, one launch (start us, length us, event | category | flops | bytes accessed | tf_op | source)
XLA Modules:
  0.0 232.8 jit_solution(12264663430247784388)
XLA Ops:
  7.2 0.0 all-gather.3.cloned.1.call-start
  7.3 0.1 pad_add_fusion.which
  7.3 0.0 copy-start
  7.3 1.8 copy-done
  9.1 0.0 copy-start.1
  9.1 1.8 copy-done.1
  11.0 0.0 copy-start.11
  11.0 0.0 copy-start.6
  11.0 0.8 shard_map.132
  11.8 23.5 %collective-permute-start = (bf16[64,1408]{1,0:T(8,128)(2,1)S(1)}, bf16[64,1408]{1,0:T(8,128)(2,1)S(1)}, u32[]{:S(2)}, u32[]{:S(2)}) collective-permute-start(bf16[64,1408]{1,0:T(8,128)(2,1)S(1)} %shard_map.132), channel_id=1, source_target_pairs={{0,0},{257,1},{514,16},{771,17},{4,32},{261,33},{518,48},{775,49},... | collective-permute-start | bytes 540680 | tf_op jit(solution)/shard_map/ppermute | solution.py:289
  35.3 4.3 %collective-permute-done = bf16[64,1408]{1,0:T(8,128)(2,1)S(1)} collective-permute-done((bf16[64,1408]{1,0:T(8,128)(2,1)S(1)}, bf16[64,1408]{1,0:T(8,128)(2,1)S(1)}, u32[]{:S(2)}, u32[]{:S(2)}) %collective-permute-start) | collective-permute-done | bytes 180256 | tf_op jit(solution)/shard_map/ppermute | solution.py:289
  39.7 0.7 copy-done.9
  40.4 0.0 all-gather.3.cloned.1.call-update
  40.4 0.0 copy-done.11
  40.4 0.1 copy.16
  40.5 0.1 reshape.59.picks_ref
  40.6 0.0 copy-done.2
  40.6 0.0 copy-done.6
  40.6 0.5 shard_map.131
  41.1 38.9 %all_to_all.15 = bf16[64,8,1024]{2,1,0:T(8,128)(2,1)S(1)} all-to-all(bf16[64,8,1024]{2,1,0:T(8,128)(2,1)S(1)} %bitcast.12), channel_id=1, replica_groups=mesh['dp'=4,'block'=16,'parity'=2,'row'=4,'core'=2] {'dp','parity','row'..., dimensions={0} | all-to-all | bytes 2097152 | tf_op jit(solution)/shard_map/all_to_all | solution.py:298
  80.0 94.6 %all-gather.3.cloned.1.call-done = bf16[2048,1408]{1,0:T(8,128)(2,1)} async-done(((bf16[64,1408]{1,0:T(8,128)(2,1)}), bf16[2048,1408]{1,0:T(8,128)(2,1)}) %all-gather.3.cloned.1.call-update) | async-done | bytes 5767184 | tf_op jit(solution)/shard_map/all_gather | solution.py:290
  174.6 0.0 copy-start.8
  174.6 2.6 %copy-done.8 = bf16[2048,1408]{1,0:T(8,128)(2,1)S(1)} copy-done((bf16[2048,1408]{1,0:T(8,128)(2,1)S(1)}, bf16[2048,1408]{1,0:T(8,128)(2,1)}, u32[]{:S(2)}) %copy-start.8) | copy-done | bytes 5767192
  177.3 0.0 copy-start.13
  177.3 0.0 copy-start.12
  177.3 0.0 copy-start.10
  177.3 0.0 copy-start.7
  177.3 5.0 %shard_map.133 = bf16[512,1024]{1,0:T(8,128)(2,1)} custom-call(bf16[512,1024]{1,0:T(8,128)(2,1)S(1)} %bitcast.13, bf16[16,2,64,1408]{3,2,1,0:T(8,128)(2,1)S(1)} %bitcast.17), custom_call_target="tpu_custom_call" | custom-call | flops 2952790016 | bytes 7864320 | tf_op jit(solution)/shard_map/pallas_call | solution.py:120
  182.3 0.0 copy-start.3
  182.3 9.1 %all-to-all-start.1 = ((bf16[64,8,1024]{2,1,0:T(8,128)(2,1)}), bf16[64,8,1024]{2,1,0:T(8,128)(2,1)S(1)}, u32[]{:S(2)}, u32[]{:S(2)}) async-start(bf16[64,8,1024]{2,1,0:T(8,128)(2,1)} %bitcast.6), calls=%async_computation.1 | async-start | bytes 2097152 | tf_op jit(solution)/shard_map/all_to_all | solution.py:304
  191.4 0.0 copy-done.13
  191.4 0.1 iota_compare_fusion
  191.5 0.1 lt.35
  191.6 0.0 copy-done.12
  191.6 0.1 copy.17
  191.6 0.1 squeeze.3
  191.7 0.0 copy-done.10
  191.7 19.3 %all_gather.11.query_ref = bf16[256,512]{1,0:T(8,128)(2,1)S(1)} all-gather(bf16[32,512]{1,0:T(8,128)(2,1)S(1)} %copy-done.10), channel_id=1, replica_groups=mesh['dp'=4,'block'=16,'parity'=2,'row'=4,'core'=2] {'row','core'}, dimensions={0}, use_global_device_ids=true | all-gather | bytes 294912 | tf_op jit(solution)/shard_map/all_gather | solution.py:301
  211.0 0.0 all-to-all-done.1
  211.0 0.0 copy-done.7
  211.0 0.0 copy-done.3
  211.1 0.0 copy-start.4
  211.1 1.2 copy-done.4
  212.3 0.0 copy-start.5
  212.3 2.0 shard_map.134
  214.3 10.2 %all_to_all.16.got_ref = bf16[8,32,640]{2,1,0:T(8,128)(2,1)S(1)} all-to-all(bf16[8,32,640]{2,1,0:T(8,128)(2,1)S(1)} %bitcast.14), channel_id=1, replica_groups=mesh['dp'=4,'block'=16,'parity'=2,'row'=4,'core'=2] {'row','core'}, dimensions={0} | all-to-all | bytes 655360 | tf_op jit(solution)/shard_map/all_to_all | solution.py:311
  224.5 0.0 copy-done.5
  224.5 1.5 shard_map.135
  (3 shorter events, 0.0 us)
Async XLA Ops:
  7.2 167.5 %all-gather.3.cloned.1.call-start = ((), (), s32[]{:S(2)}) async-start(), calls=%async_computation.3 | async-start | bytes 5947392 | tf_op jit(solution)/shard_map/all_gather | solution.py:290
  7.3 1.8 copy-start
  9.1 1.8 copy-start.1
  11.0 29.4 %copy-start.11 = (s32[1,32,16]{1,2,0:T(8,128)S(1)}, s32[1,32,16]{1,2,0:T(8,128)}, u32[]{:S(2)}) copy-start(s32[1,32,16]{1,2,0:T(8,128)} %param.13) | copy-start | bytes 6148
  11.0 29.6 %copy-start.2 = (bf16[128,1024]{1,0:T(8,128)(2,1)S(1)}, bf16[128,1024]{1,0:T(8,128)(2,1)}, u32[]{:S(2)}) copy-start(bf16[128,1024]{1,0:T(8,128)(2,1)} %tokens_ref.3) | copy-start | bytes 786436
  11.0 29.6 %copy-start.6 = (f32[1024]{0:T(1024)S(1)}, f32[1024]{0:T(1024)}, u32[]{:S(2)}) copy-start(f32[1024]{0:T(1024)} %param.16) | copy-start | bytes 12292
  11.8 27.9 %collective-permute-start = (bf16[64,1408]{1,0:T(8,128)(2,1)S(1)}, bf16[64,1408]{1,0:T(8,128)(2,1)S(1)}, u32[]{:S(2)}, u32[]{:S(2)}) collective-permute-start(bf16[64,1408]{1,0:T(8,128)(2,1)S(1)} %shard_map.132), channel_id=1, source_target_pairs={{0,0},{257,1},{514,16},{771,17},{4,32},{261,33},{518,48},{775,49},... | collective-permute-start | bytes 540680 | tf_op jit(solution)/shard_map/ppermute | solution.py:289
  39.7 0.7 copy-start.9
  174.6 2.6 %copy-start.8 = (bf16[2048,1408]{1,0:T(8,128)(2,1)S(1)}, bf16[2048,1408]{1,0:T(8,128)(2,1)}, u32[]{:S(2)}) copy-start(bf16[2048,1408]{1,0:T(8,128)(2,1)} %all-gather.3.cloned.1.call-done) | copy-start | bytes 17301508
  177.3 14.1 %copy-start.13 = (s32[1,32]{1,0:T(1,128)S(1)}, s32[1,32]{1,0:T(1,128)}, u32[]{:S(2)}) copy-start(s32[1,32]{1,0:T(1,128)} %param.15) | copy-start | bytes 388
  177.3 14.3 %copy-start.12 = (f32[1,32,16]{1,2,0:T(8,128)S(1)}, f32[1,32,16]{1,2,0:T(8,128)}, u32[]{:S(2)}) copy-start(f32[1,32,16]{1,2,0:T(8,128)} %param.14) | copy-start | bytes 6148
  177.3 14.5 %copy-start.10 = (bf16[32,512]{1,0:T(8,128)(2,1)S(1)}, bf16[32,512]{1,0:T(8,128)(2,1)}, u32[]{:S(2)}) copy-start(bf16[32,512]{1,0:T(8,128)(2,1)} %param.22) | copy-start | bytes 98308
  177.3 33.8 %copy-start.7 = (f32[1024]{0:T(1024)S(1)}, f32[1024]{0:T(1024)}, u32[]{:S(2)}) copy-start(f32[1024]{0:T(1024)} %param.17) | copy-start | bytes 12292
  182.3 28.7 %copy-start.3 = (bf16[1024,512]{1,0:T(8,128)(2,1)S(1)}, bf16[1024,512]{1,0:T(8,128)(2,1)}, u32[]{:S(2)}) copy-start(bf16[1024,512]{1,0:T(8,128)(2,1)} %key_ref.1) | copy-start | bytes 3145732
  182.3 28.7 %all-to-all-start.1 = ((bf16[64,8,1024]{2,1,0:T(8,128)(2,1)}), bf16[64,8,1024]{2,1,0:T(8,128)(2,1)S(1)}, u32[]{:S(2)}, u32[]{:S(2)}) async-start(bf16[64,8,1024]{2,1,0:T(8,128)(2,1)} %bitcast.6), calls=%async_computation.1 | async-start | bytes 2097152 | tf_op jit(solution)/shard_map/all_to_all | solution.py:304
  211.1 1.2 copy-start.4
  212.3 12.2 %copy-start.5 = (bf16[512,1024]{1,0:T(8,128)(2,1)S(1)}, bf16[512,1024]{1,0:T(8,128)(2,1)}, u32[]{:S(2)}) copy-start(bf16[512,1024]{1,0:T(8,128)(2,1)} %proj_ref.1) | copy-start | bytes 3145732
Sparse Core Ops, SparseCore 0:
  40.5 134.0 all-gather.2

commit v2 on v1

--- a/solution.py
+++ b/solution.py
@@ -17,6 +17,7 @@
 STEP_J, STEP_E, INV_J = 9, 30, 25
 STATS = 5
 VMEM = 60 * 1024 * 1024
+FULL = 61 * 1024 * 1024
 F32 = jnp.float32
 BF16 = jnp.bfloat16
 
@@ -58,7 +59,7 @@
             out_specs=pl.BlockSpec((rows, hidden), lambda i, s: (0, 0)),
         ),
         out_shape=jax.ShapeDtypeStruct((rows, hidden), BF16),
-        compiler_params=pltpu.CompilerParams(vmem_limit_bytes=VMEM // 4),
+        compiler_params=pltpu.CompilerParams(vmem_limit_bytes=FULL),
     )(which, w_in, w_out)
 
 
@@ -88,52 +89,126 @@
     return 0.5 * v * (1.0 + jnp.tanh(0.7978845608028654 * (v + 0.044715 * (v * v * v))))
 
 
-def expert_kernel(rows_ref, weights_ref, out_ref, w_in, w_out, sems):
-    first = pltpu.make_async_copy(weights_ref.at[:, 0], w_in, sems.at[0])
-    second = pltpu.make_async_copy(weights_ref.at[:, 1], w_out, sems.at[1])
-    first.start()
-    second.start()
-    first.wait()
+def expert_kernel(place, rows_ref, gathered_ref, own_ref, *refs):
+    blocks = gathered_ref.shape[0]
+    ring = refs[:-7]
+    early, late, out_ref, w_in, w_out, middle, sems = refs[-7:]
+    block, turn = place[0], place[1]
+    head = gathered_ref.shape[2]
+    rest = pl.ds(head, own_ref.shape[0] // 2)
+
+    def at(offset):
+        return lax.rem(block + offset + blocks, blocks)
+
+    def halves(ref, start, index):
+        size = own_ref.shape[0] // 2
+        return [
+            (ref.at[pl.ds(start + k * size, size)], buffer.at[index, rest])
+            for k, buffer in enumerate((w_in, w_out))
+        ]
+
+    jobs = [
+        [(gathered_ref.at[:, k], buffer.at[:, pl.ds(0, head)])]
+        for k, buffer in enumerate((w_in, w_out))
+    ]
+    found = [halves(own_ref, 0, block)]
+    for step, ref in enumerate(ring, 1):
+        found.append(halves(ref, 0, at(-step * turn)))
+    count = early.shape[0] // own_ref.shape[0]
+    for step in range(1, len(ring)):
+        ref, k = (early, step - 1) if step <= count else (late, step - 1 - count)
+        found.append(halves(ref, k * own_ref.shape[0], at(step * turn)))
+    for pair in found:
+        for k in range(2):
+            jobs[k].append(pair[k])
+    copies = [
+        [pltpu.make_async_copy(src, dst, sems.at[k, n]) for n, (src, dst) in enumerate(jobs[k])]
+        for k in range(2)
+    ]
+    for part in copies:
+        for copy in part:
+            copy.start()
     width, hidden = rows_ref.shape[1], w_in.shape[2]
     tile = 256
-    second.wait()
+    for copy in copies[0]:
+        copy.wait()
 
     @pl.loop(0, rows_ref.shape[0] // tile)
     def _(i):
         here = pl.ds(pl.multiple_of(i * tile, tile), tile)
-        mid = gelu(
+        middle[here, :] = gelu(
             jnp.dot(
                 rows_ref[here, :], w_in[...].reshape(width, hidden), preferred_element_type=F32
             )
         ).astype(BF16)
+
+    for copy in copies[1]:
+        copy.wait()
+
+    @pl.loop(0, rows_ref.shape[0] // tile)
+    def _(i):
+        here = pl.ds(pl.multiple_of(i * tile, tile), tile)
         out_ref[here, :] = lax.dot_general(
-            mid,
+            middle[here, :],
             w_out[...].reshape(width, hidden),
             (((1,), (1,)), ((), ())),
             preferred_element_type=F32,
         ).astype(BF16)
 
 
-def expert(rows, weights):
+def expert(place, rows, gathered, own, ring, early, late):
     total, width = rows.shape
-    blocks, _, part, hidden = weights.shape
+    blocks, _, head, hidden = gathered.shape
+    part = head + own.shape[0] // 2
+    anywhere = pl.BlockSpec(memory_space=pl.ANY)
     return pl.pallas_call(
         expert_kernel,
-        in_specs=[_VM(), pl.BlockSpec(memory_space=pl.ANY)],
+        in_specs=[pl.BlockSpec(memory_space=pltpu.SMEM), _VM()]
+        + [anywhere] * (4 + len(ring)),
         out_specs=_VM(),
         out_shape=jax.ShapeDtypeStruct((total, width), BF16),
         scratch_shapes=[
             pltpu.VMEM((blocks, part, hidden), BF16),
             pltpu.VMEM((blocks, part, hidden), BF16),
-            pltpu.SemaphoreType.DMA((2,)),
+            pltpu.VMEM((total, hidden), BF16),
+            pltpu.SemaphoreType.DMA((2, 1 + 2 * len(ring))),
         ],
-        compiler_params=pltpu.CompilerParams(vmem_limit_bytes=VMEM // 2),
+        compiler_params=pltpu.CompilerParams(vmem_limit_bytes=FULL),
         cost_estimate=pl.CostEstimate(
             flops=4 * total * width * hidden,
             bytes_accessed=4 * width * hidden + 4 * total * width,
             transcendentals=total * hidden,
         ),
-    )(rows, weights)
+    )(place, rows, gathered, own, *ring, early, late)
+
+
+def spread(shard, sizes):
+    _, blocks, _, _, cores = sizes
+    half = shard.shape[0] // 2
+    gathered = lax.all_gather(shard[:half], ("block", "core"))
+    gathered = gathered.reshape(blocks, cores, half, shard.shape[1])
+    swap = [(0, 1), (1, 0)]
+    core = lax.axis_index("core")
+    mine = shard[half:]
+    other = lax.ppermute(mine, "core", swap)
+    own = jnp.where(
+        core == 0, jnp.concatenate([mine, other]), jnp.concatenate([other, mine])
+    )
+    turns = [
+        (b * cores + c, (b + (1 if c == 0 else -1)) % blocks * cores + c)
+        for b in range(blocks)
+        for c in range(cores)
+    ]
+    steps = blocks // 2
+    ring, held = [], own
+    for _ in range(steps):
+        held = lax.ppermute(held, ("block", "core"), turns)
+        ring.append(held)
+    cut = steps // 2
+    early = lax.ppermute(jnp.concatenate(ring[:cut]), "core", swap)
+    late = lax.ppermute(jnp.concatenate(ring[cut : steps - 1]), "core", swap)
+    place = jnp.stack([lax.axis_index("block"), 1 - 2 * core]).astype(jnp.int32)
+    return place, gathered, own, ring, early, late
 
 
 def pieces(v, count):
@@ -286,9 +361,9 @@
     )
     j = (INV_J * (column + (plane - STEP_E) * own)) % plane
     shard = take_shard(jnp.stack([j // cores, j % cores]).astype(jnp.int32), w_in, w_out, blocks)
+    shard, picks = lax.optimization_barrier((shard, picks))
     shard = lax.ppermute(shard, ALL, scatter_pairs(sizes))
-    weights = lax.all_gather(shard, ("block", "core"))
-    weights = weights.reshape(blocks, cores, *shard.shape)
+    weights = spread(shard, sizes)
 
     pick_row = picks.reshape(1, experts * cap)
     live = lax.broadcasted_iota(jnp.int32, (experts, cap), 1) < counts[0][:, None]
@@ -299,8 +374,10 @@
         chosen.reshape(near, -1, width), NEAR, split_axis=0, concat_axis=0, tiled=True
     )
     query = lax.all_gather(queries, SEQ, tiled=True)
-
-    result = expert(there.reshape(-1, width), weights)
+    there, query = lax.optimization_barrier((there, query))
+
+    place, gathered, own_part, ring, early, late = weights
+    result = expert(place, there.reshape(-1, width), gathered, own_part, ring, early, late)
     back = lax.all_to_all(
         result.reshape(near, -1, width), NEAR, split_axis=0, concat_axis=0, tiled=True
     ).reshape(-1, width)

time: 235 us -> 244 us (1.038)
  starting transfers between devices: 32.6 us -> 115 us
  blocking collectives: 68.4 us -> 28.8 us
  waiting for transfers between devices: 99 us -> 65.5 us
  Pallas kernels: 9.89 us -> 16.4 us
  local copies, waits for them, and re-layouts: 8.59 us -> 2.37 us
    all_gather x1, waiting for transfers between devices: 94.6 us -> 5.56 us  [spread(): gathered = lax.all_gather(shard[:half], ('block', 'core'))]
    ppermute x0 -> x11, starting transfers between devices: none -> 61.4 us  [the longest x8 44.5 us: spread(): held = lax.ppermute(held, ('block', 'core'), turns)]
    all_to_all x1 -> x0, blocking collectives: 38.9 us -> none  [local(): lax.all_to_all(chosen.reshape(near, -1, width), NEAR, split_axis=0, conca...]
    ppermute x0 -> x11, waiting for transfers between devices: none -> 37.9 us  [the longest x8 36.7 us: spread(): held = lax.ppermute(held, ('block', 'core'), turns)]
    all_to_all x0 -> x1, starting transfers between devices: none -> 18.1 us  [local(): lax.all_to_all(chosen.reshape(near, -1, width), NEAR, split_axis=0, conca...]
    all_to_all x1, waiting for transfers between devices: 0.01 us -> 17.6 us  [local(): lax.all_to_all(result.reshape(near, -1, width), NEAR, split_axis=0, conca...]
    all_to_all x1, starting transfers between devices: 9.05 us -> 21.2 us  [local(): lax.all_to_all(result.reshape(near, -1, width), NEAR, split_axis=0, conca...]
    ppermute x1, starting transfers between devices: 23.5 us -> 13.9 us  [local(): shard = lax.ppermute(shard, ALL, scatter_pairs(sizes))]
  transfers between devices with their start and end apart: 3 -> 15, of which waited for: 2 -> 10; matrix products, arithmetic and copies ran while one was open for 0% -> 1% of each run, Pallas kernels for 0% -> 0%
where the time goes in v2:
time: 244 us
  starting transfers between devices  115 us (47%)
  waiting for transfers between devices  65.5 us (27%)
  blocking collectives  28.8 us (12%)
  Pallas kernels  16.4 us (7%)
  between operations  14.4 us (6%)
    ppermute x8, starting transfers between devices, spread(): held = lax.ppermute(held, ('block', 'core'), turns)  44.5 us
    ppermute x8, waiting for transfers between devices, spread(): held = lax.ppermute(held, ('block', 'core'), turns)  36.7 us
    all_to_all x1, starting transfers between devices, local(): lax.all_to_all(result.reshape(near, -1, width), NEAR, split_axis=0, conca...  21.2 us
    all_gather x1, blocking collectives, local(): query = lax.all_gather(queries, SEQ, tiled=True)  18.4 us
    all_to_all x1, starting transfers between devices, local(): lax.all_to_all(chosen.reshape(near, -1, width), NEAR, split_axis=0, conca...  18.1 us
    all_to_all x1, waiting for transfers between devices, local(): lax.all_to_all(result.reshape(near, -1, width), NEAR, split_axis=0, conca...  17.6 us
    ppermute x1, starting transfers between devices, local(): shard = lax.ppermute(shard, ALL, scatter_pairs(sizes))  13.9 us
    all_to_all x1, blocking collectives, local(): lax.all_to_all(packet.reshape(group, -1, packet.shape[1]), SEQ, split_axi...  10.4 us
  transfers between devices with their start and end apart: 15, of which 10 were waited for; matrix products, arithmetic and copies ran while one was open for 1% of the time, Pallas kernels for 0%

profile of v2, /device:TPU:1, one launch (start us, length us, event | category | flops | bytes accessed | tf_op | source)
XLA Modules:
  0.0 243.7 jit_solution(10167133725248837453)
XLA Ops:
  7.2 0.6 pad_add_fusion.1.which
  7.8 2.7 %shard_map.131 = bf16[64,1408]{1,0:T(8,128)(2,1)} custom-call(s32[2]{0:T(128)} %pad_add_fusion.1.which, bf16[1,1024,1408]{2,1,0:T(8,128)(2,1)} %w_in_ref.1, bf16[1,1408,1024]{2,1,0:T(8,128)(2,1)} %w_out_ref.1), custom_call_target="tpu_custom_call" | custom-call | tf_op jit(solution)/shard_map/pallas_call | solution.py:50
  10.6 0.1 copy.16
  10.6 0.1 reshape.59.picks_ref
  10.7 0.0 copy-start.7
  10.7 1.5 shard_map.132
  12.3 18.1 %all-to-all-start = ((bf16[64,8,1024]{2,1,0:T(8,128)(2,1)}), bf16[64,8,1024]{2,1,0:T(8,128)(2,1)S(1)}, u32[]{:S(2)}, u32[]{:S(2)}) async-start(bf16[64,8,1024]{2,1,0:T(8,128)(2,1)} %bitcast.5), calls=%async_computation | async-start | bytes 2097152 | tf_op jit(solution)/shard_map/all_to_all | solution.py:373
  30.3 0.0 all-gather.3.cloned.1.call-start
  30.4 13.9 %collective-permute-start = (bf16[64,1408]{1,0:T(8,128)(2,1)S(1)}, bf16[64,1408]{1,0:T(8,128)(2,1)S(1)}, u32[]{:S(2)}, u32[]{:S(2)}) collective-permute-start(bf16[64,1408]{1,0:T(8,128)(2,1)S(1)} %copy-done.7), channel_id=1, source_target_pairs={{0,0},{257,1},{514,16},{771,17},{4,32},{261,33},{518,48},{775,49},... | collective-permute-start | bytes 540680 | tf_op jit(solution)/shard_map/ppermute | solution.py:365
  44.3 4.4 %collective-permute-done = bf16[64,1408]{1,0:T(8,128)(2,1)S(1)} collective-permute-done((bf16[64,1408]{1,0:T(8,128)(2,1)S(1)}, bf16[64,1408]{1,0:T(8,128)(2,1)S(1)}, u32[]{:S(2)}, u32[]{:S(2)}) %collective-permute-start) | collective-permute-done | bytes 180256 | tf_op jit(solution)/shard_map/ppermute | solution.py:365
  48.7 0.7 fusion
  49.4 0.0 all-gather.3.cloned.1.call-update
  49.4 1.9 collective-permute-start.1
  51.3 0.0 copy-start.16
  51.3 1.2 collective-permute-done.1
  52.6 0.0 copy-start.8
  52.6 10.6 %collective-permute-start.2 = (bf16[64,1408]{1,0:T(8,128)(2,1)S(1)}, bf16[64,1408]{1,0:T(8,128)(2,1)S(1)}, u32[]{:S(2)}, u32[]{:S(2)}) collective-permute-start(bf16[64,1408]{1,0:T(8,128)(2,1)S(1)} %maximum_select_fusion.own_ref), channel_id=1, source_target_pairs={{0,16},{1,241},{16,32},{17,1},{32,48},{33,17},{48,64},{49,33},{64,... | collective-permute-start | bytes 540680 | tf_op jit(solution)/shard_map/ppermute | solution.py:205
  63.3 5.2 %collective-permute-done.2.refs_0_ = bf16[64,1408]{1,0:T(8,128)(2,1)S(1)} collective-permute-done((bf16[64,1408]{1,0:T(8,128)(2,1)S(1)}, bf16[64,1408]{1,0:T(8,128)(2,1)S(1)}, u32[]{:S(2)}, u32[]{:S(2)}) %collective-permute-start.2) | collective-permute-done | bytes 180256 | tf_op jit(solution)/shard_map/ppermute | solution.py:205
  68.4 6.6 %collective-permute-start.3 = (bf16[64,1408]{1,0:T(8,128)(2,1)S(1)}, bf16[64,1408]{1,0:T(8,128)(2,1)S(1)}, u32[]{:S(2)}, u32[]{:S(2)}) collective-permute-start(bf16[64,1408]{1,0:T(8,128)(2,1)S(1)} %collective-permute-done.2.refs_0_), channel_id=1, source_target_pairs={{0,16},{1,241},{16,32},{17,1},{32,48},{33,17},{48,64},{49,33},{64,... | collective-permute-start | bytes 540680 | tf_op jit(solution)/shard_map/ppermute | solution.py:205
  75.0 4.4 %collective-permute-done.3.refs_1_ = bf16[64,1408]{1,0:T(8,128)(2,1)S(1)} collective-permute-done((bf16[64,1408]{1,0:T(8,128)(2,1)S(1)}, bf16[64,1408]{1,0:T(8,128)(2,1)S(1)}, u32[]{:S(2)}, u32[]{:S(2)}) %collective-permute-start.3) | collective-permute-done | bytes 180256 | tf_op jit(solution)/shard_map/ppermute | solution.py:205
  79.5 4.0 %collective-permute-start.4 = (bf16[64,1408]{1,0:T(8,128)(2,1)S(1)}, bf16[64,1408]{1,0:T(8,128)(2,1)S(1)}, u32[]{:S(2)}, u32[]{:S(2)}) collective-permute-start(bf16[64,1408]{1,0:T(8,128)(2,1)S(1)} %collective-permute-done.3.refs_1_), channel_id=1, source_target_pairs={{0,16},{1,241},{16,32},{17,1},{32,48},{33,17},{48,64},{49,33},{64,... | collective-permute-start | bytes 540680 | tf_op jit(solution)/shard_map/ppermute | solution.py:205
  83.5 6.3 %collective-permute-done.4.refs_2_ = bf16[64,1408]{1,0:T(8,128)(2,1)S(1)} collective-permute-done((bf16[64,1408]{1,0:T(8,128)(2,1)S(1)}, bf16[64,1408]{1,0:T(8,128)(2,1)S(1)}, u32[]{:S(2)}, u32[]{:S(2)}) %collective-permute-start.4) | collective-permute-done | bytes 180256 | tf_op jit(solution)/shard_map/ppermute | solution.py:205
  89.8 2.1 collective-permute-start.5
  91.9 8.6 %collective-permute-done.5.refs_3_ = bf16[64,1408]{1,0:T(8,128)(2,1)S(1)} collective-permute-done((bf16[64,1408]{1,0:T(8,128)(2,1)S(1)}, bf16[64,1408]{1,0:T(8,128)(2,1)S(1)}, u32[]{:S(2)}, u32[]{:S(2)}) %collective-permute-start.5) | collective-permute-done | bytes 180256 | tf_op jit(solution)/shard_map/ppermute | solution.py:205
  100.5 2.3 collective-permute-start.6
  102.9 5.5 %collective-permute-done.6.refs_4_ = bf16[64,1408]{1,0:T(8,128)(2,1)S(1)} collective-permute-done((bf16[64,1408]{1,0:T(8,128)(2,1)S(1)}, bf16[64,1408]{1,0:T(8,128)(2,1)S(1)}, u32[]{:S(2)}, u32[]{:S(2)}) %collective-permute-start.6) | collective-permute-done | bytes 180256 | tf_op jit(solution)/shard_map/ppermute | solution.py:205
  108.3 9.3 %collective-permute-start.7 = (bf16[64,1408]{1,0:T(8,128)(2,1)S(1)}, bf16[64,1408]{1,0:T(8,128)(2,1)S(1)}, u32[]{:S(2)}, u32[]{:S(2)}) collective-permute-start(bf16[64,1408]{1,0:T(8,128)(2,1)S(1)} %collective-permute-done.6.refs_4_), channel_id=1, source_target_pairs={{0,16},{1,241},{16,32},{17,1},{32,48},{33,17},{48,64},{49,33},{64,... | collective-permute-start | bytes 540680 | tf_op jit(solution)/shard_map/ppermute | solution.py:205
  117.6 6.7 %collective-permute-done.7.refs_5_ = bf16[64,1408]{1,0:T(8,128)(2,1)S(1)} collective-permute-done((bf16[64,1408]{1,0:T(8,128)(2,1)S(1)}, bf16[64,1408]{1,0:T(8,128)(2,1)S(1)}, u32[]{:S(2)}, u32[]{:S(2)}) %collective-permute-start.7) | collective-permute-done | bytes 180256 | tf_op jit(solution)/shard_map/ppermute | solution.py:205
  124.3 5.9 %collective-permute-start.8 = (bf16[64,1408]{1,0:T(8,128)(2,1)S(1)}, bf16[64,1408]{1,0:T(8,128)(2,1)S(1)}, u32[]{:S(2)}, u32[]{:S(2)}) collective-permute-start(bf16[64,1408]{1,0:T(8,128)(2,1)S(1)} %collective-permute-done.7.refs_5_), channel_id=1, source_target_pairs={{0,16},{1,241},{16,32},{17,1},{32,48},{33,17},{48,64},{49,33},{64,... | collective-permute-start | bytes 540680 | tf_op jit(solution)/shard_map/ppermute | solution.py:205
  130.3 0.1 pad_maximum_fusion
  130.3 8.3 %collective-permute-start.10 = (bf16[256,1408]{1,0:T(8,128)(2,1)S(1)}, bf16[256,1408]{1,0:T(8,128)(2,1)}, u32[]{:S(2)}, u32[]{:S(2)}) collective-permute-start(bf16[256,1408]{1,0:T(8,128)(2,1)S(1)} %pad_maximum_fusion), channel_id=1, source_target_pairs={{0,1},{1,0},{2,3},{3,2},{4,5},{5,4},{6,7},{7,6},{8,9},{9,8},{10,11... | collective-permute-start | bytes 2162696 | tf_op jit(solution)/shard_map/ppermute | solution.py:208
  138.7 6.7 %collective-permute-start.11 = (bf16[192,1408]{1,0:T(8,128)(2,1)S(1)}, bf16[192,1408]{1,0:T(8,128)(2,1)}, u32[]{:S(2)}, u32[]{:S(2)}) collective-permute-start(bf16[192,1408]{1,0:T(8,128)(2,1)S(1)} %pad_maximum_fusion.1), channel_id=1, source_target_pairs={{0,1},{1,0},{2,3},{3,2},{4,5},{5,4},{6,7},{7,6},{8,9},{9,8},{10,11... | collective-permute-start | bytes 1622024 | tf_op jit(solution)/shard_map/ppermute | solution.py:209
  145.5 3.7 %collective-permute-start.9 = (bf16[64,1408]{1,0:T(8,128)(2,1)S(1)}, bf16[64,1408]{1,0:T(8,128)(2,1)S(1)}, u32[]{:S(2)}, u32[]{:S(2)}) collective-permute-start(bf16[64,1408]{1,0:T(8,128)(2,1)S(1)} %collective-permute-done.8.refs_6_), channel_id=1, source_target_pairs={{0,16},{1,241},{16,32},{17,1},{32,48},{33,17},{48,64},{49,33},{64,... | collective-permute-start | bytes 540680 | tf_op jit(solution)/shard_map/ppermute | solution.py:205
  149.1 0.6 pad_add_fusion.place
  149.8 18.4 %all_gather.9.query_ref = bf16[256,512]{1,0:T(8,128)(2,1)S(1)} all-gather(bf16[32,512]{1,0:T(8,128)(2,1)S(1)} %copy-done.16), channel_id=1, replica_groups=mesh['dp'=4,'block'=16,'parity'=2,'row'=4,'core'=2] {'row','core'}, dimensions={0}, use_global_device_ids=true | all-gather | bytes 294912 | tf_op jit(solution)/shard_map/all_gather | solution.py:376
  168.2 5.6 %all-gather.3.cloned.1.call-done = bf16[1024,1408]{1,0:T(8,128)(2,1)} async-done(((bf16[32,1408]{1,0:T(8,128)(2,1)}), bf16[1024,1408]{1,0:T(8,128)(2,1)}) %all-gather.3.cloned.1.call-update) | async-done | bytes 2883600 | tf_op jit(solution)/shard_map/all_gather | solution.py:188
  173.8 8.6 %shard_map.133 = bf16[512,1024]{1,0:T(8,128)(2,1)} custom-call(s32[2]{0:T(128)} %pad_add_fusion.place, bf16[512,1024]{1,0:T(8,128)(2,1)} %bitcast.17, bf16[16,2,32,1408]{3,2,1,0:T(8,128)(2,1)} %bitcast.20, bf16[64,1408]{1,0:T(8,128)(2,1)} %copy-done.8, bf16[64,1408]{1,0:T(8,128)(2,1)} %copy-done.9, bf16[64,1408]{1,0:T(8,128)(2,1)} %copy-done.10, ...), custom_call_target="tpu_custom_call" | custom-call | flops 2952790016 | bytes 7864320 | tf_op jit(solution)/shard_map/pallas_call | solution.py:164
  182.4 0.0 copy-start.1
  182.5 21.2 %all-to-all-start.1 = ((bf16[64,8,1024]{2,1,0:T(8,128)(2,1)}), bf16[64,8,1024]{2,1,0:T(8,128)(2,1)S(1)}, u32[]{:S(2)}, u32[]{:S(2)}) async-start(bf16[64,8,1024]{2,1,0:T(8,128)(2,1)} %bitcast.18), calls=%async_computation.1 | async-start | bytes 2097152 | tf_op jit(solution)/shard_map/all_to_all | solution.py:381
  203.7 0.1 copy.17
  203.8 0.1 squeeze.3
  203.9 0.1 iota_compare_fusion
  203.9 0.1 lt.35
  204.0 17.6 %all-to-all-done.1 = bf16[64,8,1024]{2,1,0:T(8,128)(2,1)S(1)} async-done(((bf16[64,8,1024]{2,1,0:T(8,128)(2,1)}), bf16[64,8,1024]{2,1,0:T(8,128)(2,1)S(1)}, u32[]{:S(2)}, u32[]{:S(2)}) %all-to-all-start.1) | async-done | bytes 1048608 | tf_op jit(solution)/shard_map/all_to_all | solution.py:381
  221.6 1.2 copy-done.2
  222.9 2.0 shard_map.134
  224.9 10.4 %all_to_all.15.got_ref = bf16[8,32,640]{2,1,0:T(8,128)(2,1)S(1)} all-to-all(bf16[8,32,640]{2,1,0:T(8,128)(2,1)S(1)} %bitcast.14), channel_id=1, replica_groups=mesh['dp'=4,'block'=16,'parity'=2,'row'=4,'core'=2] {'row','core'}, dimensions={0} | all-to-all | bytes 655360 | tf_op jit(solution)/shard_map/all_to_all | solution.py:388
  235.3 1.5 shard_map.135
  (45 shorter events, 0.2 us)
Async XLA Ops:
  7.8 2.7 %copy-start.17 = (s32[1,32,16]{1,2,0:T(8,128)S(1)}, s32[1,32,16]{1,2,0:T(8,128)}, u32[]{:S(2)}) copy-start(s32[1,32,16]{1,2,0:T(8,128)} %param.13) | copy-start | bytes 6148
  7.8 2.9 %copy-start = (bf16[128,1024]{1,0:T(8,128)(2,1)S(1)}, bf16[128,1024]{1,0:T(8,128)(2,1)}, u32[]{:S(2)}) copy-start(bf16[128,1024]{1,0:T(8,128)(2,1)} %tokens_ref.3) | copy-start | bytes 786436
  7.8 2.9 %copy-start.4 = (f32[1024]{0:T(1024)S(1)}, f32[1024]{0:T(1024)}, u32[]{:S(2)}) copy-start(f32[1024]{0:T(1024)} %param.16) | copy-start | bytes 12292
  10.7 19.7 %copy-start.7 = (bf16[64,1408]{1,0:T(8,128)(2,1)S(1)}, bf16[64,1408]{1,0:T(8,128)(2,1)}, u32[]{:S(2)}) copy-start(bf16[64,1408]{1,0:T(8,128)(2,1)} %shard_map.131) | copy-start | bytes 540676
  12.3 155.9 %all-to-all-start = ((bf16[64,8,1024]{2,1,0:T(8,128)(2,1)}), bf16[64,8,1024]{2,1,0:T(8,128)(2,1)S(1)}, u32[]{:S(2)}, u32[]{:S(2)}) async-start(bf16[64,8,1024]{2,1,0:T(8,128)(2,1)} %bitcast.5), calls=%async_computation | async-start | bytes 2097152 | tf_op jit(solution)/shard_map/all_to_all | solution.py:373
  30.3 143.4 %all-gather.3.cloned.1.call-start = ((), (), s32[]{:S(2)}) async-start(), calls=%async_computation.3 | async-start | bytes 2973696 | tf_op jit(solution)/shard_map/all_gather | solution.py:188
  30.4 18.3 %collective-permute-start = (bf16[64,1408]{1,0:T(8,128)(2,1)S(1)}, bf16[64,1408]{1,0:T(8,128)(2,1)S(1)}, u32[]{:S(2)}, u32[]{:S(2)}) collective-permute-start(bf16[64,1408]{1,0:T(8,128)(2,1)S(1)} %copy-done.7), channel_id=1, source_target_pairs={{0,0},{257,1},{514,16},{771,17},{4,32},{261,33},{518,48},{775,49},... | collective-permute-start | bytes 540680 | tf_op jit(solution)/shard_map/ppermute | solution.py:365
  49.4 3.2 %collective-permute-start.1 = (bf16[32,1408]{1,0:T(8,128)(2,1)S(1)}, bf16[32,1408]{1,0:T(8,128)(2,1)S(1)}, u32[]{:S(2)}, u32[]{:S(2)}) collective-permute-start(bf16[32,1408]{1,0:T(8,128)(2,1)S(1)} %get-tuple-element.14), channel_id=1, source_target_pairs={{0,1},{1,0},{2,3},{3,2},{4,5},{5,4},{6,7},{7,6},{8,9},{9,8},{10,11... | collective-permute-start | bytes 270344 | tf_op jit(solution)/shard_map/ppermute | solution.py:193
  51.3 98.5 %copy-start.16 = (bf16[32,512]{1,0:T(8,128)(2,1)S(1)}, bf16[32,512]{1,0:T(8,128)(2,1)}, u32[]{:S(2)}) copy-start(bf16[32,512]{1,0:T(8,128)(2,1)} %param.22) | copy-start | bytes 98308
  52.6 121.2 %copy-start.8 = (bf16[64,1408]{1,0:T(8,128)(2,1)}, bf16[64,1408]{1,0:T(8,128)(2,1)S(1)}, u32[]{:S(2)}) copy-start(bf16[64,1408]{1,0:T(8,128)(2,1)S(1)} %maximum_select_fusion.own_ref) | copy-start | bytes 540676
  52.6 15.8 %collective-permute-start.2 = (bf16[64,1408]{1,0:T(8,128)(2,1)S(1)}, bf16[64,1408]{1,0:T(8,128)(2,1)S(1)}, u32[]{:S(2)}, u32[]{:S(2)}) collective-permute-start(bf16[64,1408]{1,0:T(8,128)(2,1)S(1)} %maximum_select_fusion.own_ref), channel_id=1, source_target_pairs={{0,16},{1,241},{16,32},{17,1},{32,48},{33,17},{48,64},{49,33},{64,... | collective-permute-start | bytes 540680 | tf_op jit(solution)/shard_map/ppermute | solution.py:205
  68.4 80.7 %copy-start.9 = (bf16[64,1408]{1,0:T(8,128)(2,1)}, bf16[64,1408]{1,0:T(8,128)(2,1)S(1)}, u32[]{:S(2)}) copy-start(bf16[64,1408]{1,0:T(8,128)(2,1)S(1)} %collective-permute-done.2.refs_0_) | copy-start | bytes 540676
  68.4 11.0 %collective-permute-start.3 = (bf16[64,1408]{1,0:T(8,128)(2,1)S(1)}, bf16[64,1408]{1,0:T(8,128)(2,1)S(1)}, u32[]{:S(2)}, u32[]{:S(2)}) collective-permute-start(bf16[64,1408]{1,0:T(8,128)(2,1)S(1)} %collective-permute-done.2.refs_0_), channel_id=1, source_target_pairs={{0,16},{1,241},{16,32},{17,1},{32,48},{33,17},{48,64},{49,33},{64,... | collective-permute-start | bytes 540680 | tf_op jit(solution)/shard_map/ppermute | solution.py:205
  79.5 59.1 %copy-start.10 = (bf16[64,1408]{1,0:T(8,128)(2,1)}, bf16[64,1408]{1,0:T(8,128)(2,1)S(1)}, u32[]{:S(2)}) copy-start(bf16[64,1408]{1,0:T(8,128)(2,1)S(1)} %collective-permute-done.3.refs_1_) | copy-start | bytes 540676
  79.5 10.3 %collective-permute-start.4 = (bf16[64,1408]{1,0:T(8,128)(2,1)S(1)}, bf16[64,1408]{1,0:T(8,128)(2,1)S(1)}, u32[]{:S(2)}, u32[]{:S(2)}) collective-permute-start(bf16[64,1408]{1,0:T(8,128)(2,1)S(1)} %collective-permute-done.3.refs_1_), channel_id=1, source_target_pairs={{0,16},{1,241},{16,32},{17,1},{32,48},{33,17},{48,64},{49,33},{64,... | collective-permute-start | bytes 540680 | tf_op jit(solution)/shard_map/ppermute | solution.py:205
  89.8 48.9 %copy-start.11 = (bf16[64,1408]{1,0:T(8,128)(2,1)}, bf16[64,1408]{1,0:T(8,128)(2,1)S(1)}, u32[]{:S(2)}) copy-start(bf16[64,1408]{1,0:T(8,128)(2,1)S(1)} %collective-permute-done.4.refs_2_) | copy-start | bytes 540676
  89.8 10.7 %collective-permute-start.5 = (bf16[64,1408]{1,0:T(8,128)(2,1)S(1)}, bf16[64,1408]{1,0:T(8,128)(2,1)S(1)}, u32[]{:S(2)}, u32[]{:S(2)}) collective-permute-start(bf16[64,1408]{1,0:T(8,128)(2,1)S(1)} %collective-permute-done.4.refs_2_), channel_id=1, source_target_pairs={{0,16},{1,241},{16,32},{17,1},{32,48},{33,17},{48,64},{49,33},{64,... | collective-permute-start | bytes 540680 | tf_op jit(solution)/shard_map/ppermute | solution.py:205
  100.5 38.1 %copy-start.12 = (bf16[64,1408]{1,0:T(8,128)(2,1)}, bf16[64,1408]{1,0:T(8,128)(2,1)S(1)}, u32[]{:S(2)}) copy-start(bf16[64,1408]{1,0:T(8,128)(2,1)S(1)} %collective-permute-done.5.refs_3_) | copy-start | bytes 540676
  100.5 7.8 %collective-permute-start.6 = (bf16[64,1408]{1,0:T(8,128)(2,1)S(1)}, bf16[64,1408]{1,0:T(8,128)(2,1)S(1)}, u32[]{:S(2)}, u32[]{:S(2)}) collective-permute-start(bf16[64,1408]{1,0:T(8,128)(2,1)S(1)} %collective-permute-done.5.refs_3_), channel_id=1, source_target_pairs={{0,16},{1,241},{16,32},{17,1},{32,48},{33,17},{48,64},{49,33},{64,... | collective-permute-start | bytes 540680 | tf_op jit(solution)/shard_map/ppermute | solution.py:205
  108.3 30.3 %copy-start.13 = (bf16[64,1408]{1,0:T(8,128)(2,1)}, bf16[64,1408]{1,0:T(8,128)(2,1)S(1)}, u32[]{:S(2)}) copy-start(bf16[64,1408]{1,0:T(8,128)(2,1)S(1)} %collective-permute-done.6.refs_4_) | copy-start | bytes 540676
  108.3 16.0 %collective-permute-start.7 = (bf16[64,1408]{1,0:T(8,128)(2,1)S(1)}, bf16[64,1408]{1,0:T(8,128)(2,1)S(1)}, u32[]{:S(2)}, u32[]{:S(2)}) collective-permute-start(bf16[64,1408]{1,0:T(8,128)(2,1)S(1)} %collective-permute-done.6.refs_4_), channel_id=1, source_target_pairs={{0,16},{1,241},{16,32},{17,1},{32,48},{33,17},{48,64},{49,33},{64,... | collective-permute-start | bytes 540680 | tf_op jit(solution)/shard_map/ppermute | solution.py:205
  124.3 14.4 %copy-start.14 = (bf16[64,1408]{1,0:T(8,128)(2,1)}, bf16[64,1408]{1,0:T(8,128)(2,1)S(1)}, u32[]{:S(2)}) copy-start(bf16[64,1408]{1,0:T(8,128)(2,1)S(1)} %collective-permute-done.7.refs_5_) | copy-start | bytes 540676
  124.3 14.3 %collective-permute-start.8 = (bf16[64,1408]{1,0:T(8,128)(2,1)S(1)}, bf16[64,1408]{1,0:T(8,128)(2,1)S(1)}, u32[]{:S(2)}, u32[]{:S(2)}) collective-permute-start(bf16[64,1408]{1,0:T(8,128)(2,1)S(1)} %collective-permute-done.7.refs_5_), channel_id=1, source_target_pairs={{0,16},{1,241},{16,32},{17,1},{32,48},{33,17},{48,64},{49,33},{64,... | collective-permute-start | bytes 540680 | tf_op jit(solution)/shard_map/ppermute | solution.py:205
  130.3 37.8 %collective-permute-start.10 = (bf16[256,1408]{1,0:T(8,128)(2,1)S(1)}, bf16[256,1408]{1,0:T(8,128)(2,1)}, u32[]{:S(2)}, u32[]{:S(2)}) collective-permute-start(bf16[256,1408]{1,0:T(8,128)(2,1)S(1)} %pad_maximum_fusion), channel_id=1, source_target_pairs={{0,1},{1,0},{2,3},{3,2},{4,5},{5,4},{6,7},{7,6},{8,9},{9,8},{10,11... | collective-permute-start | bytes 2162696 | tf_op jit(solution)/shard_map/ppermute | solution.py:208
  138.7 29.5 %copy-start.15 = (bf16[64,1408]{1,0:T(8,128)(2,1)}, bf16[64,1408]{1,0:T(8,128)(2,1)S(1)}, u32[]{:S(2)}) copy-start(bf16[64,1408]{1,0:T(8,128)(2,1)S(1)} %collective-permute-done.8.refs_6_) | copy-start | bytes 540676
  138.7 29.5 %collective-permute-start.11 = (bf16[192,1408]{1,0:T(8,128)(2,1)S(1)}, bf16[192,1408]{1,0:T(8,128)(2,1)}, u32[]{:S(2)}, u32[]{:S(2)}) collective-permute-start(bf16[192,1408]{1,0:T(8,128)(2,1)S(1)} %pad_maximum_fusion.1), channel_id=1, source_target_pairs={{0,1},{1,0},{2,3},{3,2},{4,5},{5,4},{6,7},{7,6},{8,9},{9,8},{10,11... | collective-permute-start | bytes 1622024 | tf_op jit(solution)/shard_map/ppermute | solution.py:209
  145.5 22.7 %collective-permute-start.9 = (bf16[64,1408]{1,0:T(8,128)(2,1)S(1)}, bf16[64,1408]{1,0:T(8,128)(2,1)S(1)}, u32[]{:S(2)}, u32[]{:S(2)}) collective-permute-start(bf16[64,1408]{1,0:T(8,128)(2,1)S(1)} %collective-permute-done.8.refs_6_), channel_id=1, source_target_pairs={{0,16},{1,241},{16,32},{17,1},{32,48},{33,17},{48,64},{49,33},{64,... | collective-permute-start | bytes 540680 | tf_op jit(solution)/shard_map/ppermute | solution.py:205
  168.2 5.6 %copy-start.6 = (bf16[64,8,1024]{2,1,0:T(8,128)(2,1)}, bf16[64,8,1024]{2,1,0:T(8,128)(2,1)S(1)}, u32[]{:S(2)}) copy-start(bf16[64,8,1024]{2,1,0:T(8,128)(2,1)S(1)} %all-to-all-done) | copy-start | bytes 3145732
  168.2 5.6 %copy-start.20 = (bf16[64,1408]{1,0:T(8,128)(2,1)}, bf16[64,1408]{1,0:T(8,128)(2,1)S(1)}, u32[]{:S(2)}) copy-start(bf16[64,1408]{1,0:T(8,128)(2,1)S(1)} %collective-permute-done.9.refs_7_) | copy-start | bytes 540676
  182.4 21.3 %copy-start.18 = (f32[1,32,16]{1,2,0:T(8,128)S(1)}, f32[1,32,16]{1,2,0:T(8,128)}, u32[]{:S(2)}) copy-start(f32[1,32,16]{1,2,0:T(8,128)} %param.14) | copy-start | bytes 6148
  182.4 21.4 %copy-start.19 = (s32[1,32]{1,0:T(1,128)S(1)}, s32[1,32]{1,0:T(1,128)}, u32[]{:S(2)}) copy-start(s32[1,32]{1,0:T(1,128)} %param.15) | copy-start | bytes 388
  182.4 39.2 %copy-start.1 = (bf16[1024,512]{1,0:T(8,128)(2,1)S(1)}, bf16[1024,512]{1,0:T(8,128)(2,1)}, u32[]{:S(2)}) copy-start(bf16[1024,512]{1,0:T(8,128)(2,1)} %key_ref.1) | copy-start | bytes 3145732
  182.5 39.2 %copy-start.5 = (f32[1024]{0:T(1024)S(1)}, f32[1024]{0:T(1024)}, u32[]{:S(2)}) copy-start(f32[1024]{0:T(1024)} %param.17) | copy-start | bytes 12292
  182.5 39.2 %all-to-all-start.1 = ((bf16[64,8,1024]{2,1,0:T(8,128)(2,1)}), bf16[64,8,1024]{2,1,0:T(8,128)(2,1)S(1)}, u32[]{:S(2)}, u32[]{:S(2)}) async-start(bf16[64,8,1024]{2,1,0:T(8,128)(2,1)} %bitcast.18), calls=%async_computation.1 | async-start | bytes 2097152 | tf_op jit(solution)/shard_map/all_to_all | solution.py:381
  221.6 1.2 copy-start.2
  222.9 12.5 %copy-start.3 = (bf16[512,1024]{1,0:T(8,128)(2,1)S(1)}, bf16[512,1024]{1,0:T(8,128)(2,1)}, u32[]{:S(2)}) copy-start(bf16[512,1024]{1,0:T(8,128)(2,1)} %proj_ref.1) | copy-start | bytes 3145732
Sparse Core Ops, SparseCore 0:
  49.5 124.2 all-gather.2

commit v3 on v2

--- a/solution.py
+++ b/solution.py
@@ -89,28 +89,22 @@
     return 0.5 * v * (1.0 + jnp.tanh(0.7978845608028654 * (v + 0.044715 * (v * v * v))))
 
 
-def expert_kernel(place, rows_ref, gathered_ref, own_ref, *refs):
-    blocks = gathered_ref.shape[0]
+def expert_kernel(blocks, place, rows_ref, own_ref, *refs):
     ring = refs[:-7]
     early, late, out_ref, w_in, w_out, middle, sems = refs[-7:]
     block, turn = place[0], place[1]
-    head = gathered_ref.shape[2]
-    rest = pl.ds(head, own_ref.shape[0] // 2)
+    size = own_ref.shape[0] // 2
 
     def at(offset):
         return lax.rem(block + offset + blocks, blocks)
 
     def halves(ref, start, index):
-        size = own_ref.shape[0] // 2
         return [
-            (ref.at[pl.ds(start + k * size, size)], buffer.at[index, rest])
+            (ref.at[pl.ds(start + k * size, size)], buffer.at[index])
             for k, buffer in enumerate((w_in, w_out))
         ]
 
-    jobs = [
-        [(gathered_ref.at[:, k], buffer.at[:, pl.ds(0, head)])]
-        for k, buffer in enumerate((w_in, w_out))
-    ]
+    jobs = [[], []]
     found = [halves(own_ref, 0, block)]
     for step, ref in enumerate(ring, 1):
         found.append(halves(ref, 0, at(-step * turn)))
@@ -156,40 +150,35 @@
         ).astype(BF16)
 
 
-def expert(place, rows, gathered, own, ring, early, late):
+def expert(blocks, place, rows, own, ring, early, late):
     total, width = rows.shape
-    blocks, _, head, hidden = gathered.shape
-    part = head + own.shape[0] // 2
+    part, hidden = own.shape[0] // 2, own.shape[1]
     anywhere = pl.BlockSpec(memory_space=pl.ANY)
     return pl.pallas_call(
-        expert_kernel,
+        functools.partial(expert_kernel, blocks),
         in_specs=[pl.BlockSpec(memory_space=pltpu.SMEM), _VM()]
-        + [anywhere] * (4 + len(ring)),
+        + [anywhere] * (3 + len(ring)),
         out_specs=_VM(),
         out_shape=jax.ShapeDtypeStruct((total, width), BF16),
         scratch_shapes=[
             pltpu.VMEM((blocks, part, hidden), BF16),
             pltpu.VMEM((blocks, part, hidden), BF16),
             pltpu.VMEM((total, hidden), BF16),
-            pltpu.SemaphoreType.DMA((2, 1 + 2 * len(ring))),
+            pltpu.SemaphoreType.DMA((2, 2 * len(ring))),
         ],
-        compiler_params=pltpu.CompilerParams(vmem_limit_bytes=FULL),
+        compiler_params=pltpu.CompilerParams(vmem_limit_bytes=VMEM // 2),
         cost_estimate=pl.CostEstimate(
             flops=4 * total * width * hidden,
             bytes_accessed=4 * width * hidden + 4 * total * width,
             transcendentals=total * hidden,
         ),
-    )(place, rows, gathered, own, *ring, early, late)
-
-
-def spread(shard, sizes):
+    )(place, rows, own, *ring, early, late)
+
+
+def spread(mine, sizes):
     _, blocks, _, _, cores = sizes
-    half = shard.shape[0] // 2
-    gathered = lax.all_gather(shard[:half], ("block", "core"))
-    gathered = gathered.reshape(blocks, cores, half, shard.shape[1])
     swap = [(0, 1), (1, 0)]
     core = lax.axis_index("core")
-    mine = shard[half:]
     other = lax.ppermute(mine, "core", swap)
     own = jnp.where(
         core == 0, jnp.concatenate([mine, other]), jnp.concatenate([other, mine])
@@ -208,7 +197,7 @@
     early = lax.ppermute(jnp.concatenate(ring[:cut]), "core", swap)
     late = lax.ppermute(jnp.concatenate(ring[cut : steps - 1]), "core", swap)
     place = jnp.stack([lax.axis_index("block"), 1 - 2 * core]).astype(jnp.int32)
-    return place, gathered, own, ring, early, late
+    return blocks, place, own, ring, early, late
 
 
 def pieces(v, count):
@@ -361,9 +350,10 @@
     )
     j = (INV_J * (column + (plane - STEP_E) * own)) % plane
     shard = take_shard(jnp.stack([j // cores, j % cores]).astype(jnp.int32), w_in, w_out, blocks)
-    shard, picks = lax.optimization_barrier((shard, picks))
     shard = lax.ppermute(shard, ALL, scatter_pairs(sizes))
-    weights = spread(shard, sizes)
+    query = lax.all_gather(queries, SEQ, tiled=True)
+    shard, query, picks = lax.optimization_barrier((shard, query, picks))
+    blocks, place, own_part, ring, early, late = spread(shard, sizes)
 
     pick_row = picks.reshape(1, experts * cap)
     live = lax.broadcasted_iota(jnp.int32, (experts, cap), 1) < counts[0][:, None]
@@ -373,11 +363,7 @@
     there = lax.all_to_all(
         chosen.reshape(near, -1, width), NEAR, split_axis=0, concat_axis=0, tiled=True
     )
-    query = lax.all_gather(queries, SEQ, tiled=True)
-    there, query = lax.optimization_barrier((there, query))
-
-    place, gathered, own_part, ring, early, late = weights
-    result = expert(place, there.reshape(-1, width), gathered, own_part, ring, early, late)
+    result = expert(blocks, place, there.reshape(-1, width), own_part, ring, early, late)
     back = lax.all_to_all(
         result.reshape(near, -1, width), NEAR, split_axis=0, concat_axis=0, tiled=True
     ).reshape(-1, width)

time: 244 us -> 247 us (1.012)
  waiting for transfers between devices: 65.5 us -> 79.9 us
  between operations: 14.4 us -> 0.89 us
  local copies, waits for them, and re-layouts: 2.37 us -> 5.59 us
  starting transfers between devices: 115 us -> 112 us
  other arithmetic: 1.47 us -> 4.14 us
    ppermute x8, waiting for transfers between devices: 36.7 us -> 61.3 us  [spread(): held = lax.ppermute(held, ('block', 'core'), turns)]
    ppermute x8, starting transfers between devices: 44.5 us -> 54.3 us  [spread(): held = lax.ppermute(held, ('block', 'core'), turns)]
    ppermute x1, starting transfers between devices: 13.9 us -> 23.5 us  [local(): shard = lax.ppermute(shard, ALL, scatter_pairs(sizes))]
    all_to_all x1, starting transfers between devices: 18.1 us -> 9.23 us  [local(): lax.all_to_all(chosen.reshape(near, -1, width), NEAR, split_axis=0, conca...]
    ppermute x1, starting transfers between devices: 8.28 us -> 1.91 us  [spread(): early = lax.ppermute(jnp.concatenate(ring[:cut]), 'core', swap)]
    all_gather x1 -> x0, waiting for transfers between devices: 5.56 us -> none  [spread(): gathered = lax.all_gather(shard[:half], ('block', 'core'))]
    ppermute x1, waiting for transfers between devices: 4.39 us -> 0.01 us  [local(): shard = lax.ppermute(shard, ALL, scatter_pairs(sizes))]
    ppermute x1, starting transfers between devices: 6.72 us -> 2.4 us  [spread(): late = lax.ppermute(jnp.concatenate(ring[cut:steps - 1]), 'core', swap)]
  transfers between devices with their start and end apart: 15 -> 14, of which waited for: 10 -> 10; matrix products, arithmetic and copies ran while one was open for 1% -> 2% of each run, Pallas kernels for 0% -> 0%
where the time goes in v3:
time: 247 us; the launch traced here: 246 us
  starting transfers between devices  112 us (45%)
  waiting for transfers between devices  79.9 us (32%)
  blocking collectives  27.2 us (11%)
  Pallas kernels  16.5 us (7%)
  local copies, waits for them, and re-layouts  5.59 us (2%)
  other arithmetic  4.14 us (2%)
    ppermute x8, waiting for transfers between devices, spread(): held = lax.ppermute(held, ('block', 'core'), turns)  61.3 us
    ppermute x8, starting transfers between devices, spread(): held = lax.ppermute(held, ('block', 'core'), turns)  54.3 us
    ppermute x1, starting transfers between devices, local(): shard = lax.ppermute(shard, ALL, scatter_pairs(sizes))  23.5 us
    all_to_all x1, starting transfers between devices, local(): lax.all_to_all(result.reshape(near, -1, width), NEAR, split_axis=0, conca...  18 us
    all_to_all x1, waiting for transfers between devices, local(): lax.all_to_all(result.reshape(near, -1, width), NEAR, split_axis=0, conca...  17.6 us
    all_gather x1, blocking collectives, local(): query = lax.all_gather(queries, SEQ, tiled=True)  16.8 us
    all_to_all x1, blocking collectives, local(): lax.all_to_all(packet.reshape(group, -1, packet.shape[1]), SEQ, split_axi...  10.4 us
    all_to_all x1, starting transfers between devices, local(): lax.all_to_all(chosen.reshape(near, -1, width), NEAR, split_axis=0, conca...  9.23 us
  transfers between devices with their start and end apart: 14, of which 10 were waited for; matrix products, arithmetic and copies ran while one was open for 2% of the time, Pallas kernels for 0%

profile of v3, /device:TPU:1, one launch (start us, length us, event | category | flops | bytes accessed | tf_op | source)
XLA Modules:
  0.0 246.0 jit_solution(18424258416338514807)
XLA Ops:
  0.7 0.7 pad_add_fusion.1.which
  1.3 2.7 %shard_map.131 = bf16[64,1408]{1,0:T(8,128)(2,1)} custom-call(s32[2]{0:T(128)} %pad_add_fusion.1.which, bf16[1,1024,1408]{2,1,0:T(8,128)(2,1)} %w_in_ref.1, bf16[1,1408,1024]{2,1,0:T(8,128)(2,1)} %w_out_ref.1), custom_call_target="tpu_custom_call" | custom-call | tf_op jit(solution)/shard_map/pallas_call | solution.py:50
  4.1 23.5 %collective-permute-start = (bf16[64,1408]{1,0:T(8,128)(2,1)}, bf16[64,1408]{1,0:T(8,128)(2,1)S(1)}, u32[]{:S(2)}, u32[]{:S(2)}) collective-permute-start(bf16[64,1408]{1,0:T(8,128)(2,1)} %shard_map.131), channel_id=1, source_target_pairs={{0,0},{257,1},{514,16},{771,17},{4,32},{261,33},{518,48},{775,49},... | collective-permute-start | bytes 540680 | tf_op jit(solution)/shard_map/ppermute | solution.py:353
  27.6 16.8 %all_gather.3.query_ref = bf16[256,512]{1,0:T(8,128)(2,1)S(1)} all-gather(bf16[32,512]{1,0:T(8,128)(2,1)S(1)} %copy-done.13), channel_id=1, replica_groups=mesh['dp'=4,'block'=16,'parity'=2,'row'=4,'core'=2] {'row','core'}, dimensions={0}, use_global_device_ids=true | all-gather | bytes 294912 | tf_op jit(solution)/shard_map/all_gather | solution.py:354
  44.4 0.0 collective-permute-done
  44.5 0.1 copy.16
  44.5 0.1 reshape.56.picks_ref
  44.6 1.5 shard_map.132
  46.2 9.2 %all-to-all-start = ((bf16[64,8,1024]{2,1,0:T(8,128)(2,1)}), bf16[64,8,1024]{2,1,0:T(8,128)(2,1)S(1)}, u32[]{:S(2)}, u32[]{:S(2)}) async-start(bf16[64,8,1024]{2,1,0:T(8,128)(2,1)} %bitcast.5), calls=%async_computation | async-start | bytes 2097152 | tf_op jit(solution)/shard_map/all_to_all | solution.py:363
  55.4 2.4 collective-permute-start.1
  57.8 1.0 collective-permute-done.1
  58.8 0.1 maximum_select_fusion.own_ref
  58.9 12.9 %collective-permute-start.2 = (bf16[128,1408]{1,0:T(8,128)(2,1)S(1)}, bf16[128,1408]{1,0:T(8,128)(2,1)S(1)}, u32[]{:S(2)}, u32[]{:S(2)}) collective-permute-start(bf16[128,1408]{1,0:T(8,128)(2,1)S(1)} %maximum_select_fusion.own_ref), channel_id=1, source_target_pairs={{0,16},{1,241},{16,32},{17,1},{32,48},{33,17},{48,64},{49,33},{64,... | collective-permute-start | bytes 1081352 | tf_op jit(solution)/shard_map/ppermute | solution.py:194
  71.8 8.3 %collective-permute-done.2.refs_0_ = bf16[128,1408]{1,0:T(8,128)(2,1)S(1)} collective-permute-done((bf16[128,1408]{1,0:T(8,128)(2,1)S(1)}, bf16[128,1408]{1,0:T(8,128)(2,1)S(1)}, u32[]{:S(2)}, u32[]{:S(2)}) %collective-permute-start.2) | collective-permute-done | bytes 360480 | tf_op jit(solution)/shard_map/ppermute | solution.py:194
  80.1 6.2 %collective-permute-start.3 = (bf16[128,1408]{1,0:T(8,128)(2,1)S(1)}, bf16[128,1408]{1,0:T(8,128)(2,1)S(1)}, u32[]{:S(2)}, u32[]{:S(2)}) collective-permute-start(bf16[128,1408]{1,0:T(8,128)(2,1)S(1)} %collective-permute-done.2.refs_0_), channel_id=1, source_target_pairs={{0,16},{1,241},{16,32},{17,1},{32,48},{33,17},{48,64},{49,33},{64,... | collective-permute-start | bytes 1081352 | tf_op jit(solution)/shard_map/ppermute | solution.py:194
  86.3 8.2 %collective-permute-done.3.refs_1_ = bf16[128,1408]{1,0:T(8,128)(2,1)S(1)} collective-permute-done((bf16[128,1408]{1,0:T(8,128)(2,1)S(1)}, bf16[128,1408]{1,0:T(8,128)(2,1)S(1)}, u32[]{:S(2)}, u32[]{:S(2)}) %collective-permute-start.3) | collective-permute-done | bytes 360480 | tf_op jit(solution)/shard_map/ppermute | solution.py:194
  94.5 5.9 %collective-permute-start.4 = (bf16[128,1408]{1,0:T(8,128)(2,1)S(1)}, bf16[128,1408]{1,0:T(8,128)(2,1)S(1)}, u32[]{:S(2)}, u32[]{:S(2)}) collective-permute-start(bf16[128,1408]{1,0:T(8,128)(2,1)S(1)} %collective-permute-done.3.refs_1_), channel_id=1, source_target_pairs={{0,16},{1,241},{16,32},{17,1},{32,48},{33,17},{48,64},{49,33},{64,... | collective-permute-start | bytes 1081352 | tf_op jit(solution)/shard_map/ppermute | solution.py:194
  100.4 8.1 %collective-permute-done.4.refs_2_ = bf16[128,1408]{1,0:T(8,128)(2,1)S(1)} collective-permute-done((bf16[128,1408]{1,0:T(8,128)(2,1)S(1)}, bf16[128,1408]{1,0:T(8,128)(2,1)S(1)}, u32[]{:S(2)}, u32[]{:S(2)}) %collective-permute-start.4) | collective-permute-done | bytes 360480 | tf_op jit(solution)/shard_map/ppermute | solution.py:194
  108.5 5.9 %collective-permute-start.5 = (bf16[128,1408]{1,0:T(8,128)(2,1)S(1)}, bf16[128,1408]{1,0:T(8,128)(2,1)S(1)}, u32[]{:S(2)}, u32[]{:S(2)}) collective-permute-start(bf16[128,1408]{1,0:T(8,128)(2,1)S(1)} %collective-permute-done.4.refs_2_), channel_id=1, source_target_pairs={{0,16},{1,241},{16,32},{17,1},{32,48},{33,17},{48,64},{49,33},{64,... | collective-permute-start | bytes 1081352 | tf_op jit(solution)/shard_map/ppermute | solution.py:194
  114.4 8.1 %collective-permute-done.5.refs_3_ = bf16[128,1408]{1,0:T(8,128)(2,1)S(1)} collective-permute-done((bf16[128,1408]{1,0:T(8,128)(2,1)S(1)}, bf16[128,1408]{1,0:T(8,128)(2,1)S(1)}, u32[]{:S(2)}, u32[]{:S(2)}) %collective-permute-start.5) | collective-permute-done | bytes 360480 | tf_op jit(solution)/shard_map/ppermute | solution.py:194
  122.5 5.9 %collective-permute-start.6 = (bf16[128,1408]{1,0:T(8,128)(2,1)S(1)}, bf16[128,1408]{1,0:T(8,128)(2,1)S(1)}, u32[]{:S(2)}, u32[]{:S(2)}) collective-permute-start(bf16[128,1408]{1,0:T(8,128)(2,1)S(1)} %collective-permute-done.5.refs_3_), channel_id=1, source_target_pairs={{0,16},{1,241},{16,32},{17,1},{32,48},{33,17},{48,64},{49,33},{64,... | collective-permute-start | bytes 1081352 | tf_op jit(solution)/shard_map/ppermute | solution.py:194
  128.5 8.1 %collective-permute-done.6.refs_4_ = bf16[128,1408]{1,0:T(8,128)(2,1)S(1)} collective-permute-done((bf16[128,1408]{1,0:T(8,128)(2,1)S(1)}, bf16[128,1408]{1,0:T(8,128)(2,1)S(1)}, u32[]{:S(2)}, u32[]{:S(2)}) %collective-permute-start.6) | collective-permute-done | bytes 360480 | tf_op jit(solution)/shard_map/ppermute | solution.py:194
  136.6 5.9 %collective-permute-start.7 = (bf16[128,1408]{1,0:T(8,128)(2,1)S(1)}, bf16[128,1408]{1,0:T(8,128)(2,1)S(1)}, u32[]{:S(2)}, u32[]{:S(2)}) collective-permute-start(bf16[128,1408]{1,0:T(8,128)(2,1)S(1)} %collective-permute-done.6.refs_4_), channel_id=1, source_target_pairs={{0,16},{1,241},{16,32},{17,1},{32,48},{33,17},{48,64},{49,33},{64,... | collective-permute-start | bytes 1081352 | tf_op jit(solution)/shard_map/ppermute | solution.py:194
  142.5 8.1 %collective-permute-done.7.refs_5_ = bf16[128,1408]{1,0:T(8,128)(2,1)S(1)} collective-permute-done((bf16[128,1408]{1,0:T(8,128)(2,1)S(1)}, bf16[128,1408]{1,0:T(8,128)(2,1)S(1)}, u32[]{:S(2)}, u32[]{:S(2)}) %collective-permute-start.7) | collective-permute-done | bytes 360480 | tf_op jit(solution)/shard_map/ppermute | solution.py:194
  150.6 5.9 %collective-permute-start.8 = (bf16[128,1408]{1,0:T(8,128)(2,1)S(1)}, bf16[128,1408]{1,0:T(8,128)(2,1)}, u32[]{:S(2)}, u32[]{:S(2)}) collective-permute-start(bf16[128,1408]{1,0:T(8,128)(2,1)S(1)} %collective-permute-done.7.refs_5_), channel_id=1, source_target_pairs={{0,16},{1,241},{16,32},{17,1},{32,48},{33,17},{48,64},{49,33},{64,... | collective-permute-start | bytes 1081352 | tf_op jit(solution)/shard_map/ppermute | solution.py:194
  156.5 1.2 pad_maximum_fusion
  157.7 1.9 collective-permute-start.10
  159.7 5.0 %collective-permute-done.8.refs_6_ = bf16[128,1408]{1,0:T(8,128)(2,1)} collective-permute-done((bf16[128,1408]{1,0:T(8,128)(2,1)S(1)}, bf16[128,1408]{1,0:T(8,128)(2,1)}, u32[]{:S(2)}, u32[]{:S(2)}) %collective-permute-start.8) | collective-permute-done | bytes 360480 | tf_op jit(solution)/shard_map/ppermute | solution.py:194
  164.6 2.0 pad_maximum_fusion.1
  166.7 2.4 collective-permute-start.11
  169.1 5.6 %collective-permute-start.9 = (bf16[128,1408]{1,0:T(8,128)(2,1)}, bf16[128,1408]{1,0:T(8,128)(2,1)}, u32[]{:S(2)}, u32[]{:S(2)}) collective-permute-start(bf16[128,1408]{1,0:T(8,128)(2,1)} %collective-permute-done.8.refs_6_), channel_id=1, source_target_pairs={{0,16},{1,241},{16,32},{17,1},{32,48},{33,17},{48,64},{49,33},{64,... | collective-permute-start | bytes 1081352 | tf_op jit(solution)/shard_map/ppermute | solution.py:194
  174.7 0.1 pad_add_fusion.place
  174.8 7.4 %collective-permute-done.9.refs_7_ = bf16[128,1408]{1,0:T(8,128)(2,1)} collective-permute-done((bf16[128,1408]{1,0:T(8,128)(2,1)}, bf16[128,1408]{1,0:T(8,128)(2,1)}, u32[]{:S(2)}, u32[]{:S(2)}) %collective-permute-start.9) | collective-permute-done | bytes 360480 | tf_op jit(solution)/shard_map/ppermute | solution.py:194
  182.1 1.0 copy-done.6
  183.1 1.0 copy-done.8
  184.1 1.0 copy-done.10
  185.1 8.8 %shard_map.133 = bf16[512,1024]{1,0:T(8,128)(2,1)S(1)} custom-call(s32[2]{0:T(128)S(1)} %pad_add_fusion.place, bf16[512,1024]{1,0:T(8,128)(2,1)S(1)} %bitcast.13, bf16[128,1408]{1,0:T(8,128)(2,1)S(1)} %maximum_select_fusion.own_ref, bf16[128,1408]{1,0:T(8,128)(2,1)S(1)} %collective-permute-done.2.refs_0_, ...), custom_call_target="tpu_custom_call" | custom-call | flops 2952790016 | bytes 7864320 | tf_op jit(solution)/shard_map/pallas_call | solution.py:157
  193.9 1.0 copy-done.4
  194.9 18.0 %all-to-all-start.1 = ((bf16[64,8,1024]{2,1,0:T(8,128)(2,1)}), bf16[64,8,1024]{2,1,0:T(8,128)(2,1)S(1)}, u32[]{:S(2)}, u32[]{:S(2)}) async-start(bf16[64,8,1024]{2,1,0:T(8,128)(2,1)} %bitcast.14), calls=%async_computation.1 | async-start | bytes 2097152 | tf_op jit(solution)/shard_map/all_to_all | solution.py:367
  212.9 0.1 copy.17
  213.0 0.1 squeeze.3
  213.1 0.1 iota_compare_fusion
  213.2 0.1 lt.35
  213.3 17.6 %all-to-all-done.1 = bf16[64,8,1024]{2,1,0:T(8,128)(2,1)S(1)} async-done(((bf16[64,8,1024]{2,1,0:T(8,128)(2,1)}), bf16[64,8,1024]{2,1,0:T(8,128)(2,1)S(1)}, u32[]{:S(2)}, u32[]{:S(2)}) %all-to-all-start.1) | async-done | bytes 1048608 | tf_op jit(solution)/shard_map/all_to_all | solution.py:367
  230.9 1.2 copy-done.2
  232.1 2.0 shard_map.134
  234.1 10.4 %all_to_all.15.got_ref = bf16[8,32,640]{2,1,0:T(8,128)(2,1)S(1)} all-to-all(bf16[8,32,640]{2,1,0:T(8,128)(2,1)S(1)} %bitcast.15), channel_id=1, replica_groups=mesh['dp'=4,'block'=16,'parity'=2,'row'=4,'core'=2] {'row','core'}, dimensions={0} | all-to-all | bytes 655360 | tf_op jit(solution)/shard_map/all_to_all | solution.py:374
  244.6 1.5 shard_map.135
  (33 shorter events, 0.1 us)
Async XLA Ops:
  1.3 26.3 %copy-start.13 = (bf16[32,512]{1,0:T(8,128)(2,1)S(1)}, bf16[32,512]{1,0:T(8,128)(2,1)}, u32[]{:S(2)}) copy-start(bf16[32,512]{1,0:T(8,128)(2,1)} %param.22) | copy-start | bytes 98308
  1.3 43.1 %copy-start.14 = (s32[1,32,16]{1,2,0:T(8,128)S(1)}, s32[1,32,16]{1,2,0:T(8,128)}, u32[]{:S(2)}) copy-start(s32[1,32,16]{1,2,0:T(8,128)} %param.13) | copy-start | bytes 6148
  1.3 43.3 %copy-start = (bf16[128,1024]{1,0:T(8,128)(2,1)S(1)}, bf16[128,1024]{1,0:T(8,128)(2,1)}, u32[]{:S(2)}) copy-start(bf16[128,1024]{1,0:T(8,128)(2,1)} %tokens_ref.3) | copy-start | bytes 786436
  1.3 43.3 %copy-start.11 = (f32[1024]{0:T(1024)S(1)}, f32[1024]{0:T(1024)}, u32[]{:S(2)}) copy-start(f32[1024]{0:T(1024)} %param.16) | copy-start | bytes 12292
  4.1 40.4 %collective-permute-start = (bf16[64,1408]{1,0:T(8,128)(2,1)}, bf16[64,1408]{1,0:T(8,128)(2,1)S(1)}, u32[]{:S(2)}, u32[]{:S(2)}) collective-permute-start(bf16[64,1408]{1,0:T(8,128)(2,1)} %shard_map.131), channel_id=1, source_target_pairs={{0,0},{257,1},{514,16},{771,17},{4,32},{261,33},{518,48},{775,49},... | collective-permute-start | bytes 540680 | tf_op jit(solution)/shard_map/ppermute | solution.py:353
  46.2 136.0 %all-to-all-start = ((bf16[64,8,1024]{2,1,0:T(8,128)(2,1)}), bf16[64,8,1024]{2,1,0:T(8,128)(2,1)S(1)}, u32[]{:S(2)}, u32[]{:S(2)}) async-start(bf16[64,8,1024]{2,1,0:T(8,128)(2,1)} %bitcast.5), calls=%async_computation | async-start | bytes 2097152 | tf_op jit(solution)/shard_map/all_to_all | solution.py:363
  55.4 3.4 %collective-permute-start.1 = (bf16[64,1408]{1,0:T(8,128)(2,1)S(1)}, bf16[64,1408]{1,0:T(8,128)(2,1)S(1)}, u32[]{:S(2)}, u32[]{:S(2)}) collective-permute-start(bf16[64,1408]{1,0:T(8,128)(2,1)S(1)} %collective-permute-done), channel_id=1, source_target_pairs={{0,1},{1,0},{2,3},{3,2},{4,5},{5,4},{6,7},{7,6},{8,9},{9,8},{10,11... | collective-permute-start | bytes 540680 | tf_op jit(solution)/shard_map/ppermute | solution.py:182
  58.9 21.2 %collective-permute-start.2 = (bf16[128,1408]{1,0:T(8,128)(2,1)S(1)}, bf16[128,1408]{1,0:T(8,128)(2,1)S(1)}, u32[]{:S(2)}, u32[]{:S(2)}) collective-permute-start(bf16[128,1408]{1,0:T(8,128)(2,1)S(1)} %maximum_select_fusion.own_ref), channel_id=1, source_target_pairs={{0,16},{1,241},{16,32},{17,1},{32,48},{33,17},{48,64},{49,33},{64,... | collective-permute-start | bytes 1081352 | tf_op jit(solution)/shard_map/ppermute | solution.py:194
  80.1 14.4 %collective-permute-start.3 = (bf16[128,1408]{1,0:T(8,128)(2,1)S(1)}, bf16[128,1408]{1,0:T(8,128)(2,1)S(1)}, u32[]{:S(2)}, u32[]{:S(2)}) collective-permute-start(bf16[128,1408]{1,0:T(8,128)(2,1)S(1)} %collective-permute-done.2.refs_0_), channel_id=1, source_target_pairs={{0,16},{1,241},{16,32},{17,1},{32,48},{33,17},{48,64},{49,33},{64,... | collective-permute-start | bytes 1081352 | tf_op jit(solution)/shard_map/ppermute | solution.py:194
  94.5 14.0 %collective-permute-start.4 = (bf16[128,1408]{1,0:T(8,128)(2,1)S(1)}, bf16[128,1408]{1,0:T(8,128)(2,1)S(1)}, u32[]{:S(2)}, u32[]{:S(2)}) collective-permute-start(bf16[128,1408]{1,0:T(8,128)(2,1)S(1)} %collective-permute-done.3.refs_1_), channel_id=1, source_target_pairs={{0,16},{1,241},{16,32},{17,1},{32,48},{33,17},{48,64},{49,33},{64,... | collective-permute-start | bytes 1081352 | tf_op jit(solution)/shard_map/ppermute | solution.py:194
  108.5 14.0 %collective-permute-start.5 = (bf16[128,1408]{1,0:T(8,128)(2,1)S(1)}, bf16[128,1408]{1,0:T(8,128)(2,1)S(1)}, u32[]{:S(2)}, u32[]{:S(2)}) collective-permute-start(bf16[128,1408]{1,0:T(8,128)(2,1)S(1)} %collective-permute-done.4.refs_2_), channel_id=1, source_target_pairs={{0,16},{1,241},{16,32},{17,1},{32,48},{33,17},{48,64},{49,33},{64,... | collective-permute-start | bytes 1081352 | tf_op jit(solution)/shard_map/ppermute | solution.py:194
  122.5 44.2 %copy-start.5 = (bf16[128,1408]{1,0:T(8,128)(2,1)}, bf16[128,1408]{1,0:T(8,128)(2,1)S(1)}, u32[]{:S(2)}) copy-start(bf16[128,1408]{1,0:T(8,128)(2,1)S(1)} %collective-permute-done.5.refs_3_) | copy-start | bytes 1081348
  122.5 14.0 %collective-permute-start.6 = (bf16[128,1408]{1,0:T(8,128)(2,1)S(1)}, bf16[128,1408]{1,0:T(8,128)(2,1)S(1)}, u32[]{:S(2)}, u32[]{:S(2)}) collective-permute-start(bf16[128,1408]{1,0:T(8,128)(2,1)S(1)} %collective-permute-done.5.refs_3_), channel_id=1, source_target_pairs={{0,16},{1,241},{16,32},{17,1},{32,48},{33,17},{48,64},{49,33},{64,... | collective-permute-start | bytes 1081352 | tf_op jit(solution)/shard_map/ppermute | solution.py:194
  136.6 30.1 %copy-start.7 = (bf16[128,1408]{1,0:T(8,128)(2,1)}, bf16[128,1408]{1,0:T(8,128)(2,1)S(1)}, u32[]{:S(2)}) copy-start(bf16[128,1408]{1,0:T(8,128)(2,1)S(1)} %collective-permute-done.6.refs_4_) | copy-start | bytes 1081348
  136.6 14.0 %collective-permute-start.7 = (bf16[128,1408]{1,0:T(8,128)(2,1)S(1)}, bf16[128,1408]{1,0:T(8,128)(2,1)S(1)}, u32[]{:S(2)}, u32[]{:S(2)}) collective-permute-start(bf16[128,1408]{1,0:T(8,128)(2,1)S(1)} %collective-permute-done.6.refs_4_), channel_id=1, source_target_pairs={{0,16},{1,241},{16,32},{17,1},{32,48},{33,17},{48,64},{49,33},{64,... | collective-permute-start | bytes 1081352 | tf_op jit(solution)/shard_map/ppermute | solution.py:194
  150.6 16.1 %copy-start.9 = (bf16[128,1408]{1,0:T(8,128)(2,1)}, bf16[128,1408]{1,0:T(8,128)(2,1)S(1)}, u32[]{:S(2)}) copy-start(bf16[128,1408]{1,0:T(8,128)(2,1)S(1)} %collective-permute-done.7.refs_5_) | copy-start | bytes 1081348
  150.6 14.0 %collective-permute-start.8 = (bf16[128,1408]{1,0:T(8,128)(2,1)S(1)}, bf16[128,1408]{1,0:T(8,128)(2,1)}, u32[]{:S(2)}, u32[]{:S(2)}) collective-permute-start(bf16[128,1408]{1,0:T(8,128)(2,1)S(1)} %collective-permute-done.7.refs_5_), channel_id=1, source_target_pairs={{0,16},{1,241},{16,32},{17,1},{32,48},{33,17},{48,64},{49,33},{64,... | collective-permute-start | bytes 1081352 | tf_op jit(solution)/shard_map/ppermute | solution.py:194
  157.7 17.0 %collective-permute-start.10 = (bf16[512,1408]{1,0:T(8,128)(2,1)}, bf16[512,1408]{1,0:T(8,128)(2,1)}, u32[]{:S(2)}, u32[]{:S(2)}) collective-permute-start(bf16[512,1408]{1,0:T(8,128)(2,1)} %pad_maximum_fusion), channel_id=1, source_target_pairs={{0,1},{1,0},{2,3},{3,2},{4,5},{5,4},{6,7},{7,6},{8,9},{9,8},{10,11... | collective-permute-start | bytes 4325384 | tf_op jit(solution)/shard_map/ppermute | solution.py:197
  166.7 15.4 %collective-permute-start.11 = (bf16[384,1408]{1,0:T(8,128)(2,1)}, bf16[384,1408]{1,0:T(8,128)(2,1)}, u32[]{:S(2)}, u32[]{:S(2)}) collective-permute-start(bf16[384,1408]{1,0:T(8,128)(2,1)} %pad_maximum_fusion.1), channel_id=1, source_target_pairs={{0,1},{1,0},{2,3},{3,2},{4,5},{5,4},{6,7},{7,6},{8,9},{9,8},{10,11... | collective-permute-start | bytes 3244040 | tf_op jit(solution)/shard_map/ppermute | solution.py:198
  169.1 13.0 %collective-permute-start.9 = (bf16[128,1408]{1,0:T(8,128)(2,1)}, bf16[128,1408]{1,0:T(8,128)(2,1)}, u32[]{:S(2)}, u32[]{:S(2)}) collective-permute-start(bf16[128,1408]{1,0:T(8,128)(2,1)} %collective-permute-done.8.refs_6_), channel_id=1, source_target_pairs={{0,16},{1,241},{16,32},{17,1},{32,48},{33,17},{48,64},{49,33},{64,... | collective-permute-start | bytes 1081352 | tf_op jit(solution)/shard_map/ppermute | solution.py:194
  182.1 1.0 copy-start.6
  183.1 1.0 copy-start.8
  184.1 1.0 copy-start.10
  185.1 27.8 %copy-start.15 = (f32[1,32,16]{1,2,0:T(8,128)S(1)}, f32[1,32,16]{1,2,0:T(8,128)}, u32[]{:S(2)}) copy-start(f32[1,32,16]{1,2,0:T(8,128)} %param.14) | copy-start | bytes 6148
  185.1 28.0 %copy-start.16 = (s32[1,32]{1,0:T(1,128)S(1)}, s32[1,32]{1,0:T(1,128)}, u32[]{:S(2)}) copy-start(s32[1,32]{1,0:T(1,128)} %param.15) | copy-start | bytes 388
  193.9 1.0 copy-start.4
  194.9 36.0 %copy-start.1 = (bf16[1024,512]{1,0:T(8,128)(2,1)S(1)}, bf16[1024,512]{1,0:T(8,128)(2,1)}, u32[]{:S(2)}) copy-start(bf16[1024,512]{1,0:T(8,128)(2,1)} %key_ref.1) | copy-start | bytes 3145732
  194.9 36.0 %copy-start.12 = (f32[1024]{0:T(1024)S(1)}, f32[1024]{0:T(1024)}, u32[]{:S(2)}) copy-start(f32[1024]{0:T(1024)} %param.17) | copy-start | bytes 12292
  194.9 36.0 %all-to-all-start.1 = ((bf16[64,8,1024]{2,1,0:T(8,128)(2,1)}), bf16[64,8,1024]{2,1,0:T(8,128)(2,1)S(1)}, u32[]{:S(2)}, u32[]{:S(2)}) async-start(bf16[64,8,1024]{2,1,0:T(8,128)(2,1)} %bitcast.14), calls=%async_computation.1 | async-start | bytes 2097152 | tf_op jit(solution)/shard_map/all_to_all | solution.py:367
  230.9 1.2 copy-start.2
  232.1 12.5 %copy-start.3 = (bf16[512,1024]{1,0:T(8,128)(2,1)S(1)}, bf16[512,1024]{1,0:T(8,128)(2,1)}, u32[]{:S(2)}) copy-start(bf16[512,1024]{1,0:T(8,128)(2,1)} %proj_ref.1) | copy-start | bytes 3145732

commit v4 on v3

--- a/solution.py
+++ b/solution.py
@@ -12,7 +12,7 @@
 EPSILON = 1e-06
 BLOCK = 2
 ALL = ("dp", "block", "parity", "row", "core")
-NEAR = ("dp", "parity", "row", "core")
+NEAR = ("dp", "parity", "row")
 SEQ = ("row", "core")
 STEP_J, STEP_E, INV_J = 9, 30, 25
 STATS = 5
@@ -90,28 +90,27 @@
 
 
 def expert_kernel(blocks, place, rows_ref, own_ref, *refs):
-    ring = refs[:-7]
-    early, late, out_ref, w_in, w_out, middle, sems = refs[-7:]
+    parts = refs[:-5]
+    out_ref, w_in, w_out, middle, sems = refs[-5:]
+    ring, twins = parts[: blocks // 2], parts[blocks // 2 :]
     block, turn = place[0], place[1]
     size = own_ref.shape[0] // 2
 
     def at(offset):
         return lax.rem(block + offset + blocks, blocks)
 
-    def halves(ref, start, index):
+    def halves(ref, index):
         return [
-            (ref.at[pl.ds(start + k * size, size)], buffer.at[index])
+            (ref.at[pl.ds(k * size, size)], buffer.at[index])
             for k, buffer in enumerate((w_in, w_out))
         ]
 
     jobs = [[], []]
-    found = [halves(own_ref, 0, block)]
+    found = [halves(own_ref, block)]
     for step, ref in enumerate(ring, 1):
-        found.append(halves(ref, 0, at(-step * turn)))
-    count = early.shape[0] // own_ref.shape[0]
-    for step in range(1, len(ring)):
-        ref, k = (early, step - 1) if step <= count else (late, step - 1 - count)
-        found.append(halves(ref, k * own_ref.shape[0], at(step * turn)))
+        found.append(halves(ref, at(-step * turn)))
+    for step, ref in enumerate(twins, 1):
+        found.append(halves(ref, at(step * turn)))
     for pair in found:
         for k in range(2):
             jobs[k].append(pair[k])
@@ -123,41 +122,32 @@
         for copy in part:
             copy.start()
     width, hidden = rows_ref.shape[1], w_in.shape[2]
-    tile = 256
+    step = 512
     for copy in copies[0]:
         copy.wait()
-
-    @pl.loop(0, rows_ref.shape[0] // tile)
-    def _(i):
-        here = pl.ds(pl.multiple_of(i * tile, tile), tile)
-        middle[here, :] = gelu(
-            jnp.dot(
-                rows_ref[here, :], w_in[...].reshape(width, hidden), preferred_element_type=F32
-            )
-        ).astype(BF16)
-
+    rows = rows_ref[...]
+    for start in range(0, hidden, step):
+        span = slice(start, min(start + step, hidden))
+        first = w_in[:, :, span].reshape(width, -1)
+        middle[:, span] = gelu(jnp.dot(rows, first, preferred_element_type=F32)).astype(BF16)
     for copy in copies[1]:
         copy.wait()
-
-    @pl.loop(0, rows_ref.shape[0] // tile)
-    def _(i):
-        here = pl.ds(pl.multiple_of(i * tile, tile), tile)
-        out_ref[here, :] = lax.dot_general(
-            middle[here, :],
-            w_out[...].reshape(width, hidden),
-            (((1,), (1,)), ((), ())),
-            preferred_element_type=F32,
+    mid = middle[...]
+    for start in range(0, width, step):
+        second = w_out[start // size : (start + step) // size].reshape(step, hidden)
+        out_ref[:, start : start + step] = lax.dot_general(
+            mid, second, (((1,), (1,)), ((), ())), preferred_element_type=F32
         ).astype(BF16)
 
 
-def expert(blocks, place, rows, own, ring, early, late):
+def expert(blocks, place, rows, own, ring, twins):
     total, width = rows.shape
     part, hidden = own.shape[0] // 2, own.shape[1]
     anywhere = pl.BlockSpec(memory_space=pl.ANY)
     return pl.pallas_call(
         functools.partial(expert_kernel, blocks),
         in_specs=[pl.BlockSpec(memory_space=pltpu.SMEM), _VM()]
-        + [anywhere] * (3 + len(ring)),
+        + [anywhere] * (1 + len(ring) + len(twins)),
         out_specs=_VM(),
         out_shape=jax.ShapeDtypeStruct((total, width), BF16),
         scratch_shapes=[
@@ -166,13 +156,13 @@
             pltpu.VMEM((total, hidden), BF16),
             pltpu.SemaphoreType.DMA((2, 2 * len(ring))),
         ],
-        compiler_params=pltpu.CompilerParams(vmem_limit_bytes=VMEM // 2),
+        compiler_params=pltpu.CompilerParams(vmem_limit_bytes=FULL),
         cost_estimate=pl.CostEstimate(
             flops=4 * total * width * hidden,
             bytes_accessed=4 * width * hidden + 4 * total * width,
             transcendentals=total * hidden,
         ),
-    )(place, rows, own, *ring, early, late)
+    )(place, rows, own, *ring, *twins)
 
 
 def spread(mine, sizes):
@@ -193,11 +183,9 @@
     for _ in range(steps):
         held = lax.ppermute(held, ("block", "core"), turns)
         ring.append(held)
-    cut = steps // 2
-    early = lax.ppermute(jnp.concatenate(ring[:cut]), "core", swap)
-    late = lax.ppermute(jnp.concatenate(ring[cut : steps - 1]), "core", swap)
+    twins = [lax.ppermute(held, "core", swap) for held in ring[:-1]]
     place = jnp.stack([lax.axis_index("block"), 1 - 2 * core]).astype(jnp.int32)
-    return blocks, place, own, ring, early, late
+    return blocks, place, own, ring, twins
 
 
 def pieces(v, count):
@@ -353,19 +341,18 @@
     shard = lax.ppermute(shard, ALL, scatter_pairs(sizes))
     query = lax.all_gather(queries, SEQ, tiled=True)
     shard, query, picks = lax.optimization_barrier((shard, query, picks))
-    blocks, place, own_part, ring, early, late = spread(shard, sizes)
+    blocks, place, own_part, ring, twins = spread(shard, sizes)
 
     pick_row = picks.reshape(1, experts * cap)
     live = lax.broadcasted_iota(jnp.int32, (experts, cap), 1) < counts[0][:, None]
     slot_weight = jnp.where(live, gates[0], 0.0).reshape(1, experts * cap)
     chosen = pick_rows(tokens, norm_in[None, :], pick_row)
-    near = experts * cores
     there = lax.all_to_all(
-        chosen.reshape(near, -1, width), NEAR, split_axis=0, concat_axis=0, tiled=True
-    )
-    result = expert(blocks, place, there.reshape(-1, width), own_part, ring, early, late)
+        chosen.reshape(experts, -1, width), NEAR, split_axis=0, concat_axis=0, tiled=True
+    )
+    result = expert(blocks, place, there.reshape(-1, width), own_part, ring, twins)
     back = lax.all_to_all(
-        result.reshape(near, -1, width), NEAR, split_axis=0, concat_axis=0, tiled=True
+        result.reshape(experts, -1, width), NEAR, split_axis=0, concat_axis=0, tiled=True
     ).reshape(-1, width)
     encoded, packet = tail(
         back, pick_row, slot_weight, tokens, norm_out[None, :], w_key, w_value, query

time: 247 us -> 234 us (0.947)
  waiting for transfers between devices: 79.9 us -> 46.9 us
  starting transfers between devices: 112 us -> 128 us
  blocking collectives: 27.2 us -> 36.7 us
  other arithmetic: 4.14 us -> 1.35 us
    ppermute x8, waiting for transfers between devices: 61.3 us -> 35 us  [spread(): held = lax.ppermute(held, ('block', 'core'), turns)]
    ppermute x2 -> x7, starting transfers between devices: 4.31 us -> 27.8 us  [spread(): twins = [lax.ppermute(held, 'core', swap) for held in ring[:-1]]]
    all_to_all x1, blocking collectives: 10.4 us -> 19.8 us  [local(): lax.all_to_all(packet.reshape(group, -1, packet.shape[1]), SEQ, split_axi...]
    all_to_all x2, starting transfers between devices: 27.3 us -> 17.9 us  [the longest x1 9.33 us: local(): lax.all_to_all(result.reshape(experts, -1, width), NEAR, split_axis=0, co...]
    all_to_all x2, waiting for transfers between devices: 17.6 us -> 10.8 us  [the longest x1 10.8 us: local(): lax.all_to_all(result.reshape(experts, -1, width), NEAR, split_axis=0, co...]
    concatenate x2 -> x0, other arithmetic: 3.26 us -> none  [the longest x1 2.05 us: spread(): late = lax.ppermute(jnp.concatenate(ring[cut:steps - 1]), 'core', swap)]
    unnamed x35 -> x41, local copies, waits for them, and re-layouts: 5.26 us -> 3.07 us
  transfers between devices with their start and end apart: 14 -> 19, of which waited for: 10 -> 8; matrix products, arithmetic and copies ran while one was open for 2% -> 0% of each run, Pallas kernels for 0% -> 0%
where the time goes in v4:
time: 234 us; the launch traced here: 233 us
  starting transfers between devices  128 us (55%)
  waiting for transfers between devices  46.9 us (20%)
  blocking collectives  36.7 us (16%)
  Pallas kernels  16.2 us (7%)
  local copies, waits for them, and re-layouts  3.39 us (1%)
    ppermute x8, starting transfers between devices, spread(): held = lax.ppermute(held, ('block', 'core'), turns)  56.1 us
    ppermute x8, waiting for transfers between devices, spread(): held = lax.ppermute(held, ('block', 'core'), turns)  35 us
    ppermute x7, starting transfers between devices, spread(): twins = [lax.ppermute(held, 'core', swap) for held in ring[:-1]]  27.8 us
    ppermute x1, starting transfers between devices, local(): shard = lax.ppermute(shard, ALL, scatter_pairs(sizes))  23.5 us
    all_to_all x1, blocking collectives, local(): lax.all_to_all(packet.reshape(group, -1, packet.shape[1]), SEQ, split_axi...  19.8 us
    all_gather x1, blocking collectives, local(): query = lax.all_gather(queries, SEQ, tiled=True)  16.8 us
    all_to_all x1, waiting for transfers between devices, local(): lax.all_to_all(result.reshape(experts, -1, width), NEAR, split_axis=0, co...  10.8 us
    all_to_all x1, starting transfers between devices, local(): lax.all_to_all(result.reshape(experts, -1, width), NEAR, split_axis=0, co...  9.33 us
  transfers between devices with their start and end apart: 19, of which 8 were waited for; matrix products, arithmetic and copies ran while one was open for 0% of the time, Pallas kernels for 0%

profile of v4, /device:TPU:1, one launch (start us, length us, event | category | flops | bytes accessed | tf_op | source)
XLA Modules:
  0.0 233.2 jit_solution(6580120196455859783)
XLA Ops:
  0.7 0.6 pad_add_fusion.1.which
  1.3 2.7 %shard_map.131 = bf16[64,1408]{1,0:T(8,128)(2,1)} custom-call(s32[2]{0:T(128)} %pad_add_fusion.1.which, bf16[1,1024,1408]{2,1,0:T(8,128)(2,1)} %w_in_ref.1, bf16[1,1408,1024]{2,1,0:T(8,128)(2,1)} %w_out_ref.1), custom_call_target="tpu_custom_call" | custom-call | tf_op jit(solution)/shard_map/pallas_call | solution.py:50
  4.0 23.5 %collective-permute-start = (bf16[64,1408]{1,0:T(8,128)(2,1)}, bf16[64,1408]{1,0:T(8,128)(2,1)S(1)}, u32[]{:S(2)}, u32[]{:S(2)}) collective-permute-start(bf16[64,1408]{1,0:T(8,128)(2,1)} %shard_map.131), channel_id=1, source_target_pairs={{0,0},{257,1},{514,16},{771,17},{4,32},{261,33},{518,48},{775,49},... | collective-permute-start | bytes 540680 | tf_op jit(solution)/shard_map/ppermute | solution.py:341
  27.6 16.8 %all_gather.3.query_ref = bf16[256,512]{1,0:T(8,128)(2,1)S(1)} all-gather(bf16[32,512]{1,0:T(8,128)(2,1)S(1)} %copy-done.8), channel_id=1, replica_groups=mesh['dp'=4,'block'=16,'parity'=2,'row'=4,'core'=2] {'row','core'}, dimensions={0}, use_global_device_ids=true | all-gather | bytes 294912 | tf_op jit(solution)/shard_map/all_gather | solution.py:342
  44.4 0.1 copy.16
  44.5 0.1 reshape.56.picks_ref
  44.6 1.5 shard_map.132
  46.1 8.6 %all-to-all-start = ((bf16[32,16,1024]{2,1,0:T(8,128)(2,1)}), bf16[32,16,1024]{2,1,0:T(8,128)(2,1)S(1)}, u32[]{:S(2)}, u32[]{:S(2)}) async-start(bf16[32,16,1024]{2,1,0:T(8,128)(2,1)} %bitcast.5), calls=%async_computation | async-start | bytes 2097152 | tf_op jit(solution)/shard_map/all_to_all | solution.py:350
  54.7 2.4 %collective-permute-start.1 = (bf16[64,1408]{1,0:T(8,128)(2,1)S(1)}, bf16[64,1408]{1,0:T(8,128)(2,1)S(1)}, u32[]{:S(2)}, u32[]{:S(2)}) collective-permute-start(bf16[64,1408]{1,0:T(8,128)(2,1)S(1)} %collective-permute-done), channel_id=1, source_target_pairs={{0,1},{1,0},{2,3},{3,2},{4,5},{5,4},{6,7},{7,6},{8,9},{9,8},{10,11... | collective-permute-start | bytes 540680 | tf_op jit(solution)/shard_map/ppermute | solution.py:172
  57.1 1.0 collective-permute-done.1
  58.1 0.1 maximum_select_fusion.own_ref
  58.2 12.9 %collective-permute-start.2 = (bf16[128,1408]{1,0:T(8,128)(2,1)S(1)}, bf16[128,1408]{1,0:T(8,128)(2,1)S(1)}, u32[]{:S(2)}, u32[]{:S(2)}) collective-permute-start(bf16[128,1408]{1,0:T(8,128)(2,1)S(1)} %maximum_select_fusion.own_ref), channel_id=1, source_target_pairs={{0,16},{1,241},{16,32},{17,1},{32,48},{33,17},{48,64},{49,33},{64,... | collective-permute-start | bytes 1081352 | tf_op jit(solution)/shard_map/ppermute | solution.py:184
  71.2 8.2 %collective-permute-done.2.refs_0_ = bf16[128,1408]{1,0:T(8,128)(2,1)S(1)} collective-permute-done((bf16[128,1408]{1,0:T(8,128)(2,1)S(1)}, bf16[128,1408]{1,0:T(8,128)(2,1)S(1)}, u32[]{:S(2)}, u32[]{:S(2)}) %collective-permute-start.2) | collective-permute-done | bytes 360480 | tf_op jit(solution)/shard_map/ppermute | solution.py:184
  79.4 5.9 %collective-permute-start.3 = (bf16[128,1408]{1,0:T(8,128)(2,1)S(1)}, bf16[128,1408]{1,0:T(8,128)(2,1)S(1)}, u32[]{:S(2)}, u32[]{:S(2)}) collective-permute-start(bf16[128,1408]{1,0:T(8,128)(2,1)S(1)} %collective-permute-done.2.refs_0_), channel_id=1, source_target_pairs={{0,16},{1,241},{16,32},{17,1},{32,48},{33,17},{48,64},{49,33},{64,... | collective-permute-start | bytes 1081352 | tf_op jit(solution)/shard_map/ppermute | solution.py:184
  85.3 7.3 %collective-permute-done.3.refs_1_ = bf16[128,1408]{1,0:T(8,128)(2,1)S(1)} collective-permute-done((bf16[128,1408]{1,0:T(8,128)(2,1)S(1)}, bf16[128,1408]{1,0:T(8,128)(2,1)S(1)}, u32[]{:S(2)}, u32[]{:S(2)}) %collective-permute-start.3) | collective-permute-done | bytes 360480 | tf_op jit(solution)/shard_map/ppermute | solution.py:184
  92.6 5.1 %collective-permute-start.4 = (bf16[128,1408]{1,0:T(8,128)(2,1)S(1)}, bf16[128,1408]{1,0:T(8,128)(2,1)S(1)}, u32[]{:S(2)}, u32[]{:S(2)}) collective-permute-start(bf16[128,1408]{1,0:T(8,128)(2,1)S(1)} %collective-permute-done.3.refs_1_), channel_id=1, source_target_pairs={{0,16},{1,241},{16,32},{17,1},{32,48},{33,17},{48,64},{49,33},{64,... | collective-permute-start | bytes 1081352 | tf_op jit(solution)/shard_map/ppermute | solution.py:184
  97.7 5.0 %collective-permute-done.4.refs_2_ = bf16[128,1408]{1,0:T(8,128)(2,1)S(1)} collective-permute-done((bf16[128,1408]{1,0:T(8,128)(2,1)S(1)}, bf16[128,1408]{1,0:T(8,128)(2,1)S(1)}, u32[]{:S(2)}, u32[]{:S(2)}) %collective-permute-start.4) | collective-permute-done | bytes 360480 | tf_op jit(solution)/shard_map/ppermute | solution.py:184
  102.8 5.6 %collective-permute-start.5 = (bf16[128,1408]{1,0:T(8,128)(2,1)S(1)}, bf16[128,1408]{1,0:T(8,128)(2,1)S(1)}, u32[]{:S(2)}, u32[]{:S(2)}) collective-permute-start(bf16[128,1408]{1,0:T(8,128)(2,1)S(1)} %collective-permute-done.4.refs_2_), channel_id=1, source_target_pairs={{0,16},{1,241},{16,32},{17,1},{32,48},{33,17},{48,64},{49,33},{64,... | collective-permute-start | bytes 1081352 | tf_op jit(solution)/shard_map/ppermute | solution.py:184
  108.4 6.8 %collective-permute-done.5.refs_3_ = bf16[128,1408]{1,0:T(8,128)(2,1)S(1)} collective-permute-done((bf16[128,1408]{1,0:T(8,128)(2,1)S(1)}, bf16[128,1408]{1,0:T(8,128)(2,1)S(1)}, u32[]{:S(2)}, u32[]{:S(2)}) %collective-permute-start.5) | collective-permute-done | bytes 360480 | tf_op jit(solution)/shard_map/ppermute | solution.py:184
  115.2 4.4 %collective-permute-start.6 = (bf16[128,1408]{1,0:T(8,128)(2,1)S(1)}, bf16[128,1408]{1,0:T(8,128)(2,1)S(1)}, u32[]{:S(2)}, u32[]{:S(2)}) collective-permute-start(bf16[128,1408]{1,0:T(8,128)(2,1)S(1)} %collective-permute-done.5.refs_3_), channel_id=1, source_target_pairs={{0,16},{1,241},{16,32},{17,1},{32,48},{33,17},{48,64},{49,33},{64,... | collective-permute-start | bytes 1081352 | tf_op jit(solution)/shard_map/ppermute | solution.py:184
  119.7 4.7 %collective-permute-done.6.refs_4_ = bf16[128,1408]{1,0:T(8,128)(2,1)S(1)} collective-permute-done((bf16[128,1408]{1,0:T(8,128)(2,1)S(1)}, bf16[128,1408]{1,0:T(8,128)(2,1)S(1)}, u32[]{:S(2)}, u32[]{:S(2)}) %collective-permute-start.6) | collective-permute-done | bytes 360480 | tf_op jit(solution)/shard_map/ppermute | solution.py:184
  124.4 9.4 %collective-permute-start.7 = (bf16[128,1408]{1,0:T(8,128)(2,1)S(1)}, bf16[128,1408]{1,0:T(8,128)(2,1)}, u32[]{:S(2)}, u32[]{:S(2)}) collective-permute-start(bf16[128,1408]{1,0:T(8,128)(2,1)S(1)} %collective-permute-done.6.refs_4_), channel_id=1, source_target_pairs={{0,16},{1,241},{16,32},{17,1},{32,48},{33,17},{48,64},{49,33},{64,... | collective-permute-start | bytes 1081352 | tf_op jit(solution)/shard_map/ppermute | solution.py:184
  133.8 9.8 %collective-permute-start.10 = (bf16[128,1408]{1,0:T(8,128)(2,1)S(1)}, bf16[128,1408]{1,0:T(8,128)(2,1)S(1)}, u32[]{:S(2)}, u32[]{:S(2)}) collective-permute-start(bf16[128,1408]{1,0:T(8,128)(2,1)S(1)} %collective-permute-done.2.refs_0_), channel_id=1, source_target_pairs={{0,1},{1,0},{2,3},{3,2},{4,5},{5,4},{6,7},{7,6},{8,9},{9,8},{10,11... | collective-permute-start | bytes 1081352 | tf_op jit(solution)/shard_map/ppermute | solution.py:186
  143.6 1.9 collective-permute-start.11
  145.5 0.0 collective-permute-done.7.refs_5_
  145.6 6.3 %collective-permute-start.8 = (bf16[128,1408]{1,0:T(8,128)(2,1)}, bf16[128,1408]{1,0:T(8,128)(2,1)}, u32[]{:S(2)}, u32[]{:S(2)}) collective-permute-start(bf16[128,1408]{1,0:T(8,128)(2,1)} %collective-permute-done.7.refs_5_), channel_id=1, source_target_pairs={{0,16},{1,241},{16,32},{17,1},{32,48},{33,17},{48,64},{49,33},{64,... | collective-permute-start | bytes 1081352 | tf_op jit(solution)/shard_map/ppermute | solution.py:184
  151.8 7.1 %collective-permute-start.12 = (bf16[128,1408]{1,0:T(8,128)(2,1)S(1)}, bf16[128,1408]{1,0:T(8,128)(2,1)S(1)}, u32[]{:S(2)}, u32[]{:S(2)}) collective-permute-start(bf16[128,1408]{1,0:T(8,128)(2,1)S(1)} %collective-permute-done.4.refs_2_), channel_id=1, source_target_pairs={{0,1},{1,0},{2,3},{3,2},{4,5},{5,4},{6,7},{7,6},{8,9},{9,8},{10,11... | collective-permute-start | bytes 1081352 | tf_op jit(solution)/shard_map/ppermute | solution.py:186
  158.9 1.9 collective-permute-start.13
  160.8 2.4 %collective-permute-start.14 = (bf16[128,1408]{1,0:T(8,128)(2,1)S(1)}, bf16[128,1408]{1,0:T(8,128)(2,1)}, u32[]{:S(2)}, u32[]{:S(2)}) collective-permute-start(bf16[128,1408]{1,0:T(8,128)(2,1)S(1)} %collective-permute-done.6.refs_4_), channel_id=1, source_target_pairs={{0,1},{1,0},{2,3},{3,2},{4,5},{5,4},{6,7},{7,6},{8,9},{9,8},{10,11... | collective-permute-start | bytes 1081352 | tf_op jit(solution)/shard_map/ppermute | solution.py:186
  163.3 1.9 collective-permute-start.15
  165.2 6.3 %collective-permute-start.9 = (bf16[128,1408]{1,0:T(8,128)(2,1)}, bf16[128,1408]{1,0:T(8,128)(2,1)}, u32[]{:S(2)}, u32[]{:S(2)}) collective-permute-start(bf16[128,1408]{1,0:T(8,128)(2,1)} %collective-permute-done.8.refs_6_), channel_id=1, source_target_pairs={{0,16},{1,241},{16,32},{17,1},{32,48},{33,17},{48,64},{49,33},{64,... | collective-permute-start | bytes 1081352 | tf_op jit(solution)/shard_map/ppermute | solution.py:184
  171.6 0.7 copy-done.19
  172.3 2.7 %collective-permute-start.16 = (bf16[128,1408]{1,0:T(8,128)(2,1)}, bf16[128,1408]{1,0:T(8,128)(2,1)}, u32[]{:S(2)}, u32[]{:S(2)}) collective-permute-start(bf16[128,1408]{1,0:T(8,128)(2,1)} %collective-permute-done.8.refs_6_), channel_id=1, source_target_pairs={{0,1},{1,0},{2,3},{3,2},{4,5},{5,4},{6,7},{7,6},{8,9},{9,8},{10,11... | collective-permute-start | bytes 1081352 | tf_op jit(solution)/shard_map/ppermute | solution.py:186
  175.1 0.6 pad_add_fusion.place
  175.7 3.0 %collective-permute-done.9.refs_7_ = bf16[128,1408]{1,0:T(8,128)(2,1)} collective-permute-done((bf16[128,1408]{1,0:T(8,128)(2,1)}, bf16[128,1408]{1,0:T(8,128)(2,1)}, u32[]{:S(2)}, u32[]{:S(2)}) %collective-permute-start.9) | collective-permute-done | bytes 360480 | tf_op jit(solution)/shard_map/ppermute | solution.py:184
  178.7 0.9 copy-done.6
  179.7 8.4 %shard_map.133 = bf16[512,1024]{1,0:T(8,128)(2,1)} custom-call(s32[2]{0:T(128)} %pad_add_fusion.place, bf16[512,1024]{1,0:T(8,128)(2,1)} %bitcast.16, bf16[128,1408]{1,0:T(8,128)(2,1)} %copy-done.7, bf16[128,1408]{1,0:T(8,128)(2,1)} %copy-done.12, bf16[128,1408]{1,0:T(8,128)(2,1)} %copy-done.13, bf16[128,1408]{1,0:T(8,128)(2,1)} %copy-done.14, ...), custom_call_target="tpu_custom_call" | custom-call | flops 2952790016 | bytes 7864320 | tf_op jit(solution)/shard_map/pallas_call | solution.py:147
  188.1 0.0 copy-start.1
  188.1 9.3 %all-to-all-start.1 = ((bf16[32,16,1024]{2,1,0:T(8,128)(2,1)}), bf16[32,16,1024]{2,1,0:T(8,128)(2,1)S(1)}, u32[]{:S(2)}, u32[]{:S(2)}) async-start(bf16[32,16,1024]{2,1,0:T(8,128)(2,1)} %bitcast.17), calls=%async_computation.1 | async-start | bytes 2097152 | tf_op jit(solution)/shard_map/all_to_all | solution.py:354
  197.5 0.1 iota_compare_fusion
  197.5 0.1 lt.35
  197.6 0.1 copy.17
  197.7 0.1 squeeze.3
  197.8 10.8 %all-to-all-done.1 = bf16[32,16,1024]{2,1,0:T(8,128)(2,1)S(1)} async-done(((bf16[32,16,1024]{2,1,0:T(8,128)(2,1)}), bf16[32,16,1024]{2,1,0:T(8,128)(2,1)S(1)}, u32[]{:S(2)}, u32[]{:S(2)}) %all-to-all-start.1) | async-done | bytes 1048608 | tf_op jit(solution)/shard_map/all_to_all | solution.py:354
  208.6 1.2 copy-done.2
  209.8 2.0 shard_map.134
  211.9 19.8 %all_to_all.15.got_ref = bf16[8,32,640]{2,1,0:T(8,128)(2,1)S(1)} all-to-all(bf16[8,32,640]{2,1,0:T(8,128)(2,1)S(1)} %bitcast.13), channel_id=1, replica_groups=mesh['dp'=4,'block'=16,'parity'=2,'row'=4,'core'=2] {'row','core'}, dimensions={0} | all-to-all | bytes 655360 | tf_op jit(solution)/shard_map/all_to_all | solution.py:361
  231.7 1.5 shard_map.135
  (47 shorter events, 0.1 us)
Async XLA Ops:
  1.3 26.3 %copy-start.8 = (bf16[32,512]{1,0:T(8,128)(2,1)S(1)}, bf16[32,512]{1,0:T(8,128)(2,1)}, u32[]{:S(2)}) copy-start(bf16[32,512]{1,0:T(8,128)(2,1)} %param.22) | copy-start | bytes 98308
  1.3 43.1 %copy-start.9 = (s32[1,32,16]{1,2,0:T(8,128)S(1)}, s32[1,32,16]{1,2,0:T(8,128)}, u32[]{:S(2)}) copy-start(s32[1,32,16]{1,2,0:T(8,128)} %param.13) | copy-start | bytes 6148
  1.3 43.3 %copy-start = (bf16[128,1024]{1,0:T(8,128)(2,1)S(1)}, bf16[128,1024]{1,0:T(8,128)(2,1)}, u32[]{:S(2)}) copy-start(bf16[128,1024]{1,0:T(8,128)(2,1)} %tokens_ref.3) | copy-start | bytes 786436
  1.3 43.3 %copy-start.4 = (f32[1024]{0:T(1024)S(1)}, f32[1024]{0:T(1024)}, u32[]{:S(2)}) copy-start(f32[1024]{0:T(1024)} %param.16) | copy-start | bytes 12292
  4.0 40.4 %collective-permute-start = (bf16[64,1408]{1,0:T(8,128)(2,1)}, bf16[64,1408]{1,0:T(8,128)(2,1)S(1)}, u32[]{:S(2)}, u32[]{:S(2)}) collective-permute-start(bf16[64,1408]{1,0:T(8,128)(2,1)} %shard_map.131), channel_id=1, source_target_pairs={{0,0},{257,1},{514,16},{771,17},{4,32},{261,33},{518,48},{775,49},... | collective-permute-start | bytes 540680 | tf_op jit(solution)/shard_map/ppermute | solution.py:341
  46.1 132.6 %all-to-all-start = ((bf16[32,16,1024]{2,1,0:T(8,128)(2,1)}), bf16[32,16,1024]{2,1,0:T(8,128)(2,1)S(1)}, u32[]{:S(2)}, u32[]{:S(2)}) async-start(bf16[32,16,1024]{2,1,0:T(8,128)(2,1)} %bitcast.5), calls=%async_computation | async-start | bytes 2097152 | tf_op jit(solution)/shard_map/all_to_all | solution.py:350
  54.7 3.4 %collective-permute-start.1 = (bf16[64,1408]{1,0:T(8,128)(2,1)S(1)}, bf16[64,1408]{1,0:T(8,128)(2,1)S(1)}, u32[]{:S(2)}, u32[]{:S(2)}) collective-permute-start(bf16[64,1408]{1,0:T(8,128)(2,1)S(1)} %collective-permute-done), channel_id=1, source_target_pairs={{0,1},{1,0},{2,3},{3,2},{4,5},{5,4},{6,7},{7,6},{8,9},{9,8},{10,11... | collective-permute-start | bytes 540680 | tf_op jit(solution)/shard_map/ppermute | solution.py:172
  58.2 120.5 %copy-start.7 = (bf16[128,1408]{1,0:T(8,128)(2,1)}, bf16[128,1408]{1,0:T(8,128)(2,1)S(1)}, u32[]{:S(2)}) copy-start(bf16[128,1408]{1,0:T(8,128)(2,1)S(1)} %maximum_select_fusion.own_ref) | copy-start | bytes 1081348
  58.2 21.2 %collective-permute-start.2 = (bf16[128,1408]{1,0:T(8,128)(2,1)S(1)}, bf16[128,1408]{1,0:T(8,128)(2,1)S(1)}, u32[]{:S(2)}, u32[]{:S(2)}) collective-permute-start(bf16[128,1408]{1,0:T(8,128)(2,1)S(1)} %maximum_select_fusion.own_ref), channel_id=1, source_target_pairs={{0,16},{1,241},{16,32},{17,1},{32,48},{33,17},{48,64},{49,33},{64,... | collective-permute-start | bytes 1081352 | tf_op jit(solution)/shard_map/ppermute | solution.py:184
  79.4 99.3 %copy-start.12 = (bf16[128,1408]{1,0:T(8,128)(2,1)}, bf16[128,1408]{1,0:T(8,128)(2,1)S(1)}, u32[]{:S(2)}) copy-start(bf16[128,1408]{1,0:T(8,128)(2,1)S(1)} %collective-permute-done.2.refs_0_) | copy-start | bytes 1081348
  79.4 13.2 %collective-permute-start.3 = (bf16[128,1408]{1,0:T(8,128)(2,1)S(1)}, bf16[128,1408]{1,0:T(8,128)(2,1)S(1)}, u32[]{:S(2)}, u32[]{:S(2)}) collective-permute-start(bf16[128,1408]{1,0:T(8,128)(2,1)S(1)} %collective-permute-done.2.refs_0_), channel_id=1, source_target_pairs={{0,16},{1,241},{16,32},{17,1},{32,48},{33,17},{48,64},{49,33},{64,... | collective-permute-start | bytes 1081352 | tf_op jit(solution)/shard_map/ppermute | solution.py:184
  92.6 86.1 %copy-start.13 = (bf16[128,1408]{1,0:T(8,128)(2,1)}, bf16[128,1408]{1,0:T(8,128)(2,1)S(1)}, u32[]{:S(2)}) copy-start(bf16[128,1408]{1,0:T(8,128)(2,1)S(1)} %collective-permute-done.3.refs_1_) | copy-start | bytes 1081348
  92.6 10.2 %collective-permute-start.4 = (bf16[128,1408]{1,0:T(8,128)(2,1)S(1)}, bf16[128,1408]{1,0:T(8,128)(2,1)S(1)}, u32[]{:S(2)}, u32[]{:S(2)}) collective-permute-start(bf16[128,1408]{1,0:T(8,128)(2,1)S(1)} %collective-permute-done.3.refs_1_), channel_id=1, source_target_pairs={{0,16},{1,241},{16,32},{17,1},{32,48},{33,17},{48,64},{49,33},{64,... | collective-permute-start | bytes 1081352 | tf_op jit(solution)/shard_map/ppermute | solution.py:184
  102.8 60.5 %copy-start.14 = (bf16[128,1408]{1,0:T(8,128)(2,1)}, bf16[128,1408]{1,0:T(8,128)(2,1)S(1)}, u32[]{:S(2)}) copy-start(bf16[128,1408]{1,0:T(8,128)(2,1)S(1)} %collective-permute-done.4.refs_2_) | copy-start | bytes 1081348
  102.8 12.4 %collective-permute-start.5 = (bf16[128,1408]{1,0:T(8,128)(2,1)S(1)}, bf16[128,1408]{1,0:T(8,128)(2,1)S(1)}, u32[]{:S(2)}, u32[]{:S(2)}) collective-permute-start(bf16[128,1408]{1,0:T(8,128)(2,1)S(1)} %collective-permute-done.4.refs_2_), channel_id=1, source_target_pairs={{0,16},{1,241},{16,32},{17,1},{32,48},{33,17},{48,64},{49,33},{64,... | collective-permute-start | bytes 1081352 | tf_op jit(solution)/shard_map/ppermute | solution.py:184
  115.2 63.5 %copy-start.15 = (bf16[128,1408]{1,0:T(8,128)(2,1)}, bf16[128,1408]{1,0:T(8,128)(2,1)S(1)}, u32[]{:S(2)}) copy-start(bf16[128,1408]{1,0:T(8,128)(2,1)S(1)} %collective-permute-done.5.refs_3_) | copy-start | bytes 1081348
  115.2 9.2 %collective-permute-start.6 = (bf16[128,1408]{1,0:T(8,128)(2,1)S(1)}, bf16[128,1408]{1,0:T(8,128)(2,1)S(1)}, u32[]{:S(2)}, u32[]{:S(2)}) collective-permute-start(bf16[128,1408]{1,0:T(8,128)(2,1)S(1)} %collective-permute-done.5.refs_3_), channel_id=1, source_target_pairs={{0,16},{1,241},{16,32},{17,1},{32,48},{33,17},{48,64},{49,33},{64,... | collective-permute-start | bytes 1081352 | tf_op jit(solution)/shard_map/ppermute | solution.py:184
  124.4 54.3 %copy-start.16 = (bf16[128,1408]{1,0:T(8,128)(2,1)}, bf16[128,1408]{1,0:T(8,128)(2,1)S(1)}, u32[]{:S(2)}) copy-start(bf16[128,1408]{1,0:T(8,128)(2,1)S(1)} %collective-permute-done.6.refs_4_) | copy-start | bytes 1081348
  124.4 21.2 %collective-permute-start.7 = (bf16[128,1408]{1,0:T(8,128)(2,1)S(1)}, bf16[128,1408]{1,0:T(8,128)(2,1)}, u32[]{:S(2)}, u32[]{:S(2)}) collective-permute-start(bf16[128,1408]{1,0:T(8,128)(2,1)S(1)} %collective-permute-done.6.refs_4_), channel_id=1, source_target_pairs={{0,16},{1,241},{16,32},{17,1},{32,48},{33,17},{48,64},{49,33},{64,... | collective-permute-start | bytes 1081352 | tf_op jit(solution)/shard_map/ppermute | solution.py:184
  133.8 27.0 %collective-permute-start.10 = (bf16[128,1408]{1,0:T(8,128)(2,1)S(1)}, bf16[128,1408]{1,0:T(8,128)(2,1)S(1)}, u32[]{:S(2)}, u32[]{:S(2)}) collective-permute-start(bf16[128,1408]{1,0:T(8,128)(2,1)S(1)} %collective-permute-done.2.refs_0_), channel_id=1, source_target_pairs={{0,1},{1,0},{2,3},{3,2},{4,5},{5,4},{6,7},{7,6},{8,9},{9,8},{10,11... | collective-permute-start | bytes 1081352 | tf_op jit(solution)/shard_map/ppermute | solution.py:186
  143.6 19.7 %collective-permute-start.11 = (bf16[128,1408]{1,0:T(8,128)(2,1)S(1)}, bf16[128,1408]{1,0:T(8,128)(2,1)S(1)}, u32[]{:S(2)}, u32[]{:S(2)}) collective-permute-start(bf16[128,1408]{1,0:T(8,128)(2,1)S(1)} %collective-permute-done.3.refs_1_), channel_id=1, source_target_pairs={{0,1},{1,0},{2,3},{3,2},{4,5},{5,4},{6,7},{7,6},{8,9},{9,8},{10,11... | collective-permute-start | bytes 1081352 | tf_op jit(solution)/shard_map/ppermute | solution.py:186
  145.6 19.7 %collective-permute-start.8 = (bf16[128,1408]{1,0:T(8,128)(2,1)}, bf16[128,1408]{1,0:T(8,128)(2,1)}, u32[]{:S(2)}, u32[]{:S(2)}) collective-permute-start(bf16[128,1408]{1,0:T(8,128)(2,1)} %collective-permute-done.7.refs_5_), channel_id=1, source_target_pairs={{0,16},{1,241},{16,32},{17,1},{32,48},{33,17},{48,64},{49,33},{64,... | collective-permute-start | bytes 1081352 | tf_op jit(solution)/shard_map/ppermute | solution.py:184
  151.8 19.7 %collective-permute-start.12 = (bf16[128,1408]{1,0:T(8,128)(2,1)S(1)}, bf16[128,1408]{1,0:T(8,128)(2,1)S(1)}, u32[]{:S(2)}, u32[]{:S(2)}) collective-permute-start(bf16[128,1408]{1,0:T(8,128)(2,1)S(1)} %collective-permute-done.4.refs_2_), channel_id=1, source_target_pairs={{0,1},{1,0},{2,3},{3,2},{4,5},{5,4},{6,7},{7,6},{8,9},{9,8},{10,11... | collective-permute-start | bytes 1081352 | tf_op jit(solution)/shard_map/ppermute | solution.py:186
  158.9 16.8 %collective-permute-start.13 = (bf16[128,1408]{1,0:T(8,128)(2,1)S(1)}, bf16[128,1408]{1,0:T(8,128)(2,1)}, u32[]{:S(2)}, u32[]{:S(2)}) collective-permute-start(bf16[128,1408]{1,0:T(8,128)(2,1)S(1)} %collective-permute-done.5.refs_3_), channel_id=1, source_target_pairs={{0,1},{1,0},{2,3},{3,2},{4,5},{5,4},{6,7},{7,6},{8,9},{9,8},{10,11... | collective-permute-start | bytes 1081352 | tf_op jit(solution)/shard_map/ppermute | solution.py:186
  160.8 10.7 %copy-start.17 = (bf16[128,1408]{1,0:T(8,128)(2,1)}, bf16[128,1408]{1,0:T(8,128)(2,1)S(1)}, u32[]{:S(2)}) copy-start(bf16[128,1408]{1,0:T(8,128)(2,1)S(1)} %collective-permute-done.10.refs_8_) | copy-start | bytes 1081348
  160.8 14.8 %collective-permute-start.14 = (bf16[128,1408]{1,0:T(8,128)(2,1)S(1)}, bf16[128,1408]{1,0:T(8,128)(2,1)}, u32[]{:S(2)}, u32[]{:S(2)}) collective-permute-start(bf16[128,1408]{1,0:T(8,128)(2,1)S(1)} %collective-permute-done.6.refs_4_), channel_id=1, source_target_pairs={{0,1},{1,0},{2,3},{3,2},{4,5},{5,4},{6,7},{7,6},{8,9},{9,8},{10,11... | collective-permute-start | bytes 1081352 | tf_op jit(solution)/shard_map/ppermute | solution.py:186
  163.3 8.3 %copy-start.18 = (bf16[128,1408]{1,0:T(8,128)(2,1)}, bf16[128,1408]{1,0:T(8,128)(2,1)S(1)}, u32[]{:S(2)}) copy-start(bf16[128,1408]{1,0:T(8,128)(2,1)S(1)} %collective-permute-done.11.refs_9_) | copy-start | bytes 1081348
  163.3 12.4 %collective-permute-start.15 = (bf16[128,1408]{1,0:T(8,128)(2,1)}, bf16[128,1408]{1,0:T(8,128)(2,1)}, u32[]{:S(2)}, u32[]{:S(2)}) collective-permute-start(bf16[128,1408]{1,0:T(8,128)(2,1)} %collective-permute-done.7.refs_5_), channel_id=1, source_target_pairs={{0,1},{1,0},{2,3},{3,2},{4,5},{5,4},{6,7},{7,6},{8,9},{9,8},{10,11... | collective-permute-start | bytes 1081352 | tf_op jit(solution)/shard_map/ppermute | solution.py:186
  165.2 13.4 %collective-permute-start.9 = (bf16[128,1408]{1,0:T(8,128)(2,1)}, bf16[128,1408]{1,0:T(8,128)(2,1)}, u32[]{:S(2)}, u32[]{:S(2)}) collective-permute-start(bf16[128,1408]{1,0:T(8,128)(2,1)} %collective-permute-done.8.refs_6_), channel_id=1, source_target_pairs={{0,16},{1,241},{16,32},{17,1},{32,48},{33,17},{48,64},{49,33},{64,... | collective-permute-start | bytes 1081352 | tf_op jit(solution)/shard_map/ppermute | solution.py:184
  171.6 0.8 copy-start.19
  172.3 6.3 %collective-permute-start.16 = (bf16[128,1408]{1,0:T(8,128)(2,1)}, bf16[128,1408]{1,0:T(8,128)(2,1)}, u32[]{:S(2)}, u32[]{:S(2)}) collective-permute-start(bf16[128,1408]{1,0:T(8,128)(2,1)} %collective-permute-done.8.refs_6_), channel_id=1, source_target_pairs={{0,1},{1,0},{2,3},{3,2},{4,5},{5,4},{6,7},{7,6},{8,9},{9,8},{10,11... | collective-permute-start | bytes 1081352 | tf_op jit(solution)/shard_map/ppermute | solution.py:186
  178.7 1.0 copy-start.6
  179.7 17.8 %copy-start.11 = (s32[1,32]{1,0:T(1,128)S(1)}, s32[1,32]{1,0:T(1,128)}, u32[]{:S(2)}) copy-start(s32[1,32]{1,0:T(1,128)} %param.15) | copy-start | bytes 388
  179.7 18.0 %copy-start.10 = (f32[1,32,16]{1,2,0:T(8,128)S(1)}, f32[1,32,16]{1,2,0:T(8,128)}, u32[]{:S(2)}) copy-start(f32[1,32,16]{1,2,0:T(8,128)} %param.14) | copy-start | bytes 6148
  179.7 28.9 %copy-start.5 = (f32[1024]{0:T(1024)S(1)}, f32[1024]{0:T(1024)}, u32[]{:S(2)}) copy-start(f32[1024]{0:T(1024)} %param.17) | copy-start | bytes 12292
  188.1 20.5 %copy-start.1 = (bf16[1024,512]{1,0:T(8,128)(2,1)S(1)}, bf16[1024,512]{1,0:T(8,128)(2,1)}, u32[]{:S(2)}) copy-start(bf16[1024,512]{1,0:T(8,128)(2,1)} %key_ref.1) | copy-start | bytes 3145732
  188.1 20.5 %all-to-all-start.1 = ((bf16[32,16,1024]{2,1,0:T(8,128)(2,1)}), bf16[32,16,1024]{2,1,0:T(8,128)(2,1)S(1)}, u32[]{:S(2)}, u32[]{:S(2)}) async-start(bf16[32,16,1024]{2,1,0:T(8,128)(2,1)} %bitcast.17), calls=%async_computation.1 | async-start | bytes 2097152 | tf_op jit(solution)/shard_map/all_to_all | solution.py:354
  208.6 1.2 copy-start.2
  209.8 21.9 %copy-start.3 = (bf16[512,1024]{1,0:T(8,128)(2,1)S(1)}, bf16[512,1024]{1,0:T(8,128)(2,1)}, u32[]{:S(2)}) copy-start(bf16[512,1024]{1,0:T(8,128)(2,1)} %proj_ref.1) | copy-start | bytes 3145732

commit v5 on v1

--- a/solution.py
+++ b/solution.py
@@ -12,11 +12,13 @@
 EPSILON = 1e-06
 BLOCK = 2
 ALL = ("dp", "block", "parity", "row", "core")
-NEAR = ("dp", "parity", "row", "core")
+NEAR = ("dp", "parity", "row")
 SEQ = ("row", "core")
 STEP_J, STEP_E, INV_J = 9, 30, 25
 STATS = 5
+STEP = 512
 VMEM = 60 * 1024 * 1024
+FULL = 61 * 1024 * 1024
 F32 = jnp.float32
 BF16 = jnp.bfloat16
 
@@ -58,7 +60,7 @@
             out_specs=pl.BlockSpec((rows, hidden), lambda i, s: (0, 0)),
         ),
         out_shape=jax.ShapeDtypeStruct((rows, hidden), BF16),
-        compiler_params=pltpu.CompilerParams(vmem_limit_bytes=VMEM // 4),
+        compiler_params=pltpu.CompilerParams(vmem_limit_bytes=FULL),
     )(which, w_in, w_out)
 
 
@@ -88,27 +90,33 @@
     return 0.5 * v * (1.0 + jnp.tanh(0.7978845608028654 * (v + 0.044715 * (v * v * v))))
 
 
-def expert_kernel(rows_ref, weights_ref, out_ref, w_in, w_out, sems):
-    first = pltpu.make_async_copy(weights_ref.at[:, 0], w_in, sems.at[0])
-    second = pltpu.make_async_copy(weights_ref.at[:, 1], w_out, sems.at[1])
-    first.start()
-    second.start()
-    first.wait()
-    width, hidden = rows_ref.shape[1], w_in.shape[2]
-    tile = 256
-    second.wait()
-
-    @pl.loop(0, rows_ref.shape[0] // tile)
-    def _(i):
-        here = pl.ds(pl.multiple_of(i * tile, tile), tile)
-        mid = gelu(
-            jnp.dot(
-                rows_ref[here, :], w_in[...].reshape(width, hidden), preferred_element_type=F32
-            )
-        ).astype(BF16)
-        out_ref[here, :] = lax.dot_general(
+def expert_kernel(rows_ref, weights_ref, out_ref, w_in, w_out, middle, sems):
+    blocks, _, part, hidden = weights_ref.shape
+    width = blocks * part
+    inner = [pl.ds(i, min(STEP, hidden - i)) for i in range(0, hidden, STEP)]
+    outer = [pl.ds(i, STEP // part) for i in range(0, blocks, STEP // part)]
+    copies = [
+        pltpu.make_async_copy(weights_ref.at[:, 0, :, span], w_in.at[:, :, span], sems.at[n])
+        for n, span in enumerate(inner)
+    ] + [
+        pltpu.make_async_copy(
+            weights_ref.at[span, 1], w_out.at[span], sems.at[len(inner) + n]
+        )
+        for n, span in enumerate(outer)
+    ]
+    for copy in copies:
+        copy.start()
+    rows = rows_ref[...]
+    for n, span in enumerate(inner):
+        copies[n].wait()
+        first = w_in[:, :, span].reshape(width, -1)
+        middle[:, span] = gelu(jnp.dot(rows, first, preferred_element_type=F32)).astype(BF16)
+    mid = middle[...]
+    for n, span in enumerate(outer):
+        copies[len(inner) + n].wait()
+        out_ref[:, n * STEP : (n + 1) * STEP] = lax.dot_general(
             mid,
-            w_out[...].reshape(width, hidden),
+            w_out[span].reshape(STEP, hidden),
             (((1,), (1,)), ((), ())),
             preferred_element_type=F32,
         ).astype(BF16)
@@ -119,13 +127,14 @@
     blocks, _, part, hidden = weights.shape
     return pl.pallas_call(
         expert_kernel,
-        in_specs=[_VM(), pl.BlockSpec(memory_space=pl.ANY)],
+        in_specs=[_VM(), pl.BlockSpec(memory_space=pltpu.HBM)],
         out_specs=_VM(),
         out_shape=jax.ShapeDtypeStruct((total, width), BF16),
         scratch_shapes=[
             pltpu.VMEM((blocks, part, hidden), BF16),
             pltpu.VMEM((blocks, part, hidden), BF16),
-            pltpu.SemaphoreType.DMA((2,)),
+            pltpu.VMEM((total, hidden), BF16),
+            pltpu.SemaphoreType.DMA((-(-hidden // STEP) + width // STEP,)),
         ],
         compiler_params=pltpu.CompilerParams(vmem_limit_bytes=VMEM // 2),
         cost_estimate=pl.CostEstimate(
@@ -147,8 +156,10 @@
 
 def tail_kernel(
     back_ref, picks_ref, weight_ref, tokens_ref, gain_ref, key_ref, value_ref, query_ref,
-    encoded_ref, packet_ref,
+    encoded_ref, packet_ref, value_held, value_sem,
 ):
+    value_copy = pltpu.make_async_copy(value_ref, value_held, value_sem)
+    value_copy.start()
     rows = tokens_ref.shape[0]
     slots = picks_ref.shape[1]
     here = lax.broadcasted_iota(jnp.int32, (rows, slots), 0) == picks_ref[...]
@@ -161,7 +172,8 @@
     encoded = rms_norm(mixed, gain_ref[...]).astype(BF16)
     encoded_ref[...] = encoded
     keys = jnp.dot(encoded, key_ref[...], preferred_element_type=F32).astype(BF16)
-    values = jnp.dot(encoded, value_ref[...], preferred_element_type=F32).astype(BF16)
+    value_copy.wait()
+    values = jnp.dot(encoded, value_held[...], preferred_element_type=F32).astype(BF16)
     query = query_ref[...]
     count, features = query.shape
     size = features // HEADS
@@ -202,8 +214,9 @@
     count, features = query.shape
     return pl.pallas_call(
         tail_kernel,
-        in_specs=[_VM()] * 8,
+        in_specs=[_VM()] * 6 + [pl.BlockSpec(memory_space=pltpu.HBM), _VM()],
         out_specs=(_VM(), _VM()),
+        scratch_shapes=[pltpu.VMEM(w_value.shape, BF16), pltpu.SemaphoreType.DMA(())],
         out_shape=(
             jax.ShapeDtypeStruct((rows, width), BF16),
             jax.ShapeDtypeStruct((count, features + 128), BF16),
@@ -287,6 +300,8 @@
     j = (INV_J * (column + (plane - STEP_E) * own)) % plane
     shard = take_shard(jnp.stack([j // cores, j % cores]).astype(jnp.int32), w_in, w_out, blocks)
     shard = lax.ppermute(shard, ALL, scatter_pairs(sizes))
+    query = lax.all_gather(queries, SEQ, tiled=True)
+    shard, query = lax.optimization_barrier((shard, query))
     weights = lax.all_gather(shard, ("block", "core"))
     weights = weights.reshape(blocks, cores, *shard.shape)
 
@@ -294,15 +309,12 @@
     live = lax.broadcasted_iota(jnp.int32, (experts, cap), 1) < counts[0][:, None]
     slot_weight = jnp.where(live, gates[0], 0.0).reshape(1, experts * cap)
     chosen = pick_rows(tokens, norm_in[None, :], pick_row)
-    near = experts * cores
     there = lax.all_to_all(
-        chosen.reshape(near, -1, width), NEAR, split_axis=0, concat_axis=0, tiled=True
-    )
-    query = lax.all_gather(queries, SEQ, tiled=True)
-
+        chosen.reshape(experts, -1, width), NEAR, split_axis=0, concat_axis=0, tiled=True
+    )
     result = expert(there.reshape(-1, width), weights)
     back = lax.all_to_all(
-        result.reshape(near, -1, width), NEAR, split_axis=0, concat_axis=0, tiled=True
+        result.reshape(experts, -1, width), NEAR, split_axis=0, concat_axis=0, tiled=True
     ).reshape(-1, width)
     encoded, packet = tail(
         back, pick_row, slot_weight, tokens, norm_out[None, :], w_key, w_value, query

time: 235 us -> 232 us (0.987)
  blocking collectives: 68.4 us -> 53.9 us
  waiting for transfers between devices: 99 us -> 112 us
  local copies, waits for them, and re-layouts: 8.59 us -> 5.94 us
  Pallas kernels: 9.89 us -> 12.4 us
    all_to_all x1, waiting for transfers between devices: 0.01 us -> 15.2 us  [local(): lax.all_to_all(result.reshape(experts, -1, width), NEAR, split_axis=0, co...]
    all_to_all x1, blocking collectives: 38.9 us -> 24.1 us  [local(): lax.all_to_all(chosen.reshape(experts, -1, width), NEAR, split_axis=0, co...]
    ppermute x1, waiting for transfers between devices: 4.35 us -> 0.01 us  [local(): shard = lax.ppermute(shard, ALL, scatter_pairs(sizes))]
    all_to_all x1, blocking collectives: 10.2 us -> 13 us  [local(): lax.all_to_all(packet.reshape(group, -1, packet.shape[1]), SEQ, split_axi...]
    unnamed x30 -> x28, local copies, waits for them, and re-layouts: 8.34 us -> 5.69 us
    all_gather x1, waiting for transfers between devices: 94.6 us -> 97.1 us  [local(): weights = lax.all_gather(shard, ('block', 'core'))]
    all_gather x1, blocking collectives: 19.3 us -> 16.8 us  [local(): query = lax.all_gather(queries, SEQ, tiled=True)]
where the time goes in v5:
time: 232 us; the launch traced here: 231 us
  waiting for transfers between devices  112 us (48%)
  blocking collectives  53.9 us (23%)
  starting transfers between devices  31.9 us (14%)
  between operations  14.2 us (6%)
  Pallas kernels  12.4 us (5%)
  local copies, waits for them, and re-layouts  5.94 us (3%)
    all_gather x1, waiting for transfers between devices, local(): weights = lax.all_gather(shard, ('block', 'core'))  97.1 us
    all_to_all x1, blocking collectives, local(): lax.all_to_all(chosen.reshape(experts, -1, width), NEAR, split_axis=0, co...  24.1 us
    ppermute x1, starting transfers between devices, local(): shard = lax.ppermute(shard, ALL, scatter_pairs(sizes))  23.5 us
    all_gather x1, blocking collectives, local(): query = lax.all_gather(queries, SEQ, tiled=True)  16.8 us
    all_to_all x1, waiting for transfers between devices, local(): lax.all_to_all(result.reshape(experts, -1, width), NEAR, split_axis=0, co...  15.2 us
    all_to_all x1, blocking collectives, local(): lax.all_to_all(packet.reshape(group, -1, packet.shape[1]), SEQ, split_axi...  13 us
    all_to_all x1, starting transfers between devices, local(): lax.all_to_all(result.reshape(experts, -1, width), NEAR, split_axis=0, co...  8.31 us
    unnamed x28, local copies, waits for them, and re-layouts  5.69 us
  transfers between devices with their start and end apart: 3, of which 2 were waited for; matrix products, arithmetic and copies ran while one was open for 0% of the time, Pallas kernels for 0%

profile of v5, /device:TPU:1, one launch (start us, length us, event | category | flops | bytes accessed | tf_op | source)
XLA Modules:
  0.0 231.4 jit_solution(2474811613901949929)
XLA Ops:
  7.2 0.0 all-gather.3.cloned.1.call-start
  7.3 0.7 pad_add_fusion.which
  7.9 0.0 copy-start.9
  7.9 0.0 copy-start.10
  7.9 0.0 copy-start
  7.9 0.0 copy-start.5
  7.9 2.7 %shard_map.132 = bf16[64,1408]{1,0:T(8,128)(2,1)} custom-call(s32[2]{0:T(128)} %pad_add_fusion.which, bf16[1,1024,1408]{2,1,0:T(8,128)(2,1)} %w_in_ref.1, bf16[1,1408,1024]{2,1,0:T(8,128)(2,1)} %w_out_ref.1), custom_call_target="tpu_custom_call" | custom-call | tf_op jit(solution)/shard_map/pallas_call | solution.py:51
  10.7 23.5 %collective-permute-start = (bf16[64,1408]{1,0:T(8,128)(2,1)}, bf16[64,1408]{1,0:T(8,128)(2,1)S(1)}, u32[]{:S(2)}, u32[]{:S(2)}) collective-permute-start(bf16[64,1408]{1,0:T(8,128)(2,1)} %shard_map.132), channel_id=1, source_target_pairs={{0,0},{257,1},{514,16},{771,17},{4,32},{261,33},{518,48},{775,49},... | collective-permute-start | bytes 540680 | tf_op jit(solution)/shard_map/ppermute | solution.py:302
  34.2 0.0 copy-done.9
  34.2 16.8 %all_gather.9.query_ref = bf16[256,512]{1,0:T(8,128)(2,1)S(1)} all-gather(bf16[32,512]{1,0:T(8,128)(2,1)S(1)} %copy-done.9), channel_id=1, replica_groups=mesh['dp'=4,'block'=16,'parity'=2,'row'=4,'core'=2] {'row','core'}, dimensions={0}, use_global_device_ids=true | all-gather | bytes 294912 | tf_op jit(solution)/shard_map/all_gather | solution.py:303
  51.0 0.0 collective-permute-done
  51.0 0.0 copy-start.8
  51.0 0.7 copy-done.8
  51.7 0.0 all-gather.3.cloned.1.call-update
  51.7 0.0 copy-done.10
  51.7 0.1 copy.16
  51.8 0.1 reshape.59.picks_ref
  51.9 0.0 copy-done
  51.9 0.0 copy-done.5
  51.9 0.5 shard_map.131
  52.5 24.1 %all_to_all.15 = bf16[32,16,1024]{2,1,0:T(8,128)(2,1)S(1)} all-to-all(bf16[32,16,1024]{2,1,0:T(8,128)(2,1)S(1)} %bitcast.12), channel_id=1, replica_groups=mesh['dp'=4,'block'=16,'parity'=2,'row'=4,'core'=2] {'dp','parity','row'}, dimensions={0} | all-to-all | bytes 2097152 | tf_op jit(solution)/shard_map/all_to_all | solution.py:312
  76.6 97.1 %all-gather.3.cloned.1.call-done = bf16[2048,1408]{1,0:T(8,128)(2,1)} async-done(((bf16[64,1408]{1,0:T(8,128)(2,1)}), bf16[2048,1408]{1,0:T(8,128)(2,1)}) %all-gather.3.cloned.1.call-update) | async-done | bytes 5767184 | tf_op jit(solution)/shard_map/all_gather | solution.py:305
  173.7 0.0 copy-start.7
  173.7 2.6 %copy-done.7 = bf16[2048,1408]{1,0:T(8,128)(2,1)S(1)} copy-done((bf16[2048,1408]{1,0:T(8,128)(2,1)S(1)}, bf16[2048,1408]{1,0:T(8,128)(2,1)}, u32[]{:S(2)}) %copy-start.7) | copy-done | bytes 5767192
  176.3 0.0 copy-start.12
  176.3 0.0 copy-start.11
  176.3 0.0 copy-start.6
  176.3 5.3 %shard_map.133 = bf16[512,1024]{1,0:T(8,128)(2,1)S(1)} custom-call(bf16[512,1024]{1,0:T(8,128)(2,1)S(1)} %bitcast.14, bf16[16,2,64,1408]{3,2,1,0:T(8,128)(2,1)S(1)} %bitcast.18), custom_call_target="tpu_custom_call" | custom-call | flops 2952790016 | bytes 7864320 | tf_op jit(solution)/shard_map/pallas_call | solution.py:128
  181.7 0.0 copy-start.4
  181.7 1.0 copy-done.4
  182.7 0.0 copy-start.1
  182.7 8.3 %all-to-all-start.1 = ((bf16[32,16,1024]{2,1,0:T(8,128)(2,1)}), bf16[32,16,1024]{2,1,0:T(8,128)(2,1)S(1)}, u32[]{:S(2)}, u32[]{:S(2)}) async-start(bf16[32,16,1024]{2,1,0:T(8,128)(2,1)} %bitcast.13), calls=%async_computation.1 | async-start | bytes 2097152 | tf_op jit(solution)/shard_map/all_to_all | solution.py:316
  191.0 0.0 copy-done.12
  191.0 0.1 iota_compare_fusion
  191.1 0.1 lt.35
  191.2 0.0 copy-done.11
  191.2 0.1 copy.17
  191.2 0.1 squeeze.3
  191.3 15.2 %all-to-all-done.1 = bf16[32,16,1024]{2,1,0:T(8,128)(2,1)S(1)} async-done(((bf16[32,16,1024]{2,1,0:T(8,128)(2,1)}), bf16[32,16,1024]{2,1,0:T(8,128)(2,1)S(1)}, u32[]{:S(2)}, u32[]{:S(2)}) %all-to-all-start.1) | async-done | bytes 1048608 | tf_op jit(solution)/shard_map/all_to_all | solution.py:316
  206.6 0.0 copy-done.6
  206.6 0.0 copy-done.1
  206.6 0.0 copy-start.2
  206.6 1.2 copy-done.2
  207.8 0.0 copy-start.3
  207.8 2.3 shard_map.134
  210.1 13.0 %all_to_all.16.got_ref = bf16[8,32,640]{2,1,0:T(8,128)(2,1)S(1)} all-to-all(bf16[8,32,640]{2,1,0:T(8,128)(2,1)S(1)} %bitcast.15), channel_id=1, replica_groups=mesh['dp'=4,'block'=16,'parity'=2,'row'=4,'core'=2] {'row','core'}, dimensions={0} | all-to-all | bytes 655360 | tf_op jit(solution)/shard_map/all_to_all | solution.py:323
  223.0 0.0 copy-done.3
  223.0 1.5 shard_map.135
  (1 shorter events, 0.0 us)
Async XLA Ops:
  7.2 166.5 %all-gather.3.cloned.1.call-start = ((), (), s32[]{:S(2)}) async-start(), calls=%async_computation.3 | async-start | bytes 5947392 | tf_op jit(solution)/shard_map/all_gather | solution.py:305
  7.9 26.3 %copy-start.9 = (bf16[32,512]{1,0:T(8,128)(2,1)S(1)}, bf16[32,512]{1,0:T(8,128)(2,1)}, u32[]{:S(2)}) copy-start(bf16[32,512]{1,0:T(8,128)(2,1)} %param.22) | copy-start | bytes 98308
  7.9 43.8 %copy-start.10 = (s32[1,32,16]{1,2,0:T(8,128)S(1)}, s32[1,32,16]{1,2,0:T(8,128)}, u32[]{:S(2)}) copy-start(s32[1,32,16]{1,2,0:T(8,128)} %param.13) | copy-start | bytes 6148
  7.9 44.0 %copy-start = (bf16[128,1024]{1,0:T(8,128)(2,1)S(1)}, bf16[128,1024]{1,0:T(8,128)(2,1)}, u32[]{:S(2)}) copy-start(bf16[128,1024]{1,0:T(8,128)(2,1)} %tokens_ref.3) | copy-start | bytes 786436
  7.9 44.0 %copy-start.5 = (f32[1024]{0:T(1024)S(1)}, f32[1024]{0:T(1024)}, u32[]{:S(2)}) copy-start(f32[1024]{0:T(1024)} %param.16) | copy-start | bytes 12292
  10.7 40.4 %collective-permute-start = (bf16[64,1408]{1,0:T(8,128)(2,1)}, bf16[64,1408]{1,0:T(8,128)(2,1)S(1)}, u32[]{:S(2)}, u32[]{:S(2)}) collective-permute-start(bf16[64,1408]{1,0:T(8,128)(2,1)} %shard_map.132), channel_id=1, source_target_pairs={{0,0},{257,1},{514,16},{771,17},{4,32},{261,33},{518,48},{775,49},... | collective-permute-start | bytes 540680 | tf_op jit(solution)/shard_map/ppermute | solution.py:302
  51.0 0.7 copy-start.8
  173.7 2.6 %copy-start.7 = (bf16[2048,1408]{1,0:T(8,128)(2,1)S(1)}, bf16[2048,1408]{1,0:T(8,128)(2,1)}, u32[]{:S(2)}) copy-start(bf16[2048,1408]{1,0:T(8,128)(2,1)} %all-gather.3.cloned.1.call-done) | copy-start | bytes 17301508
  176.3 14.7 %copy-start.12 = (s32[1,32]{1,0:T(1,128)S(1)}, s32[1,32]{1,0:T(1,128)}, u32[]{:S(2)}) copy-start(s32[1,32]{1,0:T(1,128)} %param.15) | copy-start | bytes 388
  176.3 14.8 %copy-start.11 = (f32[1,32,16]{1,2,0:T(8,128)S(1)}, f32[1,32,16]{1,2,0:T(8,128)}, u32[]{:S(2)}) copy-start(f32[1,32,16]{1,2,0:T(8,128)} %param.14) | copy-start | bytes 6148
  176.3 30.2 %copy-start.6 = (f32[1024]{0:T(1024)S(1)}, f32[1024]{0:T(1024)}, u32[]{:S(2)}) copy-start(f32[1024]{0:T(1024)} %param.17) | copy-start | bytes 12292
  181.7 1.0 copy-start.4
  182.7 23.9 %copy-start.1 = (bf16[1024,512]{1,0:T(8,128)(2,1)S(1)}, bf16[1024,512]{1,0:T(8,128)(2,1)}, u32[]{:S(2)}) copy-start(bf16[1024,512]{1,0:T(8,128)(2,1)} %key_ref.1) | copy-start | bytes 3145732
  182.7 23.9 %all-to-all-start.1 = ((bf16[32,16,1024]{2,1,0:T(8,128)(2,1)}), bf16[32,16,1024]{2,1,0:T(8,128)(2,1)S(1)}, u32[]{:S(2)}, u32[]{:S(2)}) async-start(bf16[32,16,1024]{2,1,0:T(8,128)(2,1)} %bitcast.13), calls=%async_computation.1 | async-start | bytes 2097152 | tf_op jit(solution)/shard_map/all_to_all | solution.py:316
  206.6 1.2 copy-start.2
  207.8 15.3 %copy-start.3 = (bf16[512,1024]{1,0:T(8,128)(2,1)S(1)}, bf16[512,1024]{1,0:T(8,128)(2,1)}, u32[]{:S(2)}) copy-start(bf16[512,1024]{1,0:T(8,128)(2,1)} %proj_ref.1) | copy-start | bytes 3145732
Sparse Core Ops, SparseCore 0:
  51.9 121.7 all-gather.2

commit v6 on v5

--- a/solution.py
+++ b/solution.py
@@ -30,17 +30,24 @@
     return values * lax.rsqrt(mean_square + EPSILON) * gain
 
 
-def shard_kernel(which, w_in_ref, w_out_ref, out_ref):
+def shard_kernel(which, w_in_ref, w_out_ref, out_ref, columns, sem):
     rows = out_ref.shape[0]
     block, kind = which[0], which[1]
 
     @pl.when(kind == 0)
     def _():
-        out_ref[...] = w_in_ref[0]
+        here = pl.ds(pl.multiple_of(block * rows, rows), rows)
+        copy = pltpu.make_async_copy(w_in_ref.at[0, here, :], out_ref, sem)
+        copy.start()
+        copy.wait()
 
     @pl.when(kind == 1)
     def _():
-        turned = w_out_ref[0].astype(F32).T
+        here = pl.ds(pl.multiple_of(block // 2 * (2 * rows), 2 * rows), 2 * rows)
+        copy = pltpu.make_async_copy(w_out_ref.at[0, :, here], columns, sem)
+        copy.start()
+        copy.wait()
+        turned = columns[...].astype(F32).T
         upper = jnp.where(block % 2 == 1, turned[rows:], turned[:rows])
         out_ref[...] = upper.astype(BF16)
 
@@ -50,16 +57,17 @@
     rows = width // blocks
     return pl.pallas_call(
         shard_kernel,
-        grid_spec=pltpu.PrefetchScalarGridSpec(
-            num_scalar_prefetch=1,
-            grid=(1,),
-            in_specs=[
-                pl.BlockSpec((1, rows, hidden), lambda i, s: (0, s[0], 0)),
-                pl.BlockSpec((1, hidden, 2 * rows), lambda i, s: (0, 0, s[0] // 2)),
-            ],
-            out_specs=pl.BlockSpec((rows, hidden), lambda i, s: (0, 0)),
-        ),
+        in_specs=[
+            pl.BlockSpec(memory_space=pltpu.SMEM),
+            pl.BlockSpec(memory_space=pl.ANY),
+            pl.BlockSpec(memory_space=pl.ANY),
+        ],
+        out_specs=_VM(),
         out_shape=jax.ShapeDtypeStruct((rows, hidden), BF16),
+        scratch_shapes=[
+            pltpu.VMEM((hidden, 2 * rows), BF16),
+            pltpu.SemaphoreType.DMA(()),
+        ],
         compiler_params=pltpu.CompilerParams(vmem_limit_bytes=FULL),
     )(which, w_in, w_out)
 
@@ -90,7 +98,7 @@
     return 0.5 * v * (1.0 + jnp.tanh(0.7978845608028654 * (v + 0.044715 * (v * v * v))))
 
 
-def expert_kernel(rows_ref, weights_ref, out_ref, w_in, w_out, middle, sems):
+def expert_kernel(rows_ref, weights_ref, out_ref, rows_held, w_in, w_out, middle, sems):
     blocks, _, part, hidden = weights_ref.shape
     width = blocks * part
     inner = [pl.ds(i, min(STEP, hidden - i)) for i in range(0, hidden, STEP)]
@@ -104,9 +112,12 @@
         )
         for n, span in enumerate(outer)
     ]
+    rows_copy = pltpu.make_async_copy(rows_ref, rows_held, sems.at[len(copies)])
+    rows_copy.start()
     for copy in copies:
         copy.start()
-    rows = rows_ref[...]
+    rows_copy.wait()
+    rows = rows_held[...]
     for n, span in enumerate(inner):
         copies[n].wait()
         first = w_in[:, :, span].reshape(width, -1)
@@ -127,16 +138,17 @@
     blocks, _, part, hidden = weights.shape
     return pl.pallas_call(
         expert_kernel,
-        in_specs=[_VM(), pl.BlockSpec(memory_space=pltpu.HBM)],
+        in_specs=[pl.BlockSpec(memory_space=pl.ANY)] * 2,
         out_specs=_VM(),
         out_shape=jax.ShapeDtypeStruct((total, width), BF16),
         scratch_shapes=[
+            pltpu.VMEM((total, width), BF16),
             pltpu.VMEM((blocks, part, hidden), BF16),
             pltpu.VMEM((blocks, part, hidden), BF16),
             pltpu.VMEM((total, hidden), BF16),
-            pltpu.SemaphoreType.DMA((-(-hidden // STEP) + width // STEP,)),
+            pltpu.SemaphoreType.DMA((1 + -(-hidden // STEP) + width // STEP,)),
         ],
-        compiler_params=pltpu.CompilerParams(vmem_limit_bytes=VMEM // 2),
+        compiler_params=pltpu.CompilerParams(vmem_limit_bytes=FULL),
         cost_estimate=pl.CostEstimate(
             flops=4 * total * width * hidden,
             bytes_accessed=4 * width * hidden + 4 * total * width,
@@ -155,11 +167,9 @@
 
 
 def tail_kernel(
-    back_ref, picks_ref, weight_ref, tokens_ref, gain_ref, key_ref, value_ref, query_ref,
-    encoded_ref, packet_ref, value_held, value_sem,
+    back_ref, picks_ref, weight_ref, tokens_ref, gain_ref, joined_ref, query_ref,
+    encoded_ref, packet_ref,
 ):
-    value_copy = pltpu.make_async_copy(value_ref, value_held, value_sem)
-    value_copy.start()
     rows = tokens_ref.shape[0]
     slots = picks_ref.shape[1]
     here = lax.broadcasted_iota(jnp.int32, (rows, slots), 0) == picks_ref[...]
@@ -171,9 +181,8 @@
     mixed = tokens_ref[...].astype(F32) + expert_sum
     encoded = rms_norm(mixed, gain_ref[...]).astype(BF16)
     encoded_ref[...] = encoded
-    keys = jnp.dot(encoded, key_ref[...], preferred_element_type=F32).astype(BF16)
-    value_copy.wait()
-    values = jnp.dot(encoded, value_held[...], preferred_element_type=F32).astype(BF16)
+    joined = jnp.dot(encoded, joined_ref[...], preferred_element_type=F32).astype(BF16)
+    keys, values = joined[:, : joined.shape[1] // 2], joined[:, joined.shape[1] // 2 :]
     query = query_ref[...]
     count, features = query.shape
     size = features // HEADS
@@ -209,20 +218,19 @@
     packet_ref[:, features:] = stats.astype(BF16)
 
 
-def tail(back, picks, weight, tokens, gain, w_key, w_value, query):
+def tail(back, picks, weight, tokens, gain, joined, query):
     rows, width = tokens.shape
     count, features = query.shape
     return pl.pallas_call(
         tail_kernel,
-        in_specs=[_VM()] * 6 + [pl.BlockSpec(memory_space=pltpu.HBM), _VM()],
+        in_specs=[_VM()] * 7,
         out_specs=(_VM(), _VM()),
-        scratch_shapes=[pltpu.VMEM(w_value.shape, BF16), pltpu.SemaphoreType.DMA(())],
         out_shape=(
             jax.ShapeDtypeStruct((rows, width), BF16),
             jax.ShapeDtypeStruct((count, features + 128), BF16),
         ),
         compiler_params=pltpu.CompilerParams(vmem_limit_bytes=VMEM // 2),
-    )(back, picks, weight, tokens, gain, w_key, w_value, query)
+    )(back, picks, weight, tokens, gain, joined, query)
 
 
 def merge_kernel(got_ref, proj_ref, out_ref):
@@ -312,12 +320,14 @@
     there = lax.all_to_all(
         chosen.reshape(experts, -1, width), NEAR, split_axis=0, concat_axis=0, tiled=True
     )
+    joined = jnp.concatenate([w_key, w_value], axis=1)
+    there, joined, slot_weight = lax.optimization_barrier((there, joined, slot_weight))
     result = expert(there.reshape(-1, width), weights)
     back = lax.all_to_all(
         result.reshape(experts, -1, width), NEAR, split_axis=0, concat_axis=0, tiled=True
     ).reshape(-1, width)
     encoded, packet = tail(
-        back, pick_row, slot_weight, tokens, norm_out[None, :], w_key, w_value, query
+        back, pick_row, slot_weight, tokens, norm_out[None, :], joined, query
     )
     group = row_count * cores
     got = lax.all_to_all(

time: 232 us -> 229 us (0.987)
  local copies, waits for them, and re-layouts: 5.94 us -> 1.11 us
  waiting for transfers between devices: 112 us -> 109 us
  Pallas kernels: 12.4 us -> 15.1 us
    unnamed x28 -> x20, local copies, waits for them, and re-layouts: 5.69 us -> 0.86 us
  transfers between devices with their start and end apart: 3 -> 3, of which waited for: 2 -> 2; matrix products, arithmetic and copies ran while one was open for 0% -> 1% of each run, Pallas kernels for 0% -> 1%
where the time goes in v6:
time: 229 us; the launch traced here: 228 us
  waiting for transfers between devices  109 us (48%)
  blocking collectives  53.6 us (23%)
  starting transfers between devices  32.4 us (14%)
  Pallas kernels  15.1 us (7%)
  between operations  14.2 us (6%)
  other arithmetic  2.51 us (1%)
    all_gather x1, waiting for transfers between devices, local(): weights = lax.all_gather(shard, ('block', 'core'))  95.7 us
    all_to_all x1, blocking collectives, local(): lax.all_to_all(result.reshape(experts, -1, width), NEAR, split_axis=0, co...  23.9 us
    ppermute x1, starting transfers between devices, local(): shard = lax.ppermute(shard, ALL, scatter_pairs(sizes))  23.5 us
    all_gather x1, blocking collectives, local(): query = lax.all_gather(queries, SEQ, tiled=True)  16.7 us
    all_to_all x1, waiting for transfers between devices, local(): lax.all_to_all(chosen.reshape(experts, -1, width), NEAR, split_axis=0, co...  13.5 us
    all_to_all x1, blocking collectives, local(): lax.all_to_all(packet.reshape(group, -1, packet.shape[1]), SEQ, split_axi...  13 us
    all_to_all x1, starting transfers between devices, local(): lax.all_to_all(chosen.reshape(experts, -1, width), NEAR, split_axis=0, co...  8.83 us
    pallas_call x1, Pallas kernels, expert(): pl.pallas_call(expert_kernel, in_specs=[pl.BlockSpec(memory_space=pl.ANY)...  7.39 us
  transfers between devices with their start and end apart: 3, of which 2 were waited for; matrix products, arithmetic and copies ran while one was open for 1% of the time, Pallas kernels for 1%

profile of v6, /device:TPU:1, one launch (start us, length us, event | category | flops | bytes accessed | tf_op | source)
XLA Modules:
  0.0 228.2 jit_solution(18171078974202062257)
XLA Ops:
  7.2 0.0 all-gather.3.cloned.1.call-start
  7.3 0.6 pad_add_fusion.which
  7.9 0.0 copy-start.5
  7.9 0.0 copy-start.6
  7.9 0.0 copy-start
  7.9 0.0 copy-start.2
  7.9 2.6 %shard_map.132 = bf16[64,1408]{1,0:T(8,128)(2,1)} custom-call(s32[2]{0:T(128)} %pad_add_fusion.which, bf16[1,1024,1408]{2,1,0:T(8,128)(2,1)} %w_in_ref.1, bf16[1,1408,1024]{2,1,0:T(8,128)(2,1)} %w_out_ref.1), custom_call_target="tpu_custom_call" | custom-call | tf_op jit(solution)/shard_map/pallas_call | solution.py:58
  10.6 0.0 copy-start.8
  10.6 0.0 copy-start.7
  10.6 23.5 %collective-permute-start = (bf16[64,1408]{1,0:T(8,128)(2,1)}, bf16[64,1408]{1,0:T(8,128)(2,1)S(1)}, u32[]{:S(2)}, u32[]{:S(2)}) collective-permute-start(bf16[64,1408]{1,0:T(8,128)(2,1)} %shard_map.132), channel_id=1, source_target_pairs={{0,0},{257,1},{514,16},{771,17},{4,32},{261,33},{518,48},{775,49},... | collective-permute-start | bytes 540680 | tf_op jit(solution)/shard_map/ppermute | solution.py:310
  34.1 0.0 copy-done.5
  34.2 16.7 %all_gather.9.query_ref = bf16[256,512]{1,0:T(8,128)(2,1)S(1)} all-gather(bf16[32,512]{1,0:T(8,128)(2,1)S(1)} %copy-done.5), channel_id=1, replica_groups=mesh['dp'=4,'block'=16,'parity'=2,'row'=4,'core'=2] {'row','core'}, dimensions={0}, use_global_device_ids=true | all-gather | bytes 294912 | tf_op jit(solution)/shard_map/all_gather | solution.py:311
  50.9 0.0 collective-permute-done
  50.9 0.0 copy-start.4
  50.9 0.7 copy-done.4
  51.6 0.0 all-gather.3.cloned.1.call-update
  51.6 0.0 copy-done.6
  51.6 0.1 copy.16
  51.7 0.1 reshape.59.picks_ref
  51.8 0.0 copy-done
  51.8 0.0 copy-done.2
  51.8 1.5 shard_map.131
  53.3 8.8 %all-to-all-start = ((bf16[32,16,1024]{2,1,0:T(8,128)(2,1)}), bf16[32,16,1024]{2,1,0:T(8,128)(2,1)}, u32[]{:S(2)}, u32[]{:S(2)}) async-start(bf16[32,16,1024]{2,1,0:T(8,128)(2,1)} %bitcast.1), calls=%async_computation | async-start | bytes 2097152 | tf_op jit(solution)/shard_map/all_to_all | solution.py:320
  62.1 0.0 copy-done.8
  62.1 0.1 iota_compare_fusion
  62.2 0.1 lt.33
  62.3 0.0 copy-done.7
  62.3 0.1 copy.17
  62.4 0.1 squeeze.3
  62.5 1.8 pad_maximum_fusion.joined_ref
  64.3 13.5 %all-to-all-done = bf16[32,16,1024]{2,1,0:T(8,128)(2,1)} async-done(((bf16[32,16,1024]{2,1,0:T(8,128)(2,1)}), bf16[32,16,1024]{2,1,0:T(8,128)(2,1)}, u32[]{:S(2)}, u32[]{:S(2)}) %all-to-all-start) | async-done | bytes 1048608 | tf_op jit(solution)/shard_map/all_to_all | solution.py:320
  77.8 95.7 %all-gather.3.cloned.1.call-done = bf16[2048,1408]{1,0:T(8,128)(2,1)} async-done(((bf16[64,1408]{1,0:T(8,128)(2,1)}), bf16[2048,1408]{1,0:T(8,128)(2,1)}) %all-gather.3.cloned.1.call-update) | async-done | bytes 5767184 | tf_op jit(solution)/shard_map/all_gather | solution.py:313
  173.5 0.0 copy-start.3
  173.5 7.4 %shard_map.133 = bf16[512,1024]{1,0:T(8,128)(2,1)} custom-call(bf16[512,1024]{1,0:T(8,128)(2,1)} %bitcast.3.rows_ref, bf16[16,2,64,1408]{3,2,1,0:T(8,128)(2,1)} %bitcast.17), custom_call_target="tpu_custom_call" | custom-call | flops 2952790016 | bytes 7864320 | tf_op jit(solution)/shard_map/pallas_call | solution.py:139
  180.9 0.0 copy-start.1
  181.0 23.9 %all_to_all.15 = bf16[32,16,1024]{2,1,0:T(8,128)(2,1)S(1)} all-to-all(bf16[32,16,1024]{2,1,0:T(8,128)(2,1)} %bitcast.15), channel_id=1, replica_groups=mesh['dp'=4,'block'=16,'parity'=2,'row'=4,'core'=2] {'dp','parity','row'}, dimensions={0} | all-to-all | bytes 2097152 | tf_op jit(solution)/shard_map/all_to_all | solution.py:326
  204.9 0.0 copy-done.3
  204.9 2.1 shard_map.134
  206.9 13.0 %all_to_all.16.got_ref = bf16[8,32,640]{2,1,0:T(8,128)(2,1)S(1)} all-to-all(bf16[8,32,640]{2,1,0:T(8,128)(2,1)S(1)} %bitcast.12), channel_id=1, replica_groups=mesh['dp'=4,'block'=16,'parity'=2,'row'=4,'core'=2] {'row','core'}, dimensions={0} | all-to-all | bytes 655360 | tf_op jit(solution)/shard_map/all_to_all | solution.py:333
  219.9 0.0 copy-done.1
  219.9 1.5 shard_map.135
  (1 shorter events, 0.0 us)
Async XLA Ops:
  7.2 166.4 %all-gather.3.cloned.1.call-start = ((), (), s32[]{:S(2)}) async-start(), calls=%async_computation.3 | async-start | bytes 5947392 | tf_op jit(solution)/shard_map/all_gather | solution.py:313
  7.9 26.2 %copy-start.5 = (bf16[32,512]{1,0:T(8,128)(2,1)S(1)}, bf16[32,512]{1,0:T(8,128)(2,1)}, u32[]{:S(2)}) copy-start(bf16[32,512]{1,0:T(8,128)(2,1)} %param.22) | copy-start | bytes 98308
  7.9 43.7 %copy-start.6 = (s32[1,32,16]{1,2,0:T(8,128)S(1)}, s32[1,32,16]{1,2,0:T(8,128)}, u32[]{:S(2)}) copy-start(s32[1,32,16]{1,2,0:T(8,128)} %param.13) | copy-start | bytes 6148
  7.9 43.9 %copy-start = (bf16[128,1024]{1,0:T(8,128)(2,1)S(1)}, bf16[128,1024]{1,0:T(8,128)(2,1)}, u32[]{:S(2)}) copy-start(bf16[128,1024]{1,0:T(8,128)(2,1)} %tokens_ref.3) | copy-start | bytes 786436
  7.9 43.9 %copy-start.2 = (f32[1024]{0:T(1024)S(1)}, f32[1024]{0:T(1024)}, u32[]{:S(2)}) copy-start(f32[1024]{0:T(1024)} %param.16) | copy-start | bytes 12292
  10.6 51.6 %copy-start.8 = (s32[1,32]{1,0:T(1,128)S(1)}, s32[1,32]{1,0:T(1,128)}, u32[]{:S(2)}) copy-start(s32[1,32]{1,0:T(1,128)} %param.15) | copy-start | bytes 388
  10.6 51.7 %copy-start.7 = (f32[1,32,16]{1,2,0:T(8,128)S(1)}, f32[1,32,16]{1,2,0:T(8,128)}, u32[]{:S(2)}) copy-start(f32[1,32,16]{1,2,0:T(8,128)} %param.14) | copy-start | bytes 6148
  10.6 40.3 %collective-permute-start = (bf16[64,1408]{1,0:T(8,128)(2,1)}, bf16[64,1408]{1,0:T(8,128)(2,1)S(1)}, u32[]{:S(2)}, u32[]{:S(2)}) collective-permute-start(bf16[64,1408]{1,0:T(8,128)(2,1)} %shard_map.132), channel_id=1, source_target_pairs={{0,0},{257,1},{514,16},{771,17},{4,32},{261,33},{518,48},{775,49},... | collective-permute-start | bytes 540680 | tf_op jit(solution)/shard_map/ppermute | solution.py:310
  50.9 0.7 copy-start.4
  53.3 24.5 %all-to-all-start = ((bf16[32,16,1024]{2,1,0:T(8,128)(2,1)}), bf16[32,16,1024]{2,1,0:T(8,128)(2,1)}, u32[]{:S(2)}, u32[]{:S(2)}) async-start(bf16[32,16,1024]{2,1,0:T(8,128)(2,1)} %bitcast.1), calls=%async_computation | async-start | bytes 2097152 | tf_op jit(solution)/shard_map/all_to_all | solution.py:320
  173.5 31.3 %copy-start.3 = (f32[1024]{0:T(1024)S(1)}, f32[1024]{0:T(1024)}, u32[]{:S(2)}) copy-start(f32[1024]{0:T(1024)} %param.17) | copy-start | bytes 12292
  180.9 39.0 %copy-start.1 = (bf16[512,1024]{1,0:T(8,128)(2,1)S(1)}, bf16[512,1024]{1,0:T(8,128)(2,1)}, u32[]{:S(2)}) copy-start(bf16[512,1024]{1,0:T(8,128)(2,1)} %proj_ref.1) | copy-start | bytes 3145732
Sparse Core Ops, SparseCore 0:
  51.7 121.7 all-gather.2

commit v7 on v6

--- a/solution.py
+++ b/solution.py
@@ -308,8 +308,8 @@
     j = (INV_J * (column + (plane - STEP_E) * own)) % plane
     shard = take_shard(jnp.stack([j // cores, j % cores]).astype(jnp.int32), w_in, w_out, blocks)
     shard = lax.ppermute(shard, ALL, scatter_pairs(sizes))
+    shard, queries = lax.optimization_barrier((shard, queries))
     query = lax.all_gather(queries, SEQ, tiled=True)
-    shard, query = lax.optimization_barrier((shard, query))
     weights = lax.all_gather(shard, ("block", "core"))
     weights = weights.reshape(blocks, cores, *shard.shape)
 
@@ -321,7 +321,9 @@
         chosen.reshape(experts, -1, width), NEAR, split_axis=0, concat_axis=0, tiled=True
     )
     joined = jnp.concatenate([w_key, w_value], axis=1)
-    there, joined, slot_weight = lax.optimization_barrier((there, joined, slot_weight))
+    there, joined, slot_weight, query = lax.optimization_barrier(
+        (there, joined, slot_weight, query)
+    )
     result = expert(there.reshape(-1, width), weights)
     back = lax.all_to_all(
         result.reshape(experts, -1, width), NEAR, split_axis=0, concat_axis=0, tiled=True

time: 229 us -> 229 us (level)
  waiting for transfers between devices: 109 us -> 92.4 us
  starting transfers between devices: 32.4 us -> 43.9 us
  blocking collectives: 53.6 us -> 59 us
    all_to_all x1, waiting for transfers between devices: 13.5 us -> 0.01 us  [local(): lax.all_to_all(chosen.reshape(experts, -1, width), NEAR, split_axis=0, co...]
    all_to_all x1, starting transfers between devices: 8.83 us -> 20.3 us  [local(): lax.all_to_all(chosen.reshape(experts, -1, width), NEAR, split_axis=0, co...]
    all_gather x1, waiting for transfers between devices: 95.7 us -> 87.7 us  [local(): weights = lax.all_gather(shard, ('block', 'core'))]
    all_gather x1, blocking collectives: 16.7 us -> 22.1 us  [local(): query = lax.all_gather(queries, SEQ, tiled=True)]
    ppermute x1, waiting for transfers between devices: 0.01 us -> 4.7 us  [local(): shard = lax.ppermute(shard, ALL, scatter_pairs(sizes))]
where the time goes in v7:
time: 229 us; the launch traced here: 228 us
  waiting for transfers between devices  92.4 us (40%)
  blocking collectives  59 us (26%)
  starting transfers between devices  43.9 us (19%)
  Pallas kernels  15.1 us (7%)
  between operations  14.2 us (6%)
  other arithmetic  2.51 us (1%)
    all_gather x1, waiting for transfers between devices, local(): weights = lax.all_gather(shard, ('block', 'core'))  87.7 us
    all_to_all x1, blocking collectives, local(): lax.all_to_all(result.reshape(experts, -1, width), NEAR, split_axis=0, co...  23.9 us
    ppermute x1, starting transfers between devices, local(): shard = lax.ppermute(shard, ALL, scatter_pairs(sizes))  23.5 us
    all_gather x1, blocking collectives, local(): query = lax.all_gather(queries, SEQ, tiled=True)  22.1 us
    all_to_all x1, starting transfers between devices, local(): lax.all_to_all(chosen.reshape(experts, -1, width), NEAR, split_axis=0, co...  20.3 us
    all_to_all x1, blocking collectives, local(): lax.all_to_all(packet.reshape(group, -1, packet.shape[1]), SEQ, split_axi...  13 us
    pallas_call x1, Pallas kernels, expert(): pl.pallas_call(expert_kernel, in_specs=[pl.BlockSpec(memory_space=pl.ANY)...  7.39 us
    ppermute x1, waiting for transfers between devices, local(): shard = lax.ppermute(shard, ALL, scatter_pairs(sizes))  4.7 us
  transfers between devices with their start and end apart: 3, of which 2 were waited for; matrix products, arithmetic and copies ran while one was open for 1% of the time, Pallas kernels for 1%

profile of v7, /device:TPU:1, one launch (start us, length us, event | category | flops | bytes accessed | tf_op | source)
XLA Modules:
  0.0 228.2 jit_solution(2198762639365354971)
XLA Ops:
  7.2 0.0 all-gather.3.cloned.1.call-start
  7.3 0.6 pad_add_fusion.which
  7.9 0.0 copy-start.6
  7.9 0.0 copy-start
  7.9 0.0 copy-start.2
  7.9 2.6 %shard_map.132 = bf16[64,1408]{1,0:T(8,128)(2,1)} custom-call(s32[2]{0:T(128)} %pad_add_fusion.which, bf16[1,1024,1408]{2,1,0:T(8,128)(2,1)} %w_in_ref.1, bf16[1,1408,1024]{2,1,0:T(8,128)(2,1)} %w_out_ref.1), custom_call_target="tpu_custom_call" | custom-call | tf_op jit(solution)/shard_map/pallas_call | solution.py:58
  10.6 0.0 copy-start.8
  10.6 0.0 copy-start.7
  10.6 23.5 %collective-permute-start = (bf16[64,1408]{1,0:T(8,128)(2,1)}, bf16[64,1408]{1,0:T(8,128)(2,1)S(1)}, u32[]{:S(2)}, u32[]{:S(2)}) collective-permute-start(bf16[64,1408]{1,0:T(8,128)(2,1)} %shard_map.132), channel_id=1, source_target_pairs={{0,0},{257,1},{514,16},{771,17},{4,32},{261,33},{518,48},{775,49},... | collective-permute-start | bytes 540680 | tf_op jit(solution)/shard_map/ppermute | solution.py:310
  34.1 4.7 %collective-permute-done = bf16[64,1408]{1,0:T(8,128)(2,1)S(1)} collective-permute-done((bf16[64,1408]{1,0:T(8,128)(2,1)}, bf16[64,1408]{1,0:T(8,128)(2,1)S(1)}, u32[]{:S(2)}, u32[]{:S(2)}) %collective-permute-start) | collective-permute-done | bytes 180256 | tf_op jit(solution)/shard_map/ppermute | solution.py:310
  38.8 0.0 copy-start.4
  38.8 0.7 copy-done.4
  39.5 0.0 all-gather.3.cloned.1.call-update
  39.5 0.0 copy-done.6
  39.5 0.1 copy.16
  39.6 0.1 reshape.59.picks_ref
  39.7 0.0 copy-done
  39.7 0.0 copy-done.2
  39.7 1.5 shard_map.131
  41.2 0.0 copy-start.5
  41.2 20.3 %all-to-all-start = ((bf16[32,16,1024]{2,1,0:T(8,128)(2,1)}), bf16[32,16,1024]{2,1,0:T(8,128)(2,1)}, u32[]{:S(2)}, u32[]{:S(2)}) async-start(bf16[32,16,1024]{2,1,0:T(8,128)(2,1)} %bitcast.1), calls=%async_computation | async-start | bytes 2097152 | tf_op jit(solution)/shard_map/all_to_all | solution.py:320
  61.6 0.0 copy-done.8
  61.6 0.1 iota_compare_fusion
  61.7 0.1 lt.33
  61.7 0.0 copy-done.7
  61.7 0.1 copy.17
  61.8 0.1 squeeze.3
  61.9 1.8 pad_maximum_fusion.joined_ref
  63.7 0.0 copy-done.5
  63.7 22.1 %all_gather.9.query_ref = bf16[256,512]{1,0:T(8,128)(2,1)S(1)} all-gather(bf16[32,512]{1,0:T(8,128)(2,1)S(1)} %copy-done.5), channel_id=1, replica_groups=mesh['dp'=4,'block'=16,'parity'=2,'row'=4,'core'=2] {'row','core'}, dimensions={0}, use_global_device_ids=true | all-gather | bytes 294912 | tf_op jit(solution)/shard_map/all_gather | solution.py:312
  85.8 0.0 all-to-all-done
  85.8 87.7 %all-gather.3.cloned.1.call-done = bf16[2048,1408]{1,0:T(8,128)(2,1)} async-done(((bf16[64,1408]{1,0:T(8,128)(2,1)}), bf16[2048,1408]{1,0:T(8,128)(2,1)}) %all-gather.3.cloned.1.call-update) | async-done | bytes 5767184 | tf_op jit(solution)/shard_map/all_gather | solution.py:313
  173.5 0.0 copy-start.3
  173.5 7.4 %shard_map.133 = bf16[512,1024]{1,0:T(8,128)(2,1)} custom-call(bf16[512,1024]{1,0:T(8,128)(2,1)} %bitcast.5.rows_ref, bf16[16,2,64,1408]{3,2,1,0:T(8,128)(2,1)} %bitcast.17), custom_call_target="tpu_custom_call" | custom-call | flops 2952790016 | bytes 7864320 | tf_op jit(solution)/shard_map/pallas_call | solution.py:139
  180.9 0.0 copy-start.1
  180.9 23.9 %all_to_all.15 = bf16[32,16,1024]{2,1,0:T(8,128)(2,1)S(1)} all-to-all(bf16[32,16,1024]{2,1,0:T(8,128)(2,1)} %bitcast.15), channel_id=1, replica_groups=mesh['dp'=4,'block'=16,'parity'=2,'row'=4,'core'=2] {'dp','parity','row'}, dimensions={0} | all-to-all | bytes 2097152 | tf_op jit(solution)/shard_map/all_to_all | solution.py:328
  204.9 0.0 copy-done.3
  204.9 2.1 shard_map.134
  206.9 13.0 %all_to_all.16.got_ref = bf16[8,32,640]{2,1,0:T(8,128)(2,1)S(1)} all-to-all(bf16[8,32,640]{2,1,0:T(8,128)(2,1)S(1)} %bitcast.12), channel_id=1, replica_groups=mesh['dp'=4,'block'=16,'parity'=2,'row'=4,'core'=2] {'row','core'}, dimensions={0} | all-to-all | bytes 655360 | tf_op jit(solution)/shard_map/all_to_all | solution.py:335
  219.9 0.0 copy-done.1
  219.9 1.5 shard_map.135
  (1 shorter events, 0.0 us)
Async XLA Ops:
  7.2 166.4 %all-gather.3.cloned.1.call-start = ((), (), s32[]{:S(2)}) async-start(), calls=%async_computation.3 | async-start | bytes 5947392 | tf_op jit(solution)/shard_map/all_gather | solution.py:313
  7.9 31.6 %copy-start.6 = (s32[1,32,16]{1,2,0:T(8,128)S(1)}, s32[1,32,16]{1,2,0:T(8,128)}, u32[]{:S(2)}) copy-start(s32[1,32,16]{1,2,0:T(8,128)} %param.13) | copy-start | bytes 6148
  7.9 31.8 %copy-start = (bf16[128,1024]{1,0:T(8,128)(2,1)S(1)}, bf16[128,1024]{1,0:T(8,128)(2,1)}, u32[]{:S(2)}) copy-start(bf16[128,1024]{1,0:T(8,128)(2,1)} %tokens_ref.3) | copy-start | bytes 786436
  7.9 31.8 %copy-start.2 = (f32[1024]{0:T(1024)S(1)}, f32[1024]{0:T(1024)}, u32[]{:S(2)}) copy-start(f32[1024]{0:T(1024)} %param.16) | copy-start | bytes 12292
  10.6 51.0 %copy-start.8 = (s32[1,32]{1,0:T(1,128)S(1)}, s32[1,32]{1,0:T(1,128)}, u32[]{:S(2)}) copy-start(s32[1,32]{1,0:T(1,128)} %param.15) | copy-start | bytes 388
  10.6 51.2 %copy-start.7 = (f32[1,32,16]{1,2,0:T(8,128)S(1)}, f32[1,32,16]{1,2,0:T(8,128)}, u32[]{:S(2)}) copy-start(f32[1,32,16]{1,2,0:T(8,128)} %param.14) | copy-start | bytes 6148
  10.6 28.3 %collective-permute-start = (bf16[64,1408]{1,0:T(8,128)(2,1)}, bf16[64,1408]{1,0:T(8,128)(2,1)S(1)}, u32[]{:S(2)}, u32[]{:S(2)}) collective-permute-start(bf16[64,1408]{1,0:T(8,128)(2,1)} %shard_map.132), channel_id=1, source_target_pairs={{0,0},{257,1},{514,16},{771,17},{4,32},{261,33},{518,48},{775,49},... | collective-permute-start | bytes 540680 | tf_op jit(solution)/shard_map/ppermute | solution.py:310
  38.8 0.7 copy-start.4
  41.2 22.5 %copy-start.5 = (bf16[32,512]{1,0:T(8,128)(2,1)S(1)}, bf16[32,512]{1,0:T(8,128)(2,1)}, u32[]{:S(2)}) copy-start(bf16[32,512]{1,0:T(8,128)(2,1)} %param.22) | copy-start | bytes 98308
  41.2 44.6 %all-to-all-start = ((bf16[32,16,1024]{2,1,0:T(8,128)(2,1)}), bf16[32,16,1024]{2,1,0:T(8,128)(2,1)}, u32[]{:S(2)}, u32[]{:S(2)}) async-start(bf16[32,16,1024]{2,1,0:T(8,128)(2,1)} %bitcast.1), calls=%async_computation | async-start | bytes 2097152 | tf_op jit(solution)/shard_map/all_to_all | solution.py:320
  173.5 31.3 %copy-start.3 = (f32[1024]{0:T(1024)S(1)}, f32[1024]{0:T(1024)}, u32[]{:S(2)}) copy-start(f32[1024]{0:T(1024)} %param.17) | copy-start | bytes 12292
  180.9 38.9 %copy-start.1 = (bf16[512,1024]{1,0:T(8,128)(2,1)S(1)}, bf16[512,1024]{1,0:T(8,128)(2,1)}, u32[]{:S(2)}) copy-start(bf16[512,1024]{1,0:T(8,128)(2,1)} %proj_ref.1) | copy-start | bytes 3145732
Sparse Core Ops, SparseCore 0:
  39.7 133.8 all-gather.2
